TPU v7x, 128 devices: a whole 4x4x4 slice. The times are simulated.
128 devices in a mesh: base: 4 (over x), slab: 32 (over z, y, core).
Axes of the slice: x: 4, y: 4, z: 4, core: 2. Of those that a mesh axis runs over, the one named last changes fastest.
Arguments:
- residual: float32 [16384, 2, 128], P(('base', 'slab')), may hold values from -6 to 6
- position: float32 [16384, 2, 128], P(('base', 'slab')), may hold values from 4 to 124
- owner: int32 [16384, 1], P(('base', 'slab')), may hold values from 0 to 127; in each aligned block of 128 rows (0 to 127, 128 to 255, ...) at most 2 rows name the same one
- tile_local: int32 [16384], P(('base', 'slab')), may hold values from 0 to 31
- xi: float32 [4096, 4096], P(('base', 'slab')), may hold values from -6 to 6
- amplitude: float32 [4096, 4096], P(('base', 'slab')), may hold values from 0.05 to 0.5
Outputs:
- gradient: float32 [4096, 4096], P(('base', 'slab'))
Inputs may be any that keep to these rules, and one draw needn't show every extreme that they name: Among the blocks of one device no owner region is named by more than 2 blocks, a bound that some owner region reaches on some device.
All inputs are finite; a program needn't handle non-finite values.
Results may differ from a plain program's by a relative error of at most 0.00065.
Values sent between devices are 32-bit elements; how exact they have to be, the bound alone decides.
No kernel may reach another device: no remote copies, remote signals or barrier semaphores. Data moves between devices by JAX's collectives and lax.ppermute only.
A program may use at most 128 MiB of HBM per device.

v0:
```python
import functools
import math

import jax
import jax.numpy as jnp
import ml_dtypes
import numpy as np
from jax import lax
from jax.experimental import pallas as pl
from jax.experimental.pallas import tpu as pltpu
from jax.sharding import PartitionSpec as P

G = 8192
IMG = 4096
TILE = 128
GROUP = 8

NN = (((1,), (0,)), ((), ()))
NT = (((1,), (1,)), ((), ()))
TN = (((0,), (0,)), ((), ()))
f32 = jnp.float32
bf16 = jnp.bfloat16


LEFT = {6: (0, 0, 1, 1, 0, 2), 3: (0, 0, 1)}
RIGHT = {6: (0, 1, 0, 1, 2, 0), 3: (0, 1, 0)}


def pieces(x, count=3):
    out, rest = [], x
    for k in range(count):
        out.append(rest.astype(bf16))
        if k + 1 < count:
            rest = rest - out[-1].astype(f32)
    return out


def spread(x, order, axis):
    cut = pieces(x, max(order) + 1)
    return jnp.concatenate([cut[k] for k in order], axis=axis)


def mm(a, b, dims=NN):
    return lax.dot_general(a, b, dims, preferred_element_type=f32)


def spread_table(x, order, axis):
    cut, rest = [], x.astype(np.float64)
    for _ in range(max(order) + 1):
        cut.append(rest.astype(np.float32).astype(ml_dtypes.bfloat16))
        rest = rest - cut[-1].astype(np.float64)
    return np.concatenate([cut[k] for k in order], axis=axis)


def wave(rows, cols, modulus):
    turn = np.outer(rows, cols).astype(np.int64) % modulus
    angle = turn * (2.0 * np.pi / modulus)
    return np.cos(angle), np.sin(angle)


def turned(c, s):
    return np.block([[c, -s], [s, c]])


@functools.lru_cache(None)
def tables(n_base, n_slab):
    n = np.arange
    devices = n_base * n_slab
    out = {}
    c, s = wave(n(128), n(128), 128)
    out["w128"] = spread_table(turned(c, s), LEFT[3], 1)
    out["w128t"] = spread_table(turned(c, s).T, RIGHT[3], 0)
    out["tw_row"] = np.stack(wave(n(32), n(128), IMG))
    c, s = wave(n(64) + 32, n(128), 128)
    out["w_cols"] = spread_table(turned(c, s), LEFT[6], 1)
    out["tw_cols"] = np.stack(wave(n(64), n(128), G))
    eye = np.eye(4)
    c, s = wave(n(128), n(32), IMG)
    out["tw_f"] = np.stack([np.tile(c, (1, 4)), np.tile(s, (1, 4))])
    c, s = wave(n(32), n(32), 32)
    out["r_f"] = spread_table(np.concatenate([np.kron(eye, c + s), np.kron(eye, c - s)]) / IMG, RIGHT[3], 0)
    out["r_y"] = spread_table(np.concatenate([np.kron(eye, c), np.kron(eye, s)], axis=1), RIGHT[3], 0)
    src = n(devices)
    place = (src % n_slab) * n_base + src // n_slab
    wb, twb, rb = [], [], []
    for half in range(2):
        c, s = wave(n(128) + 128 * half, place, 256)
        wb.append(turned(c, s))
        c, s = wave(n(128) + 128 * half, n(32), G)
        twb.append(np.stack([np.tile(c, (1, 4)), np.tile(s, (1, 4))]))
        c, s = wave(n(32), n(32) // 2 + 8, 32)
        keep = (n(32) % 2 == half)[None, :]
        rb += [np.kron(eye, c * keep) / G, np.kron(eye, -s * keep) / G]
    out["w_b"] = spread_table(np.concatenate(wb), LEFT[6], 1)
    out["tw_b"] = np.stack(twb)
    out["r_b"] = spread_table(np.concatenate(rb), RIGHT[6], 0)
    return {k: v if v.dtype == ml_dtypes.bfloat16 else v.astype(np.float32) for k, v in out.items()}


def times(z, k, n):
    re, im = z
    k %= n
    if k == 0:
        return z
    if 4 * k == n:
        return -im, re
    c, s = math.cos(2 * math.pi * k / n), math.sin(2 * math.pi * k / n)
    if 8 * k == n:
        return (re - im) * c, (re + im) * c
    if 8 * k == 3 * n:
        return (re + im) * -s, (re - im) * s
    return re * c - im * s, re * s + im * c


def fft_list(xs):
    n = len(xs)
    if n == 1:
        return xs
    even, odd = fft_list(xs[0::2]), fft_list(xs[1::2])
    low, high = [], []
    for k in range(n // 2):
        (a, b), (c, d) = even[k], times(odd[k], k, n)
        low.append((a + c, b + d))
        high.append((a - c, b - d))
    return low + high


def rfft_list(xs):
    n = len(xs)
    if n == 2:
        return [(xs[0] + xs[1], None), (xs[0] - xs[1], None)]
    even, odd = rfft_list(xs[0::2]), rfft_list(xs[1::2])
    out = [None] * (n // 2 + 1)
    out[0] = (even[0][0] + odd[0][0], None)
    out[n // 2] = (even[0][0] - odd[0][0], None)
    out[n // 4] = (even[n // 4][0], odd[n // 4][0])
    for k in range(1, n // 4):
        (a, b), (c, d) = even[k], times(odd[k], k, n)
        out[k] = (a + c, b + d)
        out[n // 2 - k] = (a - c, d - b)
    return out


def call(body, out_shape, in_specs, scratch=(), flops=0):
    nbytes = 4 * math.prod(out_shape)
    return pl.pallas_call(
        body,
        out_shape=jax.ShapeDtypeStruct(out_shape, f32),
        in_specs=[pl.BlockSpec(memory_space=m) for m in in_specs],
        out_specs=pl.BlockSpec(memory_space=pltpu.VMEM),
        scratch_shapes=list(scratch),
        compiler_params=pltpu.CompilerParams(vmem_limit_bytes=48 * 2**20),
        cost_estimate=pl.CostEstimate(flops=int(flops), bytes_accessed=2 * nbytes, transcendentals=0),
    )


VM = pltpu.VMEM
SM = pltpu.SMEM


def pack_kernel(owner, tile, residual, position, out, count):
    n_base, n_slab = 4, 32
    out[...] = jnp.zeros_like(out)

    def clear(i, _):
        count[i] = 0
        return 0

    lax.fori_loop(0, count.shape[0], clear, 0, unroll=8)
    lane = lax.broadcasted_iota(jnp.int32, (1, 128), 1)

    def step(i, _):
        o, t = owner[i], tile[i]
        row = (o & (n_slab - 1)) * 2 + (t >> 4)
        group, col = o >> 5, t & 15
        flip = (row >= n_slab).astype(jnp.int32)
        row = jnp.where(flip == 1, 2 * n_slab - 1 - row, row)
        group = jnp.where(flip == 1, n_base - 1 - group, group)
        col = jnp.where(flip == 1, 15 - col, col)
        k = count[o]
        count[o] = k + 1
        slot = flip * 2 + (k & 1)
        to = group * n_slab + row
        for part in range(2):
            out[to, slot * 4 + part] = residual[i, part : part + 1, :]
            out[to, slot * 4 + 2 + part] = position[i, part : part + 1, :]
        out[to, 16] = jnp.where(lane == slot, (col + 1).astype(f32), out[to, 16])
        return 0

    lax.fori_loop(0, owner.shape[0], step, 0)


def taps(d):
    x = jnp.maximum(1.0 - d * d, 0.0)
    return x * x * x


def grid_kernel(tags, data, out, cells, order):
    slots = tags.shape[0]
    for axis in range(2):
        at = lax.broadcasted_iota(jnp.int32, (TILE, TILE), axis).astype(f32)
        cells[2 * axis] = at * 0.25
        cells[2 * axis + 1] = (float(TILE) - at) * 0.25
    out[...] = jnp.zeros_like(out)

    def scan(s, n):
        order[n] = s
        return n + (tags[s] > 0).astype(jnp.int32)

    n = lax.fori_loop(0, slots, scan, jnp.int32(0), unroll=8)
    for extra in range(GROUP):
        order[n + extra] = 0

    def down(row):
        return jnp.transpose(jnp.broadcast_to(row, (TILE, TILE)))

    def group(g, _):
        for u in range(GROUP):
            at = g * GROUP + u
            s = order[at]
            used = (at < n).astype(f32)
            src, slot = s >> 2, s & 3
            flip = slot >> 1
            t = jnp.maximum(tags[s] - 1, 0)
            value_re = data[src, slot * 4] * used
            value_im = data[src, slot * 4 + 1] * (used * (1.0 - 2.0 * flip.astype(f32)))
            rows = taps(cells[flip] - data[src, slot * 4 + 2] * 0.25)
            cols = taps(cells[2 + flip] - down(data[src, slot * 4 + 3] * 0.25))
            weighted = jnp.concatenate([cols * down(value_re), cols * down(value_im)], axis=1)
            sub = mm(spread(rows, LEFT[6], 1), spread(weighted, RIGHT[6], 0))
            for q in range(4):
                for ri in range(2):
                    out[q, ri, t] += sub[32 * q : 32 * q + 32, 128 * ri : 128 * ri + 128]
        return 0

    lax.fori_loop(0, (n + GROUP - 1) // GROUP, group, 0)


def cols_kernel(x, tw, w, out, mid):
    def rows(i, _):
        at = pl.ds(pl.multiple_of(i * 8, 8), 8)
        first = [(x[b // 16, 0, b % 16, at, :], x[b // 16, 1, b % 16, at, :]) for b in range(64)]
        for c, (re, im) in enumerate(fft_list(first)):
            cos, sin = tw[0, c : c + 1, :], tw[1, c : c + 1, :]
            mid[c, at, 0:128] = re * cos - im * sin
            mid[c, at, 128:256] = re * sin + im * cos
        return 0

    lax.fori_loop(0, 4, rows, 0)
    for pair in range(8):
        part = spread(mid[8 * pair : 8 * pair + 8].reshape(256, 256), RIGHT[6], 1)
        res = mm(w[...], part, NT)
        for k in range(2):
            chunk = 2 * pair + k
            for ri in range(2):
                out[:, chunk // 8, ri * 8 + chunk % 8, :] = res[64 * ri : 64 * ri + 64, 128 * k : 128 * k + 128]


def row_kernel(xi, amplitude, tw, w, out, mid):
    def rows(i, _):
        at = pl.ds(pl.multiple_of(i * 8, 8), 8)
        first = [
            xi[at, 128 * b : 128 * b + 128] * amplitude[at, 128 * b : 128 * b + 128] for b in range(32)
        ]
        half = rfft_list(first)
        for c in range(32):
            cos, sin = tw[0, c : c + 1, :], tw[1, c : c + 1, :]
            re, im = half[c] if c <= 16 else half[32 - c]
            if im is None:
                mid[c, at, 0:128] = re * cos
                mid[c, at, 128:256] = re * sin
            else:
                im = im if c <= 16 else -im
                mid[c, at, 0:128] = re * cos - im * sin
                mid[c, at, 128:256] = re * sin + im * cos
        return 0

    lax.fori_loop(0, 4, rows, 0)
    for pair in range(4):
        part = spread(mid[8 * pair : 8 * pair + 8].reshape(256, 256), RIGHT[3], 1)
        res = mm(w[...], part, NT)
        for k in range(2):
            for ri in range(2):
                out[:, ri * 8 + 2 * pair + k, :] = res[128 * ri : 128 * ri + 128, 128 * k : 128 * k + 128]


def chunks(ref, pair):
    return jnp.concatenate(
        [jnp.concatenate([ref[:, ri * 8 + 2 * pair + k, :] for k in range(2)], axis=1) for ri in range(2)],
        axis=0,
    )


def twist(re, im, tw):
    return re * tw[0] - im * tw[1], re * tw[1] + im * tw[0]


def halves(a, at):
    return [a[at : at + 128, 128 * k : 128 * k + 128] for k in range(2)]


def stacked(rows):
    return jnp.concatenate([jnp.concatenate(r, axis=1) for r in rows], axis=0)


def sky_kernel(field, w, tw, r, out):
    for pair in range(4):
        a = mm(w[...], spread(chunks(field, pair), RIGHT[3], 0))
        turn = stacked([twist(re, im, tw) for re, im in zip(halves(a, 0), halves(a, 128))])
        out[pair] = jnp.exp(mm(spread(turn, LEFT[3], 1), r[...]))


def image_kernel(sky, uv, w, tw_f, r_y, w_b, tw_b, r_b, out):
    for pair in range(4):
        a = mm(w_b[...], spread(chunks(uv, pair), RIGHT[6], 0))
        parts = [[], []]
        for h in range(2):
            for k, (re, im) in enumerate(zip(halves(a, 256 * h), halves(a, 256 * h + 128))):
                parts[k] += twist(re, im, tw_b[h])
        back = mm(spread(stacked(parts), LEFT[6], 1), r_b[...])
        a = mm(spread(sky[pair] * back, LEFT[3], 1), r_y[...])
        turn = [twist(a[128 * k : 128 * k + 128, 0:128], a[128 * k : 128 * k + 128, 128:256], tw_f) for k in range(2)]
        turn = jnp.concatenate([jnp.concatenate([turn[k][ri] for k in range(2)], axis=1) for ri in range(2)], axis=0)
        res = mm(w[...], spread(turn, RIGHT[3], 0))
        for ri in range(2):
            for k in range(2):
                out[:, ri * 8 + 2 * pair + k, :] = res[128 * ri : 128 * ri + 128, 128 * k : 128 * k + 128]


def last_kernel(folded, amplitude, tw, w, out, mid):
    for j in range(8):
        z = jnp.concatenate([folded[:, j, :], folded[:, 8 + j, :]], axis=0)
        v = mm(spread(z, LEFT[3], 0), w[...], TN)
        for k in range(4):
            c = 4 * j + k
            cos, sin = tw[0, c : c + 1, :], tw[1, c : c + 1, :]
            re, im = v[32 * k : 32 * k + 32, 0:128], v[32 * k : 32 * k + 32, 128:256]
            mid[c, :, 0:128] = re * cos - im * sin
            mid[c, :, 128:256] = re * sin + im * cos

    def rows(i, _):
        at = pl.ds(pl.multiple_of(i * 8, 8), 8)
        first = [(mid[c, at, 0:128], mid[c, at, 128:256]) for c in range(32)]
        for b, (re, im) in enumerate(fft_list(first)):
            to = slice(128 * b, 128 * b + 128)
            out[at, to] = amplitude[at, to] * (re + im) * (1.0 / IMG)
        return 0

    lax.fori_loop(0, 4, rows, 0)


def per_device(residual, position, owner, tile_local, xi, amplitude):
    n_base = lax.axis_size("base")
    n_slab = lax.axis_size("slab")
    devices = n_base * n_slab
    everywhere = ("base", "slab")
    t = {k: jnp.asarray(v) for k, v in tables(n_base, n_slab).items()}

    def exchange(a, axis):
        return lax.all_to_all(a, axis, split_axis=0, concat_axis=0, tiled=True)

    packed = call(
        pack_kernel, (devices, 17, 1, 128), [SM, SM, VM, VM], [SM((devices,), jnp.int32)], 2e9
    )(owner[:, 0], tile_local, residual, position)
    data = exchange(packed, everywhere)

    half = call(row_kernel, (devices, 16, 128), [VM] * 4, [VM((32, 32, 256), f32)], 2e9)(
        xi, amplitude, t["tw_row"], t["w128"]
    )
    half = exchange(half, everywhere)

    tags = data[:, 16, 0, 0:4].reshape(4 * devices).astype(jnp.int32)
    grid = call(
        grid_kernel,
        (4, 2, 16, 32, 128),
        [SM, VM],
        [VM((4, TILE, TILE), f32), SM((4 * devices + GROUP,), jnp.int32)],
        4e10,
    )(tags, data)
    grid, half = lax.optimization_barrier((grid, half))
    grid = exchange(grid, "base")
    sky = call(sky_kernel, (4, 256, 128), [VM] * 4, (), 4e9)(half, t["w128"], t["tw_f"], t["r_f"])
    cols = call(cols_kernel, (devices // 2, 2, 16, 128), [VM] * 3, [VM((64, 32, 256), f32)], 4e9)(
        grid, t["tw_cols"], t["w_cols"]
    )
    cols = exchange(cols.reshape(devices, 16, 128), everywhere)
    fold = call(image_kernel, (devices, 16, 128), [VM] * 8, (), 8e9)(
        sky, cols, t["w128"], t["tw_f"], t["r_y"], t["w_b"], t["tw_b"], t["r_b"]
    )
    fold = exchange(fold, everywhere)
    return call(last_kernel, (32, IMG), [VM] * 4, [VM((32, 32, 256), f32)], 3e9)(
        fold, amplitude, t["tw_row"], t["w128t"]
    )


def solution(mesh):
    placed = (
        P(("base", "slab"), None, None),
        P(("base", "slab"), None, None),
        P(("base", "slab"), None),
        P(("base", "slab")),
        P(("base", "slab"), None),
        P(("base", "slab"), None),
    )
    return jax.shard_map(
        per_device, mesh=mesh, in_specs=placed, out_specs=P(("base", "slab"), None), check_vma=False
    )
```

profile of v0, /device:TPU:1, one launch (start us, length us, event | category | flops | bytes accessed | tf_op | source)
XLA Modules:
  0.0 170.5 jit_solution(8440901143381440253)
XLA Ops:
  0.0 0.9 copy-done.3
  0.9 0.9 copy-done.4
  1.8 0.7 copy-done.5
  3.1 4.3 %shard_map.163 = f32[128,17,1,128]{3,2,1,0:T(1,128)} custom-call(s32[128]{0:T(128)S(1)} %bitcast.2, s32[128]{0:T(128)S(1)} %copy-done.6, f32[128,2,128]{2,1,0:T(2,128)S(1)} %copy-done.3, f32[128,2,128]{2,1,0:T(2,128)S(1)} %copy-done.4), custom_call_target="tpu_custom_call" | custom-call | flops 2000000000 | bytes 2228224 | tf_op jit(solution)/shard_map/pallas_call | solution.py:362
  7.4 11.5 %all-to-all-start = ((f32[128,17,1,128]{3,2,1,0:T(1,128)}), f32[128,17,1,128]{3,2,1,0:T(1,128)S(1)}, u32[]{:S(2)}, u32[]{:S(2)}) async-start(f32[128,17,1,128]{3,2,1,0:T(1,128)} %shard_map.163), calls=%async_computation | async-start | bytes 2228224 | tf_op jit(solution)/shard_map/all_to_all | solution.py:360
  19.0 2.2 %shard_map.165 = f32[128,16,128]{2,1,0:T(8,128)} custom-call(f32[32,4096]{1,0:T(8,128)S(1)} %copy-done, f32[32,4096]{1,0:T(8,128)S(1)} %copy-done.1, f32[2,32,128]{2,1,0:T(8,128)S(1)} %copy-done.19, bf16[256,768]{1,0:T(8,128)(2,1)S(1)} %copy-done.9), custom_call_target="tpu_custom_call" | custom-call | flops 2000000000 | bytes 2097152 | tf_op jit(solution)/shard_map/pallas_call | solution.py:367
  21.2 17.5 %all-to-all-done.data = f32[128,17,1,128]{3,2,1,0:T(1,128)S(1)} async-done(((f32[128,17,1,128]{3,2,1,0:T(1,128)}), f32[128,17,1,128]{3,2,1,0:T(1,128)S(1)}, u32[]{:S(2)}, u32[]{:S(2)}) %all-to-all-start) | async-done | bytes 1114144 | tf_op jit(solution)/shard_map/all_to_all | solution.py:360
  38.7 5.6 %all-to-all-start.1 = ((f32[128,16,128]{2,1,0:T(8,128)}), f32[128,16,128]{2,1,0:T(8,128)}, u32[]{:S(2)}, u32[]{:S(2)}) async-start(f32[128,16,128]{2,1,0:T(8,128)} %shard_map.165), calls=%async_computation.1 | async-start | bytes 2097152 | tf_op jit(solution)/shard_map/all_to_all | solution.py:360
  44.7 21.6 %shard_map.164 = f32[4,2,16,32,128]{4,3,2,1,0:T(8,128)S(1)} custom-call(s32[512]{0:T(512)S(1)} %convert_element_type.6.tags, f32[128,17,1,128]{3,2,1,0:T(1,128)S(1)} %all-to-all-done.data), custom_call_target="tpu_custom_call" | custom-call | flops 40000000000 | bytes 4194304 | tf_op jit(solution)/shard_map/pallas_call | solution.py:373
  66.3 26.5 %all_to_all.25.x = f32[4,2,16,32,128]{4,3,2,1,0:T(8,128)S(1)} all-to-all(f32[4,2,16,32,128]{4,3,2,1,0:T(8,128)S(1)} %shard_map.164), channel_id=1, replica_groups=mesh['base'=4,'slab'=32] {'base'}, dimensions={0} | all-to-all | bytes 4194304 | tf_op jit(solution)/shard_map/all_to_all | solution.py:360
  92.9 4.6 %shard_map.167 = f32[64,2,16,128]{3,2,1,0:T(8,128)} custom-call(f32[4,2,16,32,128]{4,3,2,1,0:T(8,128)S(1)} %all_to_all.25.x, f32[2,64,128]{2,1,0:T(8,128)S(1)} %copy-done.18, bf16[128,1536]{1,0:T(8,128)(2,1)S(1)} %copy-done.13), custom_call_target="tpu_custom_call" | custom-call | flops 4000000000 | bytes 2097152 | tf_op jit(solution)/shard_map/pallas_call | solution.py:383
  97.5 16.0 %all-to-all-start.3 = ((f32[128,16,128]{2,1,0:T(8,128)}), f32[128,16,128]{2,1,0:T(8,128)S(1)}, u32[]{:S(2)}, u32[]{:S(2)}) async-start(f32[128,16,128]{2,1,0:T(8,128)} %bitcast.1), calls=%async_computation.3 | async-start | bytes 2097152 | tf_op jit(solution)/shard_map/all_to_all | solution.py:360
  113.5 1.0 copy-done.10
  114.5 0.9 copy-done.16
  115.5 3.2 %shard_map.166.sky = f32[4,256,128]{2,1,0:T(8,128)S(1)} custom-call(f32[128,16,128]{2,1,0:T(8,128)} %all-to-all-done.1.field, bf16[256,768]{1,0:T(8,128)(2,1)S(1)} %copy-done.10, f32[2,128,128]{2,1,0:T(8,128)S(1)} %copy-done.17, bf16[768,128]{1,0:T(8,128)(2,1)S(1)} %copy-done.16), custom_call_target="tpu_custom_call" | custom-call | flops 4000000000 | bytes 1048576 | tf_op jit(solution)/shard_map/pallas_call | solution.py:382
  118.6 0.8 copy-done.21
  119.4 13.2 %all-to-all-done.3.uv = f32[128,16,128]{2,1,0:T(8,128)S(1)} async-done(((f32[128,16,128]{2,1,0:T(8,128)}), f32[128,16,128]{2,1,0:T(8,128)S(1)}, u32[]{:S(2)}, u32[]{:S(2)}) %all-to-all-start.3) | async-done | bytes 1048608 | tf_op jit(solution)/shard_map/all_to_all | solution.py:360
  132.6 1.0 copy-done.11
  133.6 0.9 copy-done.14
  134.5 0.9 copy-done.15
  135.5 1.0 copy-done.22
  136.5 8.1 %shard_map.168 = f32[128,16,128]{2,1,0:T(8,128)S(1)} custom-call(f32[4,256,128]{2,1,0:T(8,128)S(1)} %copy-done.22, f32[128,16,128]{2,1,0:T(8,128)S(1)} %all-to-all-done.3.uv, bf16[256,768]{1,0:T(8,128)(2,1)S(1)} %copy-done.11, f32[2,128,128]{2,1,0:T(8,128)S(1)} %copy-done.17, bf16[384,256]{1,0:T(8,128)(2,1)S(1)} %copy-done.15, ...), custom_call_target="tpu_custom_call" | custom-call | flops 8000000000 | bytes 2097152 | tf_op jit(solution)/shard_map/pallas_call | solution.py:387
  144.6 23.6 %all_to_all.26.folded = f32[128,16,128]{2,1,0:T(8,128)S(1)} all-to-all(f32[128,16,128]{2,1,0:T(8,128)S(1)} %shard_map.168), channel_id=1, replica_groups=mesh['base'=4,'slab'=32] {'base','slab'}, dimensions={0} | all-to-all | bytes 2097152 | tf_op jit(solution)/shard_map/all_to_all | solution.py:360
  168.2 2.2 %shard_map.169 = f32[32,4096]{1,0:T(8,128)} custom-call(f32[128,16,128]{2,1,0:T(8,128)S(1)} %all_to_all.26.folded, f32[32,4096]{1,0:T(8,128)S(1)} %copy-done.2, f32[2,32,128]{2,1,0:T(8,128)S(1)} %copy-done.20, bf16[768,256]{1,0:T(8,128)(2,1)S(1)} %copy-done.12), custom_call_target="tpu_custom_call" | custom-call | flops 3000000000 | bytes 1048576 | tf_op jit(solution)/shard_map/pallas_call | solution.py:391
  (39 shorter events, 1.0 us)
Async XLA Ops:
  0.0 0.9 copy-start.3
  0.9 0.9 copy-start.4
  7.4 11.5 %copy-start = (f32[32,4096]{1,0:T(8,128)S(1)}, f32[32,4096]{1,0:T(8,128)}, u32[]{:S(2)}) copy-start(f32[32,4096]{1,0:T(8,128)} %xi.1) | copy-start | bytes 1572868
  7.4 11.5 %copy-start.1 = (f32[32,4096]{1,0:T(8,128)S(1)}, f32[32,4096]{1,0:T(8,128)}, u32[]{:S(2)}) copy-start(f32[32,4096]{1,0:T(8,128)} %amplitude.3) | copy-start | bytes 1572868
  7.4 11.5 %copy-start.9 = (bf16[256,768]{1,0:T(8,128)(2,1)S(1)}, bf16[256,768]{1,0:T(8,128)(2,1)}, u32[]{:S(2)}) copy-start(bf16[256,768]{1,0:T(8,128)(2,1)} %constant.22.clone.w) | copy-start | bytes 1179652
  7.4 11.6 %copy-start.19 = (f32[2,32,128]{2,1,0:T(8,128)S(1)}, f32[2,32,128]{2,1,0:T(8,128)}, u32[]{:S(2)}) copy-start(f32[2,32,128]{2,1,0:T(8,128)} %constant.24.clone.tw) | copy-start | bytes 98308
  7.4 31.3 %all-to-all-start = ((f32[128,17,1,128]{3,2,1,0:T(1,128)}), f32[128,17,1,128]{3,2,1,0:T(1,128)S(1)}, u32[]{:S(2)}, u32[]{:S(2)}) async-start(f32[128,17,1,128]{3,2,1,0:T(1,128)} %shard_map.163), calls=%async_computation | async-start | bytes 2228224 | tf_op jit(solution)/shard_map/all_to_all | solution.py:360
  38.7 27.6 %all-to-all-start.1 = ((f32[128,16,128]{2,1,0:T(8,128)}), f32[128,16,128]{2,1,0:T(8,128)}, u32[]{:S(2)}, u32[]{:S(2)}) async-start(f32[128,16,128]{2,1,0:T(8,128)} %shard_map.165), calls=%async_computation.1 | async-start | bytes 2097152 | tf_op jit(solution)/shard_map/all_to_all | solution.py:360
  66.3 26.6 %copy-start.13 = (bf16[128,1536]{1,0:T(8,128)(2,1)S(1)}, bf16[128,1536]{1,0:T(8,128)(2,1)}, u32[]{:S(2)}) copy-start(bf16[128,1536]{1,0:T(8,128)(2,1)} %constant.25.clone.w) | copy-start | bytes 1179652
  66.3 26.6 %copy-start.18 = (f32[2,64,128]{2,1,0:T(8,128)S(1)}, f32[2,64,128]{2,1,0:T(8,128)}, u32[]{:S(2)}) copy-start(f32[2,64,128]{2,1,0:T(8,128)} %constant.26.clone.tw) | copy-start | bytes 196612
  97.5 16.0 %copy-start.17 = (f32[2,128,128]{2,1,0:T(8,128)S(1)}, f32[2,128,128]{2,1,0:T(8,128)}, u32[]{:S(2)}) copy-start(f32[2,128,128]{2,1,0:T(8,128)} %constant.27.clone.tw.tw_f) | copy-start | bytes 393220
  97.5 35.1 %all-to-all-start.3 = ((f32[128,16,128]{2,1,0:T(8,128)}), f32[128,16,128]{2,1,0:T(8,128)S(1)}, u32[]{:S(2)}, u32[]{:S(2)}) async-start(f32[128,16,128]{2,1,0:T(8,128)} %bitcast.1), calls=%async_computation.3 | async-start | bytes 2097152 | tf_op jit(solution)/shard_map/all_to_all | solution.py:360
  113.5 1.0 copy-start.10
  114.5 0.9 copy-start.16
  115.4 17.1 %copy-start.7 = (bf16[512,1536]{1,0:T(8,128)(2,1)S(1)}, bf16[512,1536]{1,0:T(8,128)(2,1)}, u32[]{:S(2)}) copy-start(bf16[512,1536]{1,0:T(8,128)(2,1)} %constant.30.clone.w_b) | copy-start | bytes 4718596
  115.4 17.1 %copy-start.8 = (bf16[3072,128]{1,0:T(8,128)(2,1)S(1)}, bf16[3072,128]{1,0:T(8,128)(2,1)}, u32[]{:S(2)}) copy-start(bf16[3072,128]{1,0:T(8,128)(2,1)} %constant.32.clone.r_b) | copy-start | bytes 2359300
  118.6 0.8 copy-start.21
  132.6 1.0 copy-start.11
  133.6 0.9 copy-start.14
  134.5 0.9 copy-start.15
  135.5 1.0 copy-start.22
  144.6 23.6 %copy-start.2 = (f32[32,4096]{1,0:T(8,128)S(1)}, f32[32,4096]{1,0:T(8,128)}, u32[]{:S(2)}) copy-start(f32[32,4096]{1,0:T(8,128)} %amplitude.3) | copy-start | bytes 1572868
  144.6 23.6 %copy-start.12 = (bf16[768,256]{1,0:T(8,128)(2,1)S(1)}, bf16[768,256]{1,0:T(8,128)(2,1)}, u32[]{:S(2)}) copy-start(bf16[768,256]{1,0:T(8,128)(2,1)} %constant.23.clone.w) | copy-start | bytes 1179652
  144.6 23.6 %copy-start.20 = (f32[2,32,128]{2,1,0:T(8,128)S(1)}, f32[2,32,128]{2,1,0:T(8,128)}, u32[]{:S(2)}) copy-start(f32[2,32,128]{2,1,0:T(8,128)} %constant.24.clone.tw) | copy-start | bytes 98308
  (2 other events, 1.3 us)
where the time goes:
time: 173 us; the launch traced here: 170 us
  blocking collectives  50.1 us (29%)
  Pallas kernels  46.2 us (27%)
  starting transfers between devices  33.2 us (19%)
  waiting for transfers between devices  30.7 us (18%)
  local copies, waits for them, and re-layouts  9.9 us (6%)
    all_to_all x2, blocking collectives, exchange(): return lax.all_to_all(a, axis, split_axis=0, concat_axis=0, tiled=True)  50.1 us
    all_to_all x3, starting transfers between devices, exchange(): return lax.all_to_all(a, axis, split_axis=0, concat_axis=0, tiled=True)  33.2 us
    all_to_all x3, waiting for transfers between devices, exchange(): return lax.all_to_all(a, axis, split_axis=0, concat_axis=0, tiled=True)  30.7 us
    pallas_call x1, Pallas kernels, per_device(): call(grid_kernel, (4, 2, 16, 32, 128), [SM, VM], [VM((4, TILE, TILE), f32...  21.6 us
    unnamed x46, local copies, waits for them, and re-layouts  9.8 us
    pallas_call x1, Pallas kernels, per_device(): call(image_kernel, (devices, 16, 128), [VM] * 8, (), 8000000000.0)  8.09 us
    pallas_call x1, Pallas kernels, per_device(): call(cols_kernel, (devices // 2, 2, 16, 128), [VM] * 3, [VM((64, 32, 256)...  4.61 us
    pallas_call x1, Pallas kernels, per_device(): call(pack_kernel, (devices, 17, 1, 128), [SM, SM, VM, VM], [SM((devices,)...  4.31 us
  transfers between devices with their start and end apart: 3, of which 2 were waited for; matrix products, arithmetic and copies ran while one was open for 0% of the time, Pallas kernels for 16%

commit v1 on v0

--- a/solution.py
+++ b/solution.py
@@ -14,6 +14,7 @@
 IMG = 4096
 TILE = 128
 GROUP = 8
+GRANT = 20 * 2**20
 
 NN = (((1,), (0,)), ((), ()))
 NT = (((1,), (1,)), ((), ()))
@@ -73,7 +74,7 @@
     out["tw_row"] = np.stack(wave(n(32), n(128), IMG))
     c, s = wave(n(64) + 32, n(128), 128)
     out["w_cols"] = spread_table(turned(c, s), LEFT[6], 1)
-    out["tw_cols"] = np.stack(wave(n(64), n(128), G))
+    out["tw_cols"] = np.stack([np.stack(wave(n(64), n(128) + G // n_base * me, G)) for me in range(n_base)])
     eye = np.eye(4)
     c, s = wave(n(128), n(32), IMG)
     out["tw_f"] = np.stack([np.tile(c, (1, 4)), np.tile(s, (1, 4))])
@@ -141,17 +142,57 @@
     return out
 
 
-def call(body, out_shape, in_specs, scratch=(), flops=0):
-    nbytes = 4 * math.prod(out_shape)
-    return pl.pallas_call(
-        body,
-        out_shape=jax.ShapeDtypeStruct(out_shape, f32),
-        in_specs=[pl.BlockSpec(memory_space=m) for m in in_specs],
-        out_specs=pl.BlockSpec(memory_space=pltpu.VMEM),
-        scratch_shapes=list(scratch),
-        compiler_params=pltpu.CompilerParams(vmem_limit_bytes=48 * 2**20),
-        cost_estimate=pl.CostEstimate(flops=int(flops), bytes_accessed=2 * nbytes, transcendentals=0),
+def call(body, out_shapes, in_specs, scratch=(), flops=0, far=(), far_out=False):
+    outs = [out_shapes] if isinstance(out_shapes[0], int) else list(out_shapes)
+    count, own, made = len(in_specs), len(scratch), len(outs)
+    specs = [pl.BlockSpec(memory_space=m) for m in in_specs]
+    for i, _ in far:
+        specs[i] = pl.BlockSpec(memory_space=pltpu.HBM)
+
+    def kernel(*refs):
+        ins, results = list(refs[:count]), list(refs[count : count + made])
+        rest = refs[count + made : count + made + own]
+        spare = refs[count + made + own :]
+        copies = []
+        for k, (i, _) in enumerate(far):
+            copies.append(pltpu.make_async_copy(ins[i], spare[k], spare[-1].at[k]))
+            ins[i] = spare[k]
+        for c in copies:
+            c.start()
+        for c in copies:
+            c.wait()
+        if not far_out:
+            body(*ins, *results, *rest)
+            return
+        body(*ins, spare[len(far)], *rest)
+        last = pltpu.make_async_copy(spare[len(far)], results[0], spare[-1].at[len(far)])
+        last.start()
+        last.wait()
+
+    more = [shape for _, shape in far] + ([VM(outs[0], f32)] if far_out else [])
+    if more:
+        more.append(pltpu.SemaphoreType.DMA((len(more),)))
+    made_in = pltpu.HBM if far_out else pltpu.VMEM
+    got = pl.pallas_call(
+        kernel,
+        out_shape=[(pltpu.HBM if far_out else jax.ShapeDtypeStruct)(shape, f32) for shape in outs],
+        in_specs=specs,
+        out_specs=[pl.BlockSpec(memory_space=made_in)] * made,
+        scratch_shapes=list(scratch) + more,
+        compiler_params=pltpu.CompilerParams(vmem_limit_bytes=GRANT),
+        cost_estimate=pl.CostEstimate(
+            flops=int(flops), bytes_accessed=8 * sum(map(math.prod, outs)), transcendentals=0
+        ),
     )
+
+    def placed(*arrays):
+        arrays = list(arrays)
+        for i, _ in far:
+            arrays[i] = pltpu.with_memory_space_constraint(arrays[i], pltpu.HBM)
+        results = got(*arrays)
+        return results[0] if isinstance(out_shapes[0], int) else results
+
+    return placed
 
 
 VM = pltpu.VMEM
@@ -195,17 +236,28 @@
     return x * x * x
 
 
-def grid_kernel(tags, data, out, cells, order):
-    slots = tags.shape[0]
+def grid_whole_kernel(first, tags, data, total, cells, order):
+    grid_into(first, 0, tags, data, total, cells, order)
+
+
+def grid_parts_kernel(first, me, tags, data, out0, out1, out2, out3, cells, order, total):
+    grid_into(first, me[0], tags, data, total, cells, order)
+    for k, out in enumerate((out0, out1, out2, out3)):
+        out[...] = total[k]
+
+
+def grid_into(first, me, tags, data, total, cells, order):
+    slots, wide = tags.shape[0], total.shape[2]
     for axis in range(2):
         at = lax.broadcasted_iota(jnp.int32, (TILE, TILE), axis).astype(f32)
         cells[2 * axis] = at * 0.25
         cells[2 * axis + 1] = (float(TILE) - at) * 0.25
-    out[...] = jnp.zeros_like(out)
+    total[...] = jnp.zeros_like(total)
 
     def scan(s, n):
         order[n] = s
-        return n + (tags[s] > 0).astype(jnp.int32)
+        tag = tags[s] - first
+        return n + ((tag > 0) & (tag <= wide)).astype(jnp.int32)
 
     n = lax.fori_loop(0, slots, scan, jnp.int32(0), unroll=8)
     for extra in range(GROUP):
@@ -221,7 +273,7 @@
             used = (at < n).astype(f32)
             src, slot = s >> 2, s & 3
             flip = slot >> 1
-            t = jnp.maximum(tags[s] - 1, 0)
+            t = jnp.clip(tags[s] - first - 1, 0, wide - 1)
             value_re = data[src, slot * 4] * used
             value_im = data[src, slot * 4 + 1] * (used * (1.0 - 2.0 * flip.astype(f32)))
             rows = taps(cells[flip] - data[src, slot * 4 + 2] * 0.25)
@@ -230,18 +282,26 @@
             sub = mm(spread(rows, LEFT[6], 1), spread(weighted, RIGHT[6], 0))
             for q in range(4):
                 for ri in range(2):
-                    out[q, ri, t] += sub[32 * q : 32 * q + 32, 128 * ri : 128 * ri + 128]
+                    total[(q - me) & 3, ri, t] += sub[32 * q : 32 * q + 32, 128 * ri : 128 * ri + 128]
         return 0
 
     lax.fori_loop(0, (n + GROUP - 1) // GROUP, group, 0)
 
 
-def cols_kernel(x, tw, w, out, mid):
+def cols_kernel(*refs):
+    me, whole, parts, (tw, w, out, mid) = refs[0], refs[1], refs[2:6], refs[6:]
+
+    def tile(b, ri, at):
+        group = b // 16
+        if b % 16 < 8:
+            return whole[(me[0] + group) & 3, ri, b % 8, at, :]
+        return parts[-group % 4][ri, b % 8, at, :]
+
     def rows(i, _):
         at = pl.ds(pl.multiple_of(i * 8, 8), 8)
-        first = [(x[b // 16, 0, b % 16, at, :], x[b // 16, 1, b % 16, at, :]) for b in range(64)]
+        first = [(tile(b, 0, at), tile(b, 1, at)) for b in range(64)]
         for c, (re, im) in enumerate(fft_list(first)):
-            cos, sin = tw[0, c : c + 1, :], tw[1, c : c + 1, :]
+            cos, sin = tw[me[0], 0, c : c + 1, :], tw[me[0], 1, c : c + 1, :]
             mid[c, at, 0:128] = re * cos - im * sin
             mid[c, at, 128:256] = re * sin + im * cos
         return 0
@@ -359,34 +419,97 @@
     def exchange(a, axis):
         return lax.all_to_all(a, axis, split_axis=0, concat_axis=0, tiled=True)
 
+    rows, width = xi.shape
+    blocks = residual.shape[0]
+    me = lax.axis_index("base").astype(jnp.int32).reshape(1)
     packed = call(
-        pack_kernel, (devices, 17, 1, 128), [SM, SM, VM, VM], [SM((devices,), jnp.int32)], 2e9
+        pack_kernel,
+        (devices, 17, 1, 128),
+        [SM, SM, VM, VM],
+        [SM((devices,), jnp.int32)],
+        2e9,
+        [
+            (0, SM((blocks,), jnp.int32)),
+            (1, SM((blocks,), jnp.int32)),
+            (2, VM(residual.shape, f32)),
+            (3, VM(position.shape, f32)),
+        ],
     )(owner[:, 0], tile_local, residual, position)
     data = exchange(packed, everywhere)
-
-    half = call(row_kernel, (devices, 16, 128), [VM] * 4, [VM((32, 32, 256), f32)], 2e9)(
-        xi, amplitude, t["tw_row"], t["w128"]
-    )
+    half = call(
+        row_kernel,
+        (devices, 16, 128),
+        [VM] * 4,
+        [VM((32, 32, 256), f32)],
+        2e9,
+        [
+            (0, VM((rows, width), f32)),
+            (1, VM((rows, width), f32)),
+            (2, VM((2, 32, 128), f32)),
+            (3, VM((256, 768), bf16)),
+        ],
+        True,
+    )(xi, amplitude, t["tw_row"], t["w128"])
+
+    data, half = lax.optimization_barrier((data, half))
+    tags = data[:, 16, 0, 0:4].reshape(4 * devices).astype(jnp.int32)
+    spare = [VM((4, TILE, TILE), f32), SM((4 * devices + GROUP,), jnp.int32)]
+    shape = (2, 8, 32, 128)
+    whole = call(
+        functools.partial(grid_whole_kernel, 0), (n_base, *shape), [SM, VM], spare, 2e10
+    )(tags, data)
+    whole, tags = lax.optimization_barrier((whole, tags))
+    whole = exchange(whole, "base")
+    parts = call(
+        functools.partial(grid_parts_kernel, 8),
+        [shape] * n_base,
+        [SM, SM, VM],
+        [*spare, VM((n_base, *shape), f32)],
+        2e10,
+    )(me, tags, data)
+    parts, half = lax.optimization_barrier((parts, half))
+    parts = [parts[0]] + [
+        lax.ppermute(parts[k], "base", [(i, (i + k) % n_base) for i in range(n_base)]) for k in range(1, n_base)
+    ]
     half = exchange(half, everywhere)
-
-    tags = data[:, 16, 0, 0:4].reshape(4 * devices).astype(jnp.int32)
-    grid = call(
-        grid_kernel,
-        (4, 2, 16, 32, 128),
-        [SM, VM],
-        [VM((4, TILE, TILE), f32), SM((4 * devices + GROUP,), jnp.int32)],
-        4e10,
-    )(tags, data)
-    grid, half = lax.optimization_barrier((grid, half))
-    grid = exchange(grid, "base")
-    sky = call(sky_kernel, (4, 256, 128), [VM] * 4, (), 4e9)(half, t["w128"], t["tw_f"], t["r_f"])
-    cols = call(cols_kernel, (devices // 2, 2, 16, 128), [VM] * 3, [VM((64, 32, 256), f32)], 4e9)(
-        grid, t["tw_cols"], t["w_cols"]
-    )
+    cols = call(
+        cols_kernel,
+        (devices // 2, 2, 16, 128),
+        [SM] + [VM] * 7,
+        [VM((64, 32, 256), f32)],
+        4e9,
+    )(me, whole, *parts, t["tw_cols"], t["w_cols"])
     cols = exchange(cols.reshape(devices, 16, 128), everywhere)
-    fold = call(image_kernel, (devices, 16, 128), [VM] * 8, (), 8e9)(
-        sky, cols, t["w128"], t["tw_f"], t["r_y"], t["w_b"], t["tw_b"], t["r_b"]
-    )
+    sky = call(
+        sky_kernel,
+        (4, 256, 128),
+        [VM] * 4,
+        (),
+        4e9,
+        [
+            (0, VM((devices, 16, 128), f32)),
+            (1, VM((256, 768), bf16)),
+            (2, VM((2, 128, 128), f32)),
+            (3, VM((768, 128), bf16)),
+        ],
+        True,
+    )(half, t["w128"], t["tw_f"], t["r_f"])
+    fold = call(
+        image_kernel,
+        (devices, 16, 128),
+        [VM] * 8,
+        (),
+        8e9,
+        [
+            (0, VM((4, 256, 128), f32)),
+            (2, VM((256, 768), bf16)),
+            (3, VM((2, 128, 128), f32)),
+            (4, VM((384, 256), bf16)),
+            (5, VM((512, 1536), bf16)),
+            (6, VM((2, 2, 128, 128), f32)),
+            (7, VM((3072, 128), bf16)),
+        ],
+    )(sky, cols, t["w128"], t["tw_f"], t["r_y"], t["w_b"], t["tw_b"], t["r_b"])
     fold = exchange(fold, everywhere)
     return call(last_kernel, (32, IMG), [VM] * 4, [VM((32, 32, 256), f32)], 3e9)(
         fold, amplitude, t["tw_row"], t["w128t"]

time: 173 us -> 169 us (0.977); the launches traced: 170 us -> 171 us
  blocking collectives: 50.1 us -> 23.6 us
  waiting for transfers between devices: 30.7 us -> 53.9 us
  Pallas kernels: 46.2 us -> 56.6 us
  local copies, waits for them, and re-layouts: 9.9 us -> 0.14 us
  starting transfers between devices: 33.2 us -> 36.5 us
    all_to_all x2 -> x1, blocking collectives: 50.1 us -> 23.6 us  [exchange(): return lax.all_to_all(a, axis, split_axis=0, concat_axis=0, tiled=True)]
    ppermute x0 -> x3, waiting for transfers between devices: none -> 20 us  [per_device(): lax.ppermute(parts[k], 'base', [(i, (i + k) % n_base) for i in range(n_ba...]
    pallas_call x7 -> x8, Pallas kernels: 46.2 us -> 56.6 us  [placed(): results = got(*arrays)]
    unnamed x46 -> x10, local copies, waits for them, and re-layouts: 9.8 us -> 0.03 us
    ppermute x0 -> x3, starting transfers between devices: none -> 5.03 us  [per_device(): lax.ppermute(parts[k], 'base', [(i, (i + k) % n_base) for i in range(n_ba...]
    all_to_all x3 -> x4, waiting for transfers between devices: 30.7 us -> 33.9 us  [exchange(): return lax.all_to_all(a, axis, split_axis=0, concat_axis=0, tiled=True)]
    all_to_all x3 -> x4, starting transfers between devices: 33.2 us -> 31.4 us  [exchange(): return lax.all_to_all(a, axis, split_axis=0, concat_axis=0, tiled=True)]
  transfers between devices with their start and end apart: 3 -> 7, of which waited for: 2 -> 5; matrix products, arithmetic and copies ran while one was open for 0% -> 0% of each run, Pallas kernels for 16% -> 15%
where the time goes in v1:
time: 169 us; the launch traced here: 171 us
  Pallas kernels  56.6 us (33%)
  waiting for transfers between devices  53.9 us (32%)
  starting transfers between devices  36.5 us (22%)
  blocking collectives  23.6 us (14%)
    pallas_call x8, Pallas kernels, placed(): results = got(*arrays)  56.6 us
    all_to_all x4, waiting for transfers between devices, exchange(): return lax.all_to_all(a, axis, split_axis=0, concat_axis=0, tiled=True)  33.9 us
    all_to_all x4, starting transfers between devices, exchange(): return lax.all_to_all(a, axis, split_axis=0, concat_axis=0, tiled=True)  31.4 us
    all_to_all x1, blocking collectives, exchange(): return lax.all_to_all(a, axis, split_axis=0, concat_axis=0, tiled=True)  23.6 us
    ppermute x3, waiting for transfers between devices, per_device(): lax.ppermute(parts[k], 'base', [(i, (i + k) % n_base) for i in range(n_ba...  20 us
    ppermute x3, starting transfers between devices, per_device(): lax.ppermute(parts[k], 'base', [(i, (i + k) % n_base) for i in range(n_ba...  5.03 us
  transfers between devices with their start and end apart: 7, of which 5 were waited for; matrix products, arithmetic and copies ran while one was open for 0% of the time, Pallas kernels for 15%

profile of v1, /device:TPU:1, one launch (start us, length us, event | category | flops | bytes accessed | tf_op | source)
XLA Modules:
  0.0 171.0 jit_solution(5574163705110584240)
XLA Ops:
  0.0 4.8 %shard_map.163 = f32[128,17,1,128]{3,2,1,0:T(1,128)} custom-call(s32[128]{0:T(128)} %bitcast.3, s32[128]{0:T(128)} %refs_1_.4, f32[128,2,128]{2,1,0:T(2,128)} %refs_2_.5, f32[128,2,128]{2,1,0:T(2,128)} %refs_3_.5), custom_call_target="tpu_custom_call" | custom-call | flops 2000000000 | bytes 2228224 | tf_op jit(solution)/shard_map/pallas_call | solution.py:192
  4.8 11.5 %all-to-all-start = ((f32[128,17,1,128]{3,2,1,0:T(1,128)}), f32[128,17,1,128]{3,2,1,0:T(1,128)S(1)}, u32[]{:S(2)}, u32[]{:S(2)}) async-start(f32[128,17,1,128]{3,2,1,0:T(1,128)} %shard_map.163), calls=%async_computation | async-start | bytes 2228224 | tf_op jit(solution)/shard_map/all_to_all | solution.py:420
  16.4 3.6 %shard_map.164 = f32[128,16,128]{2,1,0:T(8,128)} custom-call(f32[32,4096]{1,0:T(8,128)} %refs_0_.1, f32[32,4096]{1,0:T(8,128)} %refs_1_.6, f32[2,32,128]{2,1,0:T(8,128)} %constant.30.clone.refs_2_, bf16[256,768]{1,0:T(8,128)(2,1)} %constant.28.clone.refs_3_.refs_1_.refs_2_), custom_call_target="tpu_custom_call" | custom-call | flops 2000000000 | bytes 2097152 | tf_op jit(solution)/shard_map/pallas_call | solution.py:192
  20.0 16.1 %all-to-all-done.refs_1_.refs_2_ = f32[128,17,1,128]{3,2,1,0:T(1,128)S(1)} async-done(((f32[128,17,1,128]{3,2,1,0:T(1,128)}), f32[128,17,1,128]{3,2,1,0:T(1,128)S(1)}, u32[]{:S(2)}, u32[]{:S(2)}) %all-to-all-start) | async-done | bytes 1114144 | tf_op jit(solution)/shard_map/all_to_all | solution.py:420
  36.1 0.2 convert_reduce_fusion
  36.3 0.1 convert_element_type.6.refs_0_.refs_1_
  36.4 14.4 %shard_map.165 = f32[4,2,8,32,128]{4,3,2,1,0:T(8,128)} custom-call(s32[512]{0:T(512)S(1)} %convert_element_type.6.refs_0_.refs_1_, f32[128,17,1,128]{3,2,1,0:T(1,128)S(1)} %all-to-all-done.refs_1_.refs_2_), custom_call_target="tpu_custom_call" | custom-call | flops 20000000000 | bytes 2097152 | tf_op jit(solution)/shard_map/pallas_call | solution.py:192
  50.8 3.5 %all-to-all-start.2 = ((f32[4,2,8,32,128]{4,3,2,1,0:T(8,128)}), f32[4,2,8,32,128]{4,3,2,1,0:T(8,128)S(1)}, u32[]{:S(2)}, u32[]{:S(2)}) async-start(f32[4,2,8,32,128]{4,3,2,1,0:T(8,128)} %shard_map.165), calls=%async_computation.2 | async-start | bytes 2097152 | tf_op jit(solution)/shard_map/all_to_all | solution.py:420
  54.3 12.7 %shard_map.166 = (f32[2,8,32,128]{3,2,1,0:T(8,128)S(1)}, f32[2,8,32,128]{3,2,1,0:T(8,128)S(1)}, f32[2,8,32,128]{3,2,1,0:T(8,128)S(1)}, f32[2,8,32,128]{3,2,1,0:T(8,128)S(1)}) custom-call(s32[1]{0:T(128)} %bitcast.refs_0_, s32[512]{0:T(512)S(1)} %convert_element_type.6.refs_0_.refs_1_, f32[128,17,1,128]{3,2,1,0:T(1,128)S(1)} %all-to-all-done.refs_1_.refs_2_), custom_call_target="tpu_custom_call" | custom-call | flops 20000000000 | bytes 2097152 | tf_op jit(solution)/shard_map/pallas_call | solution.py:192
  67.0 0.0 copy-start.3
  67.0 2.7 %all-to-all-done.2.refs_1_ = f32[4,2,8,32,128]{4,3,2,1,0:T(8,128)S(1)} async-done(((f32[4,2,8,32,128]{4,3,2,1,0:T(8,128)}), f32[4,2,8,32,128]{4,3,2,1,0:T(8,128)S(1)}, u32[]{:S(2)}, u32[]{:S(2)}) %all-to-all-start.2) | async-done | bytes 1048608 | tf_op jit(solution)/shard_map/all_to_all | solution.py:420
  69.8 8.1 %all-to-all-start.1 = ((f32[128,16,128]{2,1,0:T(8,128)}), f32[128,16,128]{2,1,0:T(8,128)}, u32[]{:S(2)}, u32[]{:S(2)}) async-start(f32[128,16,128]{2,1,0:T(8,128)} %shard_map.164), calls=%async_computation.1 | async-start | bytes 2097152 | tf_op jit(solution)/shard_map/all_to_all | solution.py:420
  77.9 1.5 collective-permute-start
  79.4 2.4 %collective-permute-start.1 = (f32[2,8,32,128]{3,2,1,0:T(8,128)S(1)}, f32[2,8,32,128]{3,2,1,0:T(8,128)S(1)}, u32[]{:S(2)}, u32[]{:S(2)}) collective-permute-start(f32[2,8,32,128]{3,2,1,0:T(8,128)S(1)} %get-tuple-element.29), channel_id=1, source_target_pairs={{0,64},{32,96},{64,0},{96,32},{1,65},{33,97},{65,1},{97,33},{2,66}... | collective-permute-start | bytes 786440 | tf_op jit(solution)/shard_map/ppermute | solution.py:472
  81.8 1.2 collective-permute-start.2
  83.0 14.3 %collective-permute-done.refs_3_ = f32[2,8,32,128]{3,2,1,0:T(8,128)S(1)} collective-permute-done((f32[2,8,32,128]{3,2,1,0:T(8,128)S(1)}, f32[2,8,32,128]{3,2,1,0:T(8,128)S(1)}, u32[]{:S(2)}, u32[]{:S(2)}) %collective-permute-start) | collective-permute-done | bytes 262176 | tf_op jit(solution)/shard_map/ppermute | solution.py:472
  97.3 5.7 %collective-permute-done.1.refs_4_ = f32[2,8,32,128]{3,2,1,0:T(8,128)S(1)} collective-permute-done((f32[2,8,32,128]{3,2,1,0:T(8,128)S(1)}, f32[2,8,32,128]{3,2,1,0:T(8,128)S(1)}, u32[]{:S(2)}, u32[]{:S(2)}) %collective-permute-start.1) | collective-permute-done | bytes 262176 | tf_op jit(solution)/shard_map/ppermute | solution.py:472
  102.9 4.6 %shard_map.168 = f32[64,2,16,128]{3,2,1,0:T(8,128)} custom-call(s32[1]{0:T(128)} %bitcast.refs_0_, f32[4,2,8,32,128]{4,3,2,1,0:T(8,128)S(1)} %all-to-all-done.2.refs_1_, f32[2,8,32,128]{3,2,1,0:T(8,128)S(1)} %get-tuple-element.27.refs_2_, f32[2,8,32,128]{3,2,1,0:T(8,128)S(1)} %collective-permute-done.refs_3_, ...), custom_call_target="tpu_custom_call" | custom-call | flops 4000000000 | bytes 2097152 | tf_op jit(solution)/shard_map/pallas_call | solution.py:192
  107.5 8.3 %all-to-all-start.3 = ((f32[128,16,128]{2,1,0:T(8,128)}), f32[128,16,128]{2,1,0:T(8,128)S(1)}, u32[]{:S(2)}, u32[]{:S(2)}) async-start(f32[128,16,128]{2,1,0:T(8,128)} %bitcast.2), calls=%async_computation.3 | async-start | bytes 2097152 | tf_op jit(solution)/shard_map/all_to_all | solution.py:420
  115.8 4.0 %shard_map.167.refs_0_ = f32[4,256,128]{2,1,0:T(8,128)} custom-call(f32[128,16,128]{2,1,0:T(8,128)} %all-to-all-done.1.refs_0_, bf16[256,768]{1,0:T(8,128)(2,1)} %constant.28.clone.refs_3_.refs_1_.refs_2_, f32[2,128,128]{2,1,0:T(8,128)} %constant.33.clone.refs_2_.refs_3_, bf16[768,128]{1,0:T(8,128)(2,1)} %constant.34.clone.refs_3_), custom_call_target="tpu_custom_call" | custom-call | flops 4000000000 | bytes 1048576 | tf_op jit(solution)/shard_map/pallas_call | solution.py:192
  119.9 15.0 %all-to-all-done.3.refs_1_ = f32[128,16,128]{2,1,0:T(8,128)S(1)} async-done(((f32[128,16,128]{2,1,0:T(8,128)}), f32[128,16,128]{2,1,0:T(8,128)S(1)}, u32[]{:S(2)}, u32[]{:S(2)}) %all-to-all-start.3) | async-done | bytes 1048608 | tf_op jit(solution)/shard_map/all_to_all | solution.py:420
  134.9 10.2 %shard_map.169 = f32[128,16,128]{2,1,0:T(8,128)S(1)} custom-call(f32[4,256,128]{2,1,0:T(8,128)} %shard_map.167.refs_0_, f32[128,16,128]{2,1,0:T(8,128)S(1)} %all-to-all-done.3.refs_1_, bf16[256,768]{1,0:T(8,128)(2,1)} %constant.28.clone.refs_3_.refs_1_.refs_2_, f32[2,128,128]{2,1,0:T(8,128)} %constant.33.clone.refs_2_.refs_3_, ...), custom_call_target="tpu_custom_call" | custom-call | flops 8000000000 | bytes 2097152 | tf_op jit(solution)/shard_map/pallas_call | solution.py:192
  145.2 23.6 %all_to_all.25.refs_0_ = f32[128,16,128]{2,1,0:T(8,128)S(1)} all-to-all(f32[128,16,128]{2,1,0:T(8,128)S(1)} %shard_map.169), channel_id=1, replica_groups=mesh['base'=4,'slab'=32] {'base','slab'}, dimensions={0} | all-to-all | bytes 2097152 | tf_op jit(solution)/shard_map/all_to_all | solution.py:420
  168.7 2.3 %shard_map.170 = f32[32,4096]{1,0:T(8,128)} custom-call(f32[128,16,128]{2,1,0:T(8,128)S(1)} %all_to_all.25.refs_0_, f32[32,4096]{1,0:T(8,128)S(1)} %copy-done, f32[2,32,128]{2,1,0:T(8,128)S(1)} %copy-done.4, bf16[768,256]{1,0:T(8,128)(2,1)S(1)} %copy-done.1), custom_call_target="tpu_custom_call" | custom-call | flops 3000000000 | bytes 1048576 | tf_op jit(solution)/shard_map/pallas_call | solution.py:192
  (11 shorter events, 0.0 us)
Async XLA Ops:
  4.8 31.3 %all-to-all-start = ((f32[128,17,1,128]{3,2,1,0:T(1,128)}), f32[128,17,1,128]{3,2,1,0:T(1,128)S(1)}, u32[]{:S(2)}, u32[]{:S(2)}) async-start(f32[128,17,1,128]{3,2,1,0:T(1,128)} %shard_map.163), calls=%async_computation | async-start | bytes 2228224 | tf_op jit(solution)/shard_map/all_to_all | solution.py:420
  50.8 19.0 %all-to-all-start.2 = ((f32[4,2,8,32,128]{4,3,2,1,0:T(8,128)}), f32[4,2,8,32,128]{4,3,2,1,0:T(8,128)S(1)}, u32[]{:S(2)}, u32[]{:S(2)}) async-start(f32[4,2,8,32,128]{4,3,2,1,0:T(8,128)} %shard_map.165), calls=%async_computation.2 | async-start | bytes 2097152 | tf_op jit(solution)/shard_map/all_to_all | solution.py:420
  67.0 35.9 %copy-start.2 = (bf16[128,1536]{1,0:T(8,128)(2,1)S(1)}, bf16[128,1536]{1,0:T(8,128)(2,1)}, u32[]{:S(2)}) copy-start(bf16[128,1536]{1,0:T(8,128)(2,1)} %constant.31.clone.refs_7_) | copy-start | bytes 1179652
  67.0 35.9 %copy-start.3 = (f32[4,2,64,128]{3,2,1,0:T(8,128)S(1)}, f32[4,2,64,128]{3,2,1,0:T(8,128)}, u32[]{:S(2)}) copy-start(f32[4,2,64,128]{3,2,1,0:T(8,128)} %constant.32.clone.refs_6_) | copy-start | bytes 786436
  69.8 37.8 %all-to-all-start.1 = ((f32[128,16,128]{2,1,0:T(8,128)}), f32[128,16,128]{2,1,0:T(8,128)}, u32[]{:S(2)}, u32[]{:S(2)}) async-start(f32[128,16,128]{2,1,0:T(8,128)} %shard_map.164), calls=%async_computation.1 | async-start | bytes 2097152 | tf_op jit(solution)/shard_map/all_to_all | solution.py:420
  77.9 19.3 %collective-permute-start = (f32[2,8,32,128]{3,2,1,0:T(8,128)S(1)}, f32[2,8,32,128]{3,2,1,0:T(8,128)S(1)}, u32[]{:S(2)}, u32[]{:S(2)}) collective-permute-start(f32[2,8,32,128]{3,2,1,0:T(8,128)S(1)} %get-tuple-element.28), channel_id=1, source_target_pairs={{0,32},{32,64},{64,96},{96,0},{1,33},{33,65},{65,97},{97,1},{2,34}... | collective-permute-start | bytes 786440 | tf_op jit(solution)/shard_map/ppermute | solution.py:472
  79.4 23.6 %collective-permute-start.1 = (f32[2,8,32,128]{3,2,1,0:T(8,128)S(1)}, f32[2,8,32,128]{3,2,1,0:T(8,128)S(1)}, u32[]{:S(2)}, u32[]{:S(2)}) collective-permute-start(f32[2,8,32,128]{3,2,1,0:T(8,128)S(1)} %get-tuple-element.29), channel_id=1, source_target_pairs={{0,64},{32,96},{64,0},{96,32},{1,65},{33,97},{65,1},{97,33},{2,66}... | collective-permute-start | bytes 786440 | tf_op jit(solution)/shard_map/ppermute | solution.py:472
  81.8 21.2 %collective-permute-start.2 = (f32[2,8,32,128]{3,2,1,0:T(8,128)S(1)}, f32[2,8,32,128]{3,2,1,0:T(8,128)S(1)}, u32[]{:S(2)}, u32[]{:S(2)}) collective-permute-start(f32[2,8,32,128]{3,2,1,0:T(8,128)S(1)} %get-tuple-element.30), channel_id=1, source_target_pairs={{0,96},{32,0},{64,32},{96,64},{1,97},{33,1},{65,33},{97,65},{2,98}... | collective-permute-start | bytes 786440 | tf_op jit(solution)/shard_map/ppermute | solution.py:472
  107.5 27.4 %all-to-all-start.3 = ((f32[128,16,128]{2,1,0:T(8,128)}), f32[128,16,128]{2,1,0:T(8,128)S(1)}, u32[]{:S(2)}, u32[]{:S(2)}) async-start(f32[128,16,128]{2,1,0:T(8,128)} %bitcast.2), calls=%async_computation.3 | async-start | bytes 2097152 | tf_op jit(solution)/shard_map/all_to_all | solution.py:420
  145.1 23.6 %copy-start = (f32[32,4096]{1,0:T(8,128)S(1)}, f32[32,4096]{1,0:T(8,128)}, u32[]{:S(2)}) copy-start(f32[32,4096]{1,0:T(8,128)} %refs_1_.6) | copy-start | bytes 1572868
  145.1 23.6 %copy-start.1 = (bf16[768,256]{1,0:T(8,128)(2,1)S(1)}, bf16[768,256]{1,0:T(8,128)(2,1)}, u32[]{:S(2)}) copy-start(bf16[768,256]{1,0:T(8,128)(2,1)} %constant.29.clone.refs_3_) | copy-start | bytes 1179652
  145.1 23.6 %copy-start.4 = (f32[2,32,128]{2,1,0:T(8,128)S(1)}, f32[2,32,128]{2,1,0:T(8,128)}, u32[]{:S(2)}) copy-start(f32[2,32,128]{2,1,0:T(8,128)} %constant.30.clone.refs_2_) | copy-start | bytes 98308

commit v2 on v1

--- a/solution.py
+++ b/solution.py
@@ -74,6 +74,7 @@
     out["tw_row"] = np.stack(wave(n(32), n(128), IMG))
     c, s = wave(n(64) + 32, n(128), 128)
     out["w_cols"] = spread_table(turned(c, s), LEFT[6], 1)
+    out["w_back"] = spread_table(turned(c[::-1], s[::-1]), LEFT[6], 1)
     out["tw_cols"] = np.stack([np.stack(wave(n(64), n(128) + G // n_base * me, G)) for me in range(n_base)])
     eye = np.eye(4)
     c, s = wave(n(128), n(32), IMG)
@@ -120,6 +121,10 @@
     even, odd = fft_list(xs[0::2]), fft_list(xs[1::2])
     low, high = [], []
     for k in range(n // 2):
+        if odd[k] is None:
+            low.append(even[k])
+            high.append(even[k])
+            continue
         (a, b), (c, d) = even[k], times(odd[k], k, n)
         low.append((a + c, b + d))
         high.append((a - c, b - d))
@@ -199,9 +204,9 @@
 SM = pltpu.SMEM
 
 
-def pack_kernel(owner, tile, residual, position, out, count):
+def first_kernel(owner, tile, residual, position, xi, amplitude, tw, w, out, count, mid):
     n_base, n_slab = 4, 32
-    out[...] = jnp.zeros_like(out)
+    out[:, 0:17] = jnp.zeros((out.shape[0], 17, 1, 128), f32)
 
     def clear(i, _):
         count[i] = 0
@@ -228,7 +233,8 @@
         out[to, 16] = jnp.where(lane == slot, (col + 1).astype(f32), out[to, 16])
         return 0
 
-    lax.fori_loop(0, owner.shape[0], step, 0)
+    lax.fori_loop(0, owner.shape[0], step, 0, unroll=4)
+    row_transform(xi, amplitude, tw, w, out, mid)
 
 
 def taps(d):
@@ -289,7 +295,7 @@
 
 
 def cols_kernel(*refs):
-    me, whole, parts, (tw, w, out, mid) = refs[0], refs[1], refs[2:6], refs[6:]
+    me, whole, parts, (tw, w, w_back, out, mid) = refs[0], refs[1], refs[2:6], refs[6:]
 
     def tile(b, ri, at):
         group = b // 16
@@ -302,46 +308,77 @@
         first = [(tile(b, 0, at), tile(b, 1, at)) for b in range(64)]
         for c, (re, im) in enumerate(fft_list(first)):
             cos, sin = tw[me[0], 0, c : c + 1, :], tw[me[0], 1, c : c + 1, :]
-            mid[c, at, 0:128] = re * cos - im * sin
-            mid[c, at, 128:256] = re * sin + im * cos
+            half, c = c // 32, c % 32
+            to = 32 * half + c if c <= 16 else 32 * (1 - half) + 48 - c
+            mid[to, at, 0:128] = re * cos - im * sin
+            mid[to, at, 128:256] = re * sin + im * cos
         return 0
 
     lax.fori_loop(0, 4, rows, 0)
     for pair in range(8):
         part = spread(mid[8 * pair : 8 * pair + 8].reshape(256, 256), RIGHT[6], 1)
-        res = mm(w[...], part, NT)
+        res = mm((w if pair % 4 < 2 else w_back)[...], part, NT)
+        if pair % 4 == 2:
+            own = mm(w[...], part[0:128], NT)
+            own = jnp.concatenate([jnp.where(low_lanes(), own, res[:, 0:128]), res[:, 128:256]], axis=1)
+            res = own
         for k in range(2):
             chunk = 2 * pair + k
             for ri in range(2):
                 out[:, chunk // 8, ri * 8 + chunk % 8, :] = res[64 * ri : 64 * ri + 64, 128 * k : 128 * k + 128]
 
 
-def row_kernel(xi, amplitude, tw, w, out, mid):
+def row_transform(xi, amplitude, tw, w, out, mid):
     def rows(i, _):
         at = pl.ds(pl.multiple_of(i * 8, 8), 8)
         first = [
             xi[at, 128 * b : 128 * b + 128] * amplitude[at, 128 * b : 128 * b + 128] for b in range(32)
         ]
-        half = rfft_list(first)
-        for c in range(32):
+        for c, (re, im) in enumerate(rfft_list(first)):
             cos, sin = tw[0, c : c + 1, :], tw[1, c : c + 1, :]
-            re, im = half[c] if c <= 16 else half[32 - c]
             if im is None:
                 mid[c, at, 0:128] = re * cos
                 mid[c, at, 128:256] = re * sin
             else:
-                im = im if c <= 16 else -im
                 mid[c, at, 0:128] = re * cos - im * sin
                 mid[c, at, 128:256] = re * sin + im * cos
         return 0
 
     lax.fori_loop(0, 4, rows, 0)
-    for pair in range(4):
+    for pair in range(2):
         part = spread(mid[8 * pair : 8 * pair + 8].reshape(256, 256), RIGHT[3], 1)
         res = mm(w[...], part, NT)
         for k in range(2):
             for ri in range(2):
-                out[:, ri * 8 + 2 * pair + k, :] = res[128 * ri : 128 * ri + 128, 128 * k : 128 * k + 128]
+                out[:, 17 + ri * 4 + 2 * pair + k, 0, :] = res[128 * ri : 128 * ri + 128, 128 * k : 128 * k + 128]
+    part = spread(mid[16:20].reshape(128, 256), RIGHT[3], 1)
+    res = mm(w[...], part, NT)
+    out[:, 25, 0, :] = beside(res[0:128], res[128:256])
+
+
+def low_lanes():
+    return lax.broadcasted_iota(jnp.int32, (128, 128), 1) < 32
+
+
+def beside(a, b):
+    lane = lax.broadcasted_iota(jnp.int32, (128, 128), 1)
+    return jnp.where(lane < 32, a, jnp.where(lane < 64, pltpu.roll(b, 32, 1), 0.0))
+
+
+def column_pairs(field, pair):
+    chunk = []
+    for k in range(2):
+        j = 2 * pair + k
+        re, im = field[:, 17 + j % 4, 0, :], field[:, 21 + j % 4, 0, :]
+        if j >= 4:
+            im = -im
+        if j == 4:
+            own = field[:, 25, 0, :]
+            re, im = jnp.where(low_lanes(), own, re), jnp.where(low_lanes(), pltpu.roll(own, 96, 1), im)
+        chunk.append((re, im))
+    return jnp.concatenate(
+        [jnp.concatenate([chunk[k][ri] for k in range(2)], axis=1) for ri in range(2)], axis=0
+    )
 
 
 def chunks(ref, pair):
@@ -365,12 +402,13 @@
 
 def sky_kernel(field, w, tw, r, out):
     for pair in range(4):
-        a = mm(w[...], spread(chunks(field, pair), RIGHT[3], 0))
+        a = mm(w[...], spread(column_pairs(field, pair), RIGHT[3], 0))
         turn = stacked([twist(re, im, tw) for re, im in zip(halves(a, 0), halves(a, 128))])
         out[pair] = jnp.exp(mm(spread(turn, LEFT[3], 1), r[...]))
 
 
 def image_kernel(sky, uv, w, tw_f, r_y, w_b, tw_b, r_b, out):
+    done = []
     for pair in range(4):
         a = mm(w_b[...], spread(chunks(uv, pair), RIGHT[6], 0))
         parts = [[], []]
@@ -381,26 +419,37 @@
         a = mm(spread(sky[pair] * back, LEFT[3], 1), r_y[...])
         turn = [twist(a[128 * k : 128 * k + 128, 0:128], a[128 * k : 128 * k + 128, 128:256], tw_f) for k in range(2)]
         turn = jnp.concatenate([jnp.concatenate([turn[k][ri] for k in range(2)], axis=1) for ri in range(2)], axis=0)
-        res = mm(w[...], spread(turn, RIGHT[3], 0))
-        for ri in range(2):
-            for k in range(2):
-                out[:, ri * 8 + 2 * pair + k, :] = res[128 * ri : 128 * ri + 128, 128 * k : 128 * k + 128]
+        done.append(mm(w[...], spread(turn, RIGHT[3], 0)))
+    for j in range(4):
+        at = slice(128 * (j % 2), 128 * (j % 2) + 128)
+        straight, mirrored = done[j // 2][:, at], done[2 + j // 2][:, at]
+        re, im = mirrored[0:128], mirrored[128:256]
+        if j == 0:
+            out[:, 8, 0, :] = beside(re, im)
+            re, im = jnp.where(low_lanes(), 0.0, re), jnp.where(low_lanes(), 0.0, im)
+        out[:, j, 0, :] = straight[0:128] + im
+        out[:, 4 + j, 0, :] = straight[128:256] + re
 
 
 def last_kernel(folded, amplitude, tw, w, out, mid):
-    for j in range(8):
-        z = jnp.concatenate([folded[:, j, :], folded[:, 8 + j, :]], axis=0)
+    def residue(c, v):
+        cos, sin = tw[0, c : c + 1, :], tw[1, c : c + 1, :]
+        re, im = v[:, 0:128], v[:, 128:256]
+        mid[c, :, 0:128] = re * cos - im * sin
+        mid[c, :, 128:256] = re * sin + im * cos
+
+    for j in range(4):
+        z = jnp.concatenate([folded[:, j, 0, :], folded[:, 4 + j, 0, :]], axis=0)
         v = mm(spread(z, LEFT[3], 0), w[...], TN)
         for k in range(4):
-            c = 4 * j + k
-            cos, sin = tw[0, c : c + 1, :], tw[1, c : c + 1, :]
-            re, im = v[32 * k : 32 * k + 32, 0:128], v[32 * k : 32 * k + 32, 128:256]
-            mid[c, :, 0:128] = re * cos - im * sin
-            mid[c, :, 128:256] = re * sin + im * cos
+            residue(4 * j + k, v[32 * k : 32 * k + 32])
+    own = folded[:, 8, 0, :]
+    z = jnp.concatenate([own, pltpu.roll(own, 96, 1)], axis=0)
+    residue(16, mm(spread(z, LEFT[3], 0), w[...], TN)[0:32])
 
     def rows(i, _):
         at = pl.ds(pl.multiple_of(i * 8, 8), 8)
-        first = [(mid[c, at, 0:128], mid[c, at, 128:256]) for c in range(32)]
+        first = [(mid[c, at, 0:128], mid[c, at, 128:256]) for c in range(17)] + [None] * 15
         for b, (re, im) in enumerate(fft_list(first)):
             to = slice(128 * b, 128 * b + 128)
             out[at, to] = amplitude[at, to] * (re + im) * (1.0 / IMG)
@@ -423,35 +472,23 @@
     blocks = residual.shape[0]
     me = lax.axis_index("base").astype(jnp.int32).reshape(1)
     packed = call(
-        pack_kernel,
-        (devices, 17, 1, 128),
-        [SM, SM, VM, VM],
-        [SM((devices,), jnp.int32)],
+        first_kernel,
+        (devices, 26, 1, 128),
+        [SM, SM] + [VM] * 6,
+        [SM((devices,), jnp.int32), VM((20, 32, 256), f32)],
         2e9,
         [
             (0, SM((blocks,), jnp.int32)),
             (1, SM((blocks,), jnp.int32)),
             (2, VM(residual.shape, f32)),
             (3, VM(position.shape, f32)),
+            (4, VM((rows, width), f32)),
+            (5, VM((rows, width), f32)),
+            (6, VM((2, 32, 128), f32)),
+            (7, VM((256, 768), bf16)),
         ],
-    )(owner[:, 0], tile_local, residual, position)
+    )(owner[:, 0], tile_local, residual, position, xi, amplitude, t["tw_row"], t["w128"])
     data = exchange(packed, everywhere)
-    half = call(
-        row_kernel,
-        (devices, 16, 128),
-        [VM] * 4,
-        [VM((32, 32, 256), f32)],
-        2e9,
-        [
-            (0, VM((rows, width), f32)),
-            (1, VM((rows, width), f32)),
-            (2, VM((2, 32, 128), f32)),
-            (3, VM((256, 768), bf16)),
-        ],
-        True,
-    )(xi, amplitude, t["tw_row"], t["w128"])
-
-    data, half = lax.optimization_barrier((data, half))
     tags = data[:, 16, 0, 0:4].reshape(4 * devices).astype(jnp.int32)
     spare = [VM((4, TILE, TILE), f32), SM((4 * devices + GROUP,), jnp.int32)]
     shape = (2, 8, 32, 128)
@@ -467,36 +504,37 @@
         [*spare, VM((n_base, *shape), f32)],
         2e10,
     )(me, tags, data)
-    parts, half = lax.optimization_barrier((parts, half))
+    parts, field = lax.optimization_barrier((parts, data))
     parts = [parts[0]] + [
         lax.ppermute(parts[k], "base", [(i, (i + k) % n_base) for i in range(n_base)]) for k in range(1, n_base)
     ]
-    half = exchange(half, everywhere)
-    cols = call(
-        cols_kernel,
-        (devices // 2, 2, 16, 128),
-        [SM] + [VM] * 7,
-        [VM((64, 32, 256), f32)],
-        4e9,
-    )(me, whole, *parts, t["tw_cols"], t["w_cols"])
-    cols = exchange(cols.reshape(devices, 16, 128), everywhere)
     sky = call(
         sky_kernel,
         (4, 256, 128),
         [VM] * 4,
         (),
         4e9,
+        [(1, VM((256, 768), bf16)), (2, VM((2, 128, 128), f32)), (3, VM((768, 128), bf16))],
+        True,
+    )(field, t["w128"], t["tw_f"], t["r_f"])
+    parts[0], sky = lax.optimization_barrier((parts[0], sky))
+    cols = call(
+        cols_kernel,
+        (devices // 2, 2, 16, 128),
+        [SM] + [VM] * 8,
+        [VM((64, 32, 256), f32)],
+        4e9,
         [
-            (0, VM((devices, 16, 128), f32)),
-            (1, VM((256, 768), bf16)),
-            (2, VM((2, 128, 128), f32)),
-            (3, VM((768, 128), bf16)),
+            (1, VM((n_base, *shape), f32)),
+            (6, VM((n_base, 2, 64, 128), f32)),
+            (7, VM((128, 1536), bf16)),
+            (8, VM((128, 1536), bf16)),
         ],
-        True,
-    )(half, t["w128"], t["tw_f"], t["r_f"])
+    )(me, whole, *parts, t["tw_cols"], t["w_cols"], t["w_back"])
+    cols = exchange(cols.reshape(devices, 16, 128), everywhere)
     fold = call(
         image_kernel,
-        (devices, 16, 128),
+        (devices, 9, 1, 128),
         [VM] * 8,
         (),
         8e9,

time: 169 us -> 150 us (0.89); the launches traced: 171 us -> 150 us
  blocking collectives: 23.6 us -> 49 us
  waiting for transfers between devices: 53.9 us -> 29.4 us
  Pallas kernels: 56.6 us -> 44.5 us
  starting transfers between devices: 36.5 us -> 26.8 us
    all_to_all x1 -> x2, blocking collectives: 23.6 us -> 49 us  [exchange(): return lax.all_to_all(a, axis, split_axis=0, concat_axis=0, tiled=True)]
    ppermute x3, waiting for transfers between devices: 20 us -> 3.29 us  [per_device(): lax.ppermute(parts[k], 'base', [(i, (i + k) % n_base) for i in range(n_ba...]
    all_to_all x4 -> x2, starting transfers between devices: 31.4 us -> 18.3 us  [exchange(): return lax.all_to_all(a, axis, split_axis=0, concat_axis=0, tiled=True)]
    pallas_call x8 -> x7, Pallas kernels: 56.6 us -> 44.5 us  [placed(): results = got(*arrays)]
    all_to_all x4 -> x2, waiting for transfers between devices: 33.9 us -> 26.1 us  [exchange(): return lax.all_to_all(a, axis, split_axis=0, concat_axis=0, tiled=True)]
    ppermute x3, starting transfers between devices: 5.03 us -> 8.53 us  [per_device(): lax.ppermute(parts[k], 'base', [(i, (i + k) % n_base) for i in range(n_ba...]
  transfers between devices with their start and end apart: 7 -> 5, of which waited for: 5 -> 3; matrix products, arithmetic and copies ran while one was open for 0% -> 0% of each run, Pallas kernels for 15% -> 9%
where the time goes in v2:
time: 150 us
  blocking collectives  49 us (33%)
  Pallas kernels  44.5 us (30%)
  waiting for transfers between devices  29.4 us (20%)
  starting transfers between devices  26.8 us (18%)
    all_to_all x2, blocking collectives, exchange(): return lax.all_to_all(a, axis, split_axis=0, concat_axis=0, tiled=True)  49 us
    pallas_call x7, Pallas kernels, placed(): results = got(*arrays)  44.5 us
    all_to_all x2, waiting for transfers between devices, exchange(): return lax.all_to_all(a, axis, split_axis=0, concat_axis=0, tiled=True)  26.1 us
    all_to_all x2, starting transfers between devices, exchange(): return lax.all_to_all(a, axis, split_axis=0, concat_axis=0, tiled=True)  18.3 us
    ppermute x3, starting transfers between devices, per_device(): lax.ppermute(parts[k], 'base', [(i, (i + k) % n_base) for i in range(n_ba...  8.53 us
    ppermute x3, waiting for transfers between devices, per_device(): lax.ppermute(parts[k], 'base', [(i, (i + k) % n_base) for i in range(n_ba...  3.29 us
  transfers between devices with their start and end apart: 5, of which 3 were waited for; matrix products, arithmetic and copies ran while one was open for 0% of the time, Pallas kernels for 9%

profile of v2, /device:TPU:1, one launch (start us, length us, event | category | flops | bytes accessed | tf_op | source)
XLA Modules:
  0.0 150.1 jit_solution(7695838296471440660)
XLA Ops:
  0.0 5.8 %shard_map.172 = f32[128,26,1,128]{3,2,1,0:T(1,128)} custom-call(s32[128]{0:T(128)} %bitcast.4, s32[128]{0:T(128)} %refs_1_.3, f32[128,2,128]{2,1,0:T(2,128)} %refs_2_.4, f32[128,2,128]{2,1,0:T(2,128)} %refs_3_.4, f32[32,4096]{1,0:T(8,128)} %refs_4_.2, f32[32,4096]{1,0:T(8,128)} %refs_1_.4, f32[2,32,128]{2,1,0:T(8,128)} %constant.32.clone.refs_6_.refs_2_, ...), custom_call_target="tpu_custom_call" | custom-call | flops 2000000000 | bytes 3407872 | tf_op jit(solution)/shard_map/pallas_call | solution.py:197
  5.8 11.5 %all-to-all-start = ((f32[128,26,1,128]{3,2,1,0:T(1,128)}), f32[128,26,1,128]{3,2,1,0:T(1,128)S(1)}, u32[]{:S(2)}, u32[]{:S(2)}) async-start(f32[128,26,1,128]{3,2,1,0:T(1,128)} %shard_map.172), calls=%async_computation | async-start | bytes 3407872 | tf_op jit(solution)/shard_map/all_to_all | solution.py:469
  17.3 26.1 %all-to-all-done.refs_1_.refs_2_.refs_0_ = f32[128,26,1,128]{3,2,1,0:T(1,128)S(1)} async-done(((f32[128,26,1,128]{3,2,1,0:T(1,128)}), f32[128,26,1,128]{3,2,1,0:T(1,128)S(1)}, u32[]{:S(2)}, u32[]{:S(2)}) %all-to-all-start) | async-done | bytes 1703968 | tf_op jit(solution)/shard_map/all_to_all | solution.py:469
  43.4 0.2 fusion
  43.6 0.1 convert_element_type.6.refs_0_.refs_1_
  43.7 8.5 %shard_map.173 = f32[4,2,8,32,128]{4,3,2,1,0:T(8,128)} custom-call(s32[512]{0:T(512)S(1)} %convert_element_type.6.refs_0_.refs_1_, f32[128,26,1,128]{3,2,1,0:T(1,128)S(1)} %all-to-all-done.refs_1_.refs_2_.refs_0_), custom_call_target="tpu_custom_call" | custom-call | flops 20000000000 | bytes 2097152 | tf_op jit(solution)/shard_map/pallas_call | solution.py:197
  52.2 6.8 %all-to-all-start.1 = ((f32[4,2,8,32,128]{4,3,2,1,0:T(8,128)}), f32[4,2,8,32,128]{4,3,2,1,0:T(8,128)}, u32[]{:S(2)}, u32[]{:S(2)}) async-start(f32[4,2,8,32,128]{4,3,2,1,0:T(8,128)} %shard_map.173), calls=%async_computation.1 | async-start | bytes 2097152 | tf_op jit(solution)/shard_map/all_to_all | solution.py:469
  59.0 9.3 %shard_map.174 = (f32[2,8,32,128]{3,2,1,0:T(8,128)S(1)}, f32[2,8,32,128]{3,2,1,0:T(8,128)S(1)}, f32[2,8,32,128]{3,2,1,0:T(8,128)S(1)}, f32[2,8,32,128]{3,2,1,0:T(8,128)S(1)}) custom-call(s32[1]{0:T(128)} %bitcast.refs_0_, s32[512]{0:T(512)S(1)} %convert_element_type.6.refs_0_.refs_1_, f32[128,26,1,128]{3,2,1,0:T(1,128)S(1)} %all-to-all-done.refs_1_.refs_2_.refs_0_), custom_call_target="tpu_custom_call" | custom-call | flops 20000000000 | bytes 2097152 | tf_op jit(solution)/shard_map/pallas_call | solution.py:197
  68.2 0.1 collective-permute-start
  68.3 6.5 %collective-permute-start.1 = (f32[2,8,32,128]{3,2,1,0:T(8,128)S(1)}, f32[2,8,32,128]{3,2,1,0:T(8,128)S(1)}, u32[]{:S(2)}, u32[]{:S(2)}) collective-permute-start(f32[2,8,32,128]{3,2,1,0:T(8,128)S(1)} %get-tuple-element.29), channel_id=1, source_target_pairs={{0,64},{32,96},{64,0},{96,32},{1,65},{33,97},{65,1},{97,33},{2,66}... | collective-permute-start | bytes 786440 | tf_op jit(solution)/shard_map/ppermute | solution.py:509
  74.8 2.0 %collective-permute-start.2 = (f32[2,8,32,128]{3,2,1,0:T(8,128)S(1)}, f32[2,8,32,128]{3,2,1,0:T(8,128)S(1)}, u32[]{:S(2)}, u32[]{:S(2)}) collective-permute-start(f32[2,8,32,128]{3,2,1,0:T(8,128)S(1)} %get-tuple-element.30), channel_id=1, source_target_pairs={{0,96},{32,0},{64,32},{96,64},{1,97},{33,1},{65,33},{97,65},{2,98}... | collective-permute-start | bytes 786440 | tf_op jit(solution)/shard_map/ppermute | solution.py:509
  76.8 3.7 %shard_map.175.refs_0_ = f32[4,256,128]{2,1,0:T(8,128)} custom-call(f32[128,26,1,128]{3,2,1,0:T(1,128)S(1)} %all-to-all-done.refs_1_.refs_2_.refs_0_, bf16[256,768]{1,0:T(8,128)(2,1)} %constant.30.clone.refs_7_.refs_1_.refs_2_, f32[2,128,128]{2,1,0:T(8,128)} %constant.36.clone.refs_2_.refs_3_, bf16[768,128]{1,0:T(8,128)(2,1)} %constant.37.clone.refs_3_), custom_call_target="tpu_custom_call" | custom-call | flops 4000000000 | bytes 1048576 | tf_op jit(solution)/shard_map/pallas_call | solution.py:197
  80.4 1.4 collective-permute-done.refs_3_
  81.9 1.9 %collective-permute-done.1.refs_4_ = f32[2,8,32,128]{3,2,1,0:T(8,128)S(1)} collective-permute-done((f32[2,8,32,128]{3,2,1,0:T(8,128)S(1)}, f32[2,8,32,128]{3,2,1,0:T(8,128)S(1)}, u32[]{:S(2)}, u32[]{:S(2)}) %collective-permute-start.1) | collective-permute-done | bytes 262176 | tf_op jit(solution)/shard_map/ppermute | solution.py:509
  83.7 0.0 collective-permute-done.2.refs_5_
  83.7 0.0 all-to-all-done.1.refs_1_
  83.7 5.3 %shard_map.176 = f32[64,2,16,128]{3,2,1,0:T(8,128)S(1)} custom-call(s32[1]{0:T(128)} %bitcast.refs_0_, f32[4,2,8,32,128]{4,3,2,1,0:T(8,128)} %all-to-all-done.1.refs_1_, f32[2,8,32,128]{3,2,1,0:T(8,128)S(1)} %get-tuple-element.27.refs_2_, f32[2,8,32,128]{3,2,1,0:T(8,128)S(1)} %collective-permute-done.refs_3_, ...), custom_call_target="tpu_custom_call" | custom-call | flops 4000000000 | bytes 2097152 | tf_op jit(solution)/shard_map/pallas_call | solution.py:197
  89.1 30.3 %all_to_all.20.refs_1_ = f32[128,16,128]{2,1,0:T(8,128)S(1)} all-to-all(f32[128,16,128]{2,1,0:T(8,128)S(1)} %bitcast.3), channel_id=1, replica_groups=mesh['base'=4,'slab'=32] {'base','slab'}, dimensions={0} | all-to-all | bytes 2097152 | tf_op jit(solution)/shard_map/all_to_all | solution.py:469
  119.3 10.2 %shard_map.177 = f32[128,9,1,128]{3,2,1,0:T(1,128)S(1)} custom-call(f32[4,256,128]{2,1,0:T(8,128)} %shard_map.175.refs_0_, f32[128,16,128]{2,1,0:T(8,128)S(1)} %all_to_all.20.refs_1_, bf16[256,768]{1,0:T(8,128)(2,1)} %constant.30.clone.refs_7_.refs_1_.refs_2_, f32[2,128,128]{2,1,0:T(8,128)} %constant.36.clone.refs_2_.refs_3_, ...), custom_call_target="tpu_custom_call" | custom-call | flops 8000000000 | bytes 1179648 | tf_op jit(solution)/shard_map/pallas_call | solution.py:197
  129.6 18.7 %all_to_all.21.refs_0_ = f32[128,9,1,128]{3,2,1,0:T(1,128)S(1)} all-to-all(f32[128,9,1,128]{3,2,1,0:T(1,128)S(1)} %shard_map.177), channel_id=1, replica_groups=mesh['base'=4,'slab'=32] {'base','slab'}, dimensions={0} | all-to-all | bytes 1179648 | tf_op jit(solution)/shard_map/all_to_all | solution.py:469
  148.3 0.0 copy-done
  148.3 0.0 copy-done.1
  148.3 0.0 copy-done.2
  148.3 1.8 %shard_map.178 = f32[32,4096]{1,0:T(8,128)} custom-call(f32[128,9,1,128]{3,2,1,0:T(1,128)S(1)} %all_to_all.21.refs_0_, f32[32,4096]{1,0:T(8,128)S(1)} %copy-done, f32[2,32,128]{2,1,0:T(8,128)S(1)} %copy-done.2, bf16[768,256]{1,0:T(8,128)(2,1)S(1)} %copy-done.1), custom_call_target="tpu_custom_call" | custom-call | flops 3000000000 | bytes 1048576 | tf_op jit(solution)/shard_map/pallas_call | solution.py:197
  (3 shorter events, 0.0 us)
Async XLA Ops:
  5.8 37.6 %all-to-all-start = ((f32[128,26,1,128]{3,2,1,0:T(1,128)}), f32[128,26,1,128]{3,2,1,0:T(1,128)S(1)}, u32[]{:S(2)}, u32[]{:S(2)}) async-start(f32[128,26,1,128]{3,2,1,0:T(1,128)} %shard_map.172), calls=%async_computation | async-start | bytes 3407872 | tf_op jit(solution)/shard_map/all_to_all | solution.py:469
  52.2 31.6 %all-to-all-start.1 = ((f32[4,2,8,32,128]{4,3,2,1,0:T(8,128)}), f32[4,2,8,32,128]{4,3,2,1,0:T(8,128)}, u32[]{:S(2)}, u32[]{:S(2)}) async-start(f32[4,2,8,32,128]{4,3,2,1,0:T(8,128)} %shard_map.173), calls=%async_computation.1 | async-start | bytes 2097152 | tf_op jit(solution)/shard_map/all_to_all | solution.py:469
  68.2 13.6 %collective-permute-start = (f32[2,8,32,128]{3,2,1,0:T(8,128)S(1)}, f32[2,8,32,128]{3,2,1,0:T(8,128)S(1)}, u32[]{:S(2)}, u32[]{:S(2)}) collective-permute-start(f32[2,8,32,128]{3,2,1,0:T(8,128)S(1)} %get-tuple-element.28), channel_id=1, source_target_pairs={{0,32},{32,64},{64,96},{96,0},{1,33},{33,65},{65,97},{97,1},{2,34}... | collective-permute-start | bytes 786440 | tf_op jit(solution)/shard_map/ppermute | solution.py:509
  68.3 15.4 %collective-permute-start.1 = (f32[2,8,32,128]{3,2,1,0:T(8,128)S(1)}, f32[2,8,32,128]{3,2,1,0:T(8,128)S(1)}, u32[]{:S(2)}, u32[]{:S(2)}) collective-permute-start(f32[2,8,32,128]{3,2,1,0:T(8,128)S(1)} %get-tuple-element.29), channel_id=1, source_target_pairs={{0,64},{32,96},{64,0},{96,32},{1,65},{33,97},{65,1},{97,33},{2,66}... | collective-permute-start | bytes 786440 | tf_op jit(solution)/shard_map/ppermute | solution.py:509
  74.8 8.9 %collective-permute-start.2 = (f32[2,8,32,128]{3,2,1,0:T(8,128)S(1)}, f32[2,8,32,128]{3,2,1,0:T(8,128)S(1)}, u32[]{:S(2)}, u32[]{:S(2)}) collective-permute-start(f32[2,8,32,128]{3,2,1,0:T(8,128)S(1)} %get-tuple-element.30), channel_id=1, source_target_pairs={{0,96},{32,0},{64,32},{96,64},{1,97},{33,1},{65,33},{97,65},{2,98}... | collective-permute-start | bytes 786440 | tf_op jit(solution)/shard_map/ppermute | solution.py:509
  119.3 28.9 %copy-start = (f32[32,4096]{1,0:T(8,128)S(1)}, f32[32,4096]{1,0:T(8,128)}, u32[]{:S(2)}) copy-start(f32[32,4096]{1,0:T(8,128)} %refs_1_.4) | copy-start | bytes 1572868
  119.3 28.9 %copy-start.1 = (bf16[768,256]{1,0:T(8,128)(2,1)S(1)}, bf16[768,256]{1,0:T(8,128)(2,1)}, u32[]{:S(2)}) copy-start(bf16[768,256]{1,0:T(8,128)(2,1)} %constant.31.clone.refs_3_) | copy-start | bytes 1179652
  119.3 28.9 %copy-start.2 = (f32[2,32,128]{2,1,0:T(8,128)S(1)}, f32[2,32,128]{2,1,0:T(8,128)}, u32[]{:S(2)}) copy-start(f32[2,32,128]{2,1,0:T(8,128)} %constant.32.clone.refs_6_.refs_2_) | copy-start | bytes 98308

commit v3 on v2

--- a/solution.py
+++ b/solution.py
@@ -147,6 +147,20 @@
     return out
 
 
+class Late:
+    def __init__(self, ref, copy):
+        self.ref, self.copy, self.shape = ref, copy, ref.shape
+
+    def ready(self):
+        if self.copy is not None:
+            self.copy.wait()
+            self.copy = None
+        return self.ref
+
+    def __getitem__(self, at):
+        return self.ready()[at]
+
+
 def call(body, out_shapes, in_specs, scratch=(), flops=0, far=(), far_out=False):
     outs = [out_shapes] if isinstance(out_shapes[0], int) else list(out_shapes)
     count, own, made = len(in_specs), len(scratch), len(outs)
@@ -161,11 +175,8 @@
         copies = []
         for k, (i, _) in enumerate(far):
             copies.append(pltpu.make_async_copy(ins[i], spare[k], spare[-1].at[k]))
-            ins[i] = spare[k]
-        for c in copies:
-            c.start()
-        for c in copies:
-            c.wait()
+            copies[-1].start()
+            ins[i] = Late(spare[k], copies[-1])
         if not far_out:
             body(*ins, *results, *rest)
             return
@@ -206,13 +217,14 @@
 
 def first_kernel(owner, tile, residual, position, xi, amplitude, tw, w, out, count, mid):
     n_base, n_slab = 4, 32
-    out[:, 0:17] = jnp.zeros((out.shape[0], 17, 1, 128), f32)
+    out[:, 16] = jnp.zeros((out.shape[0], 1, 128), f32)
 
     def clear(i, _):
         count[i] = 0
         return 0
 
     lax.fori_loop(0, count.shape[0], clear, 0, unroll=8)
+    owner, tile, residual, position = (a.ready() for a in (owner, tile, residual, position))
     lane = lax.broadcasted_iota(jnp.int32, (1, 128), 1)
 
     def step(i, _):
@@ -234,7 +246,7 @@
         return 0
 
     lax.fori_loop(0, owner.shape[0], step, 0, unroll=4)
-    row_transform(xi, amplitude, tw, w, out, mid)
+    row_transform(*(a.ready() for a in (xi, amplitude, tw, w)), out, mid)
 
 
 def taps(d):
@@ -267,7 +279,7 @@
 
     n = lax.fori_loop(0, slots, scan, jnp.int32(0), unroll=8)
     for extra in range(GROUP):
-        order[n + extra] = 0
+        order[n + extra] = order[jnp.maximum(n - 1, 0)]
 
     def down(row):
         return jnp.transpose(jnp.broadcast_to(row, (TILE, TILE)))
@@ -295,7 +307,8 @@
 
 
 def cols_kernel(*refs):
-    me, whole, parts, (tw, w, w_back, out, mid) = refs[0], refs[1], refs[2:6], refs[6:]
+    me, whole, parts, (tw, w, w_back, out, mid) = refs[0], refs[1].ready(), refs[2:6], refs[6:]
+    tw = tw.ready()
 
     def tile(b, ri, at):
         group = b // 16
@@ -540,11 +553,7 @@
         8e9,
         [
             (0, VM((4, 256, 128), f32)),
-            (2, VM((256, 768), bf16)),
-            (3, VM((2, 128, 128), f32)),
-            (4, VM((384, 256), bf16)),
             (5, VM((512, 1536), bf16)),
-            (6, VM((2, 2, 128, 128), f32)),
             (7, VM((3072, 128), bf16)),
         ],
     )(sky, cols, t["w128"], t["tw_f"], t["r_y"], t["w_b"], t["tw_b"], t["r_b"])

time: 150 us -> 152 us (1.013); the launches traced: 150 us -> 154 us
  blocking collectives: 49 us -> 55.8 us
  starting transfers between devices: 26.8 us -> 20.8 us
  waiting for transfers between devices: 29.4 us -> 33.5 us
    all_to_all x2, blocking collectives: 49 us -> 55.8 us  [exchange(): return lax.all_to_all(a, axis, split_axis=0, concat_axis=0, tiled=True)]
    ppermute x3, waiting for transfers between devices: 3.29 us -> 7.34 us  [per_device(): lax.ppermute(parts[k], 'base', [(i, (i + k) % n_base) for i in range(n_ba...]
    ppermute x3, starting transfers between devices: 8.53 us -> 5.05 us  [per_device(): lax.ppermute(parts[k], 'base', [(i, (i + k) % n_base) for i in range(n_ba...]
    all_to_all x2, starting transfers between devices: 18.3 us -> 15.7 us  [exchange(): return lax.all_to_all(a, axis, split_axis=0, concat_axis=0, tiled=True)]
  transfers between devices with their start and end apart: 5 -> 5, of which waited for: 3 -> 3; matrix products, arithmetic and copies ran while one was open for 0% -> 0% of each run, Pallas kernels for 9% -> 8%
where the time goes in v3:
time: 152 us; the launch traced here: 154 us
  blocking collectives  55.8 us (37%)
  Pallas kernels  43.2 us (28%)
  waiting for transfers between devices  33.5 us (22%)
  starting transfers between devices  20.8 us (14%)
    all_to_all x2, blocking collectives, exchange(): return lax.all_to_all(a, axis, split_axis=0, concat_axis=0, tiled=True)  55.8 us
    pallas_call x7, Pallas kernels, placed(): results = got(*arrays)  43.2 us
    all_to_all x2, waiting for transfers between devices, exchange(): return lax.all_to_all(a, axis, split_axis=0, concat_axis=0, tiled=True)  26.1 us
    all_to_all x2, starting transfers between devices, exchange(): return lax.all_to_all(a, axis, split_axis=0, concat_axis=0, tiled=True)  15.7 us
    ppermute x3, waiting for transfers between devices, per_device(): lax.ppermute(parts[k], 'base', [(i, (i + k) % n_base) for i in range(n_ba...  7.34 us
    ppermute x3, starting transfers between devices, per_device(): lax.ppermute(parts[k], 'base', [(i, (i + k) % n_base) for i in range(n_ba...  5.05 us
  transfers between devices with their start and end apart: 5, of which 3 were waited for; matrix products, arithmetic and copies ran while one was open for 0% of the time, Pallas kernels for 8%

profile of v3, /device:TPU:1, one launch (start us, length us, event | category | flops | bytes accessed | tf_op | source)
XLA Modules:
  0.0 153.8 jit_solution(1601488311415949876)
XLA Ops:
  0.0 4.5 %shard_map.172 = f32[128,26,1,128]{3,2,1,0:T(1,128)} custom-call(s32[128]{0:T(128)} %bitcast.4, s32[128]{0:T(128)} %refs_1_.3, f32[128,2,128]{2,1,0:T(2,128)} %refs_2_.4, f32[128,2,128]{2,1,0:T(2,128)} %refs_3_.4, f32[32,4096]{1,0:T(8,128)} %refs_4_.2, f32[32,4096]{1,0:T(8,128)} %refs_1_.4, f32[2,32,128]{2,1,0:T(8,128)} %constant.32.clone.refs_6_.refs_2_, ...), custom_call_target="tpu_custom_call" | custom-call | flops 2000000000 | bytes 3407872 | tf_op jit(solution)/shard_map/pallas_call | solution.py:208
  4.5 11.5 %all-to-all-start = ((f32[128,26,1,128]{3,2,1,0:T(1,128)}), f32[128,26,1,128]{3,2,1,0:T(1,128)S(1)}, u32[]{:S(2)}, u32[]{:S(2)}) async-start(f32[128,26,1,128]{3,2,1,0:T(1,128)} %shard_map.172), calls=%async_computation | async-start | bytes 3407872 | tf_op jit(solution)/shard_map/all_to_all | solution.py:482
  16.0 26.1 %all-to-all-done.refs_1_.refs_2_.refs_0_ = f32[128,26,1,128]{3,2,1,0:T(1,128)S(1)} async-done(((f32[128,26,1,128]{3,2,1,0:T(1,128)}), f32[128,26,1,128]{3,2,1,0:T(1,128)S(1)}, u32[]{:S(2)}, u32[]{:S(2)}) %all-to-all-start) | async-done | bytes 1703968 | tf_op jit(solution)/shard_map/all_to_all | solution.py:482
  42.2 0.2 fusion
  42.4 0.1 convert_element_type.6.refs_0_.refs_1_
  42.5 9.3 %shard_map.173 = f32[4,2,8,32,128]{4,3,2,1,0:T(8,128)} custom-call(s32[512]{0:T(512)S(1)} %convert_element_type.6.refs_0_.refs_1_, f32[128,26,1,128]{3,2,1,0:T(1,128)S(1)} %all-to-all-done.refs_1_.refs_2_.refs_0_), custom_call_target="tpu_custom_call" | custom-call | flops 20000000000 | bytes 2097152 | tf_op jit(solution)/shard_map/pallas_call | solution.py:208
  51.7 4.2 %all-to-all-start.1 = ((f32[4,2,8,32,128]{4,3,2,1,0:T(8,128)}), f32[4,2,8,32,128]{4,3,2,1,0:T(8,128)}, u32[]{:S(2)}, u32[]{:S(2)}) async-start(f32[4,2,8,32,128]{4,3,2,1,0:T(8,128)} %shard_map.173), calls=%async_computation.1 | async-start | bytes 2097152 | tf_op jit(solution)/shard_map/all_to_all | solution.py:482
  56.0 8.4 %shard_map.174 = (f32[2,8,32,128]{3,2,1,0:T(8,128)S(1)}, f32[2,8,32,128]{3,2,1,0:T(8,128)S(1)}, f32[2,8,32,128]{3,2,1,0:T(8,128)S(1)}, f32[2,8,32,128]{3,2,1,0:T(8,128)S(1)}) custom-call(s32[1]{0:T(128)} %bitcast.refs_0_, s32[512]{0:T(512)S(1)} %convert_element_type.6.refs_0_.refs_1_, f32[128,26,1,128]{3,2,1,0:T(1,128)S(1)} %all-to-all-done.refs_1_.refs_2_.refs_0_), custom_call_target="tpu_custom_call" | custom-call | flops 20000000000 | bytes 2097152 | tf_op jit(solution)/shard_map/pallas_call | solution.py:208
  64.4 0.6 collective-permute-start
  65.0 3.3 %collective-permute-start.1 = (f32[2,8,32,128]{3,2,1,0:T(8,128)S(1)}, f32[2,8,32,128]{3,2,1,0:T(8,128)S(1)}, u32[]{:S(2)}, u32[]{:S(2)}) collective-permute-start(f32[2,8,32,128]{3,2,1,0:T(8,128)S(1)} %get-tuple-element.29), channel_id=1, source_target_pairs={{0,64},{32,96},{64,0},{96,32},{1,65},{33,97},{65,1},{97,33},{2,66}... | collective-permute-start | bytes 786440 | tf_op jit(solution)/shard_map/ppermute | solution.py:522
  68.3 1.2 collective-permute-start.2
  69.4 3.7 %shard_map.175.refs_0_ = f32[4,256,128]{2,1,0:T(8,128)} custom-call(f32[128,26,1,128]{3,2,1,0:T(1,128)S(1)} %all-to-all-done.refs_1_.refs_2_.refs_0_, bf16[256,768]{1,0:T(8,128)(2,1)} %constant.30.clone.refs_7_.refs_1_.refs_2_, f32[2,128,128]{2,1,0:T(8,128)} %constant.36.clone.refs_2_.refs_3_, bf16[768,128]{1,0:T(8,128)(2,1)} %constant.37.clone.refs_3_), custom_call_target="tpu_custom_call" | custom-call | flops 4000000000 | bytes 1048576 | tf_op jit(solution)/shard_map/pallas_call | solution.py:208
  73.1 3.0 %collective-permute-done.refs_3_ = f32[2,8,32,128]{3,2,1,0:T(8,128)S(1)} collective-permute-done((f32[2,8,32,128]{3,2,1,0:T(8,128)S(1)}, f32[2,8,32,128]{3,2,1,0:T(8,128)S(1)}, u32[]{:S(2)}, u32[]{:S(2)}) %collective-permute-start) | collective-permute-done | bytes 262176 | tf_op jit(solution)/shard_map/ppermute | solution.py:522
  76.2 4.3 %collective-permute-done.1.refs_4_ = f32[2,8,32,128]{3,2,1,0:T(8,128)S(1)} collective-permute-done((f32[2,8,32,128]{3,2,1,0:T(8,128)S(1)}, f32[2,8,32,128]{3,2,1,0:T(8,128)S(1)}, u32[]{:S(2)}, u32[]{:S(2)}) %collective-permute-start.1) | collective-permute-done | bytes 262176 | tf_op jit(solution)/shard_map/ppermute | solution.py:522
  80.5 5.6 %shard_map.176 = f32[64,2,16,128]{3,2,1,0:T(8,128)S(1)} custom-call(s32[1]{0:T(128)} %bitcast.refs_0_, f32[4,2,8,32,128]{4,3,2,1,0:T(8,128)} %all-to-all-done.1.refs_1_, f32[2,8,32,128]{3,2,1,0:T(8,128)S(1)} %get-tuple-element.27.refs_2_, f32[2,8,32,128]{3,2,1,0:T(8,128)S(1)} %collective-permute-done.refs_3_, ...), custom_call_target="tpu_custom_call" | custom-call | flops 4000000000 | bytes 2097152 | tf_op jit(solution)/shard_map/pallas_call | solution.py:208
  86.1 0.0 copy-start.3
  86.1 0.0 copy-start.4
  86.1 0.0 copy-start.5
  86.1 37.2 %all_to_all.20.refs_1_ = f32[128,16,128]{2,1,0:T(8,128)S(1)} all-to-all(f32[128,16,128]{2,1,0:T(8,128)S(1)} %bitcast.3), channel_id=1, replica_groups=mesh['base'=4,'slab'=32] {'base','slab'}, dimensions={0} | all-to-all | bytes 2097152 | tf_op jit(solution)/shard_map/all_to_all | solution.py:482
  123.3 0.0 copy-start.2
  123.3 0.0 copy-start.6
  123.3 9.9 %shard_map.177 = f32[128,9,1,128]{3,2,1,0:T(1,128)S(1)} custom-call(f32[4,256,128]{2,1,0:T(8,128)} %shard_map.175.refs_0_, f32[128,16,128]{2,1,0:T(8,128)S(1)} %all_to_all.20.refs_1_, bf16[256,768]{1,0:T(8,128)(2,1)S(1)} %copy-done.1, f32[2,128,128]{2,1,0:T(8,128)S(1)} %copy-done.5, bf16[384,256]{1,0:T(8,128)(2,1)S(1)} %copy-done.4, ...), custom_call_target="tpu_custom_call" | custom-call | flops 8000000000 | bytes 1179648 | tf_op jit(solution)/shard_map/pallas_call | solution.py:208
  133.3 18.7 %all_to_all.21.refs_0_ = f32[128,9,1,128]{3,2,1,0:T(1,128)S(1)} all-to-all(f32[128,9,1,128]{3,2,1,0:T(1,128)S(1)} %shard_map.177), channel_id=1, replica_groups=mesh['base'=4,'slab'=32] {'base','slab'}, dimensions={0} | all-to-all | bytes 1179648 | tf_op jit(solution)/shard_map/all_to_all | solution.py:482
  152.0 1.8 %shard_map.178 = f32[32,4096]{1,0:T(8,128)} custom-call(f32[128,9,1,128]{3,2,1,0:T(1,128)S(1)} %all_to_all.21.refs_0_, f32[32,4096]{1,0:T(8,128)S(1)} %copy-done, f32[2,32,128]{2,1,0:T(8,128)S(1)} %copy-done.6, bf16[768,256]{1,0:T(8,128)(2,1)S(1)} %copy-done.2), custom_call_target="tpu_custom_call" | custom-call | flops 3000000000 | bytes 1048576 | tf_op jit(solution)/shard_map/pallas_call | solution.py:208
  (11 shorter events, 0.0 us)
Async XLA Ops:
  4.5 37.6 %all-to-all-start = ((f32[128,26,1,128]{3,2,1,0:T(1,128)}), f32[128,26,1,128]{3,2,1,0:T(1,128)S(1)}, u32[]{:S(2)}, u32[]{:S(2)}) async-start(f32[128,26,1,128]{3,2,1,0:T(1,128)} %shard_map.172), calls=%async_computation | async-start | bytes 3407872 | tf_op jit(solution)/shard_map/all_to_all | solution.py:482
  51.7 28.7 %all-to-all-start.1 = ((f32[4,2,8,32,128]{4,3,2,1,0:T(8,128)}), f32[4,2,8,32,128]{4,3,2,1,0:T(8,128)}, u32[]{:S(2)}, u32[]{:S(2)}) async-start(f32[4,2,8,32,128]{4,3,2,1,0:T(8,128)} %shard_map.173), calls=%async_computation.1 | async-start | bytes 2097152 | tf_op jit(solution)/shard_map/all_to_all | solution.py:482
  64.4 11.8 %collective-permute-start = (f32[2,8,32,128]{3,2,1,0:T(8,128)S(1)}, f32[2,8,32,128]{3,2,1,0:T(8,128)S(1)}, u32[]{:S(2)}, u32[]{:S(2)}) collective-permute-start(f32[2,8,32,128]{3,2,1,0:T(8,128)S(1)} %get-tuple-element.28), channel_id=1, source_target_pairs={{0,32},{32,64},{64,96},{96,0},{1,33},{33,65},{65,97},{97,1},{2,34}... | collective-permute-start | bytes 786440 | tf_op jit(solution)/shard_map/ppermute | solution.py:522
  65.0 15.4 %collective-permute-start.1 = (f32[2,8,32,128]{3,2,1,0:T(8,128)S(1)}, f32[2,8,32,128]{3,2,1,0:T(8,128)S(1)}, u32[]{:S(2)}, u32[]{:S(2)}) collective-permute-start(f32[2,8,32,128]{3,2,1,0:T(8,128)S(1)} %get-tuple-element.29), channel_id=1, source_target_pairs={{0,64},{32,96},{64,0},{96,32},{1,65},{33,97},{65,1},{97,33},{2,66}... | collective-permute-start | bytes 786440 | tf_op jit(solution)/shard_map/ppermute | solution.py:522
  68.3 12.2 %collective-permute-start.2 = (f32[2,8,32,128]{3,2,1,0:T(8,128)S(1)}, f32[2,8,32,128]{3,2,1,0:T(8,128)S(1)}, u32[]{:S(2)}, u32[]{:S(2)}) collective-permute-start(f32[2,8,32,128]{3,2,1,0:T(8,128)S(1)} %get-tuple-element.30), channel_id=1, source_target_pairs={{0,96},{32,0},{64,32},{96,64},{1,97},{33,1},{65,33},{97,65},{2,98}... | collective-permute-start | bytes 786440 | tf_op jit(solution)/shard_map/ppermute | solution.py:522
  86.1 37.2 %copy-start.1 = (bf16[256,768]{1,0:T(8,128)(2,1)S(1)}, bf16[256,768]{1,0:T(8,128)(2,1)}, u32[]{:S(2)}) copy-start(bf16[256,768]{1,0:T(8,128)(2,1)} %constant.30.clone.refs_7_.refs_1_.refs_2_) | copy-start | bytes 1179652
  86.1 37.2 %copy-start.3 = (f32[2,2,128,128]{3,2,1,0:T(8,128)S(1)}, f32[2,2,128,128]{3,2,1,0:T(8,128)}, u32[]{:S(2)}) copy-start(f32[2,2,128,128]{3,2,1,0:T(8,128)} %constant.40.clone.refs_6_) | copy-start | bytes 786436
  86.1 37.2 %copy-start.4 = (bf16[384,256]{1,0:T(8,128)(2,1)S(1)}, bf16[384,256]{1,0:T(8,128)(2,1)}, u32[]{:S(2)}) copy-start(bf16[384,256]{1,0:T(8,128)(2,1)} %constant.38.clone.refs_4_) | copy-start | bytes 589828
  86.1 37.2 %copy-start.5 = (f32[2,128,128]{2,1,0:T(8,128)S(1)}, f32[2,128,128]{2,1,0:T(8,128)}, u32[]{:S(2)}) copy-start(f32[2,128,128]{2,1,0:T(8,128)} %constant.36.clone.refs_2_.refs_3_) | copy-start | bytes 393220
  123.3 28.7 %copy-start = (f32[32,4096]{1,0:T(8,128)S(1)}, f32[32,4096]{1,0:T(8,128)}, u32[]{:S(2)}) copy-start(f32[32,4096]{1,0:T(8,128)} %refs_1_.4) | copy-start | bytes 1572868
  123.3 28.7 %copy-start.2 = (bf16[768,256]{1,0:T(8,128)(2,1)S(1)}, bf16[768,256]{1,0:T(8,128)(2,1)}, u32[]{:S(2)}) copy-start(bf16[768,256]{1,0:T(8,128)(2,1)} %constant.31.clone.refs_3_) | copy-start | bytes 1179652
  123.3 28.6 %copy-start.6 = (f32[2,32,128]{2,1,0:T(8,128)S(1)}, f32[2,32,128]{2,1,0:T(8,128)}, u32[]{:S(2)}) copy-start(f32[2,32,128]{2,1,0:T(8,128)} %constant.32.clone.refs_6_.refs_2_) | copy-start | bytes 98308

commit v4 on v3

--- a/solution.py
+++ b/solution.py
@@ -13,7 +13,7 @@
 G = 8192
 IMG = 4096
 TILE = 128
-GROUP = 8
+GROUP = 12
 GRANT = 20 * 2**20
 
 NN = (((1,), (0,)), ((), ()))
@@ -93,9 +93,9 @@
         c, s = wave(n(32), n(32) // 2 + 8, 32)
         keep = (n(32) % 2 == half)[None, :]
         rb += [np.kron(eye, c * keep) / G, np.kron(eye, -s * keep) / G]
-    out["w_b"] = spread_table(np.concatenate(wb), LEFT[6], 1)
+    out["w_b"] = spread_table(np.concatenate(wb), LEFT[3], 1)
     out["tw_b"] = np.stack(twb)
-    out["r_b"] = spread_table(np.concatenate(rb), RIGHT[6], 0)
+    out["r_b"] = spread_table(np.concatenate(rb), RIGHT[3], 0)
     return {k: v if v.dtype == ml_dtypes.bfloat16 else v.astype(np.float32) for k, v in out.items()}
 
 
@@ -217,7 +217,6 @@
 
 def first_kernel(owner, tile, residual, position, xi, amplitude, tw, w, out, count, mid):
     n_base, n_slab = 4, 32
-    out[:, 16] = jnp.zeros((out.shape[0], 1, 128), f32)
 
     def clear(i, _):
         count[i] = 0
@@ -242,11 +241,11 @@
         for part in range(2):
             out[to, slot * 4 + part] = residual[i, part : part + 1, :]
             out[to, slot * 4 + 2 + part] = position[i, part : part + 1, :]
-        out[to, 16] = jnp.where(lane == slot, (col + 1).astype(f32), out[to, 16])
+        out[to, 24] = jnp.where(lane == 64 + slot, (col + 1).astype(f32), out[to, 24])
         return 0
 
+    row_transform(*(a.ready() for a in (xi, amplitude, tw, w)), out, mid)
     lax.fori_loop(0, owner.shape[0], step, 0, unroll=4)
-    row_transform(*(a.ready() for a in (xi, amplitude, tw, w)), out, mid)
 
 
 def taps(d):
@@ -363,10 +362,10 @@
         res = mm(w[...], part, NT)
         for k in range(2):
             for ri in range(2):
-                out[:, 17 + ri * 4 + 2 * pair + k, 0, :] = res[128 * ri : 128 * ri + 128, 128 * k : 128 * k + 128]
+                out[:, 16 + ri * 4 + 2 * pair + k, 0, :] = res[128 * ri : 128 * ri + 128, 128 * k : 128 * k + 128]
     part = spread(mid[16:20].reshape(128, 256), RIGHT[3], 1)
     res = mm(w[...], part, NT)
-    out[:, 25, 0, :] = beside(res[0:128], res[128:256])
+    out[:, 24, 0, :] = beside(res[0:128], res[128:256])
 
 
 def low_lanes():
@@ -382,11 +381,11 @@
     chunk = []
     for k in range(2):
         j = 2 * pair + k
-        re, im = field[:, 17 + j % 4, 0, :], field[:, 21 + j % 4, 0, :]
+        re, im = field[:, 16 + j % 4, 0, :], field[:, 20 + j % 4, 0, :]
         if j >= 4:
             im = -im
         if j == 4:
-            own = field[:, 25, 0, :]
+            own = field[:, 24, 0, :]
             re, im = jnp.where(low_lanes(), own, re), jnp.where(low_lanes(), pltpu.roll(own, 96, 1), im)
         chunk.append((re, im))
     return jnp.concatenate(
@@ -423,12 +422,12 @@
 def image_kernel(sky, uv, w, tw_f, r_y, w_b, tw_b, r_b, out):
     done = []
     for pair in range(4):
-        a = mm(w_b[...], spread(chunks(uv, pair), RIGHT[6], 0))
+        a = mm(w_b[...], spread(chunks(uv, pair), RIGHT[3], 0))
         parts = [[], []]
         for h in range(2):
             for k, (re, im) in enumerate(zip(halves(a, 256 * h), halves(a, 256 * h + 128))):
                 parts[k] += twist(re, im, tw_b[h])
-        back = mm(spread(stacked(parts), LEFT[6], 1), r_b[...])
+        back = mm(spread(stacked(parts), LEFT[3], 1), r_b[...])
         a = mm(spread(sky[pair] * back, LEFT[3], 1), r_y[...])
         turn = [twist(a[128 * k : 128 * k + 128, 0:128], a[128 * k : 128 * k + 128, 128:256], tw_f) for k in range(2)]
         turn = jnp.concatenate([jnp.concatenate([turn[k][ri] for k in range(2)], axis=1) for ri in range(2)], axis=0)
@@ -486,7 +485,7 @@
     me = lax.axis_index("base").astype(jnp.int32).reshape(1)
     packed = call(
         first_kernel,
-        (devices, 26, 1, 128),
+        (devices, 25, 1, 128),
         [SM, SM] + [VM] * 6,
         [SM((devices,), jnp.int32), VM((20, 32, 256), f32)],
         2e9,
@@ -502,7 +501,7 @@
         ],
     )(owner[:, 0], tile_local, residual, position, xi, amplitude, t["tw_row"], t["w128"])
     data = exchange(packed, everywhere)
-    tags = data[:, 16, 0, 0:4].reshape(4 * devices).astype(jnp.int32)
+    tags = data[:, 24, 0, 64:68].reshape(4 * devices).astype(jnp.int32)
     spare = [VM((4, TILE, TILE), f32), SM((4 * devices + GROUP,), jnp.int32)]
     shape = (2, 8, 32, 128)
     whole = call(
@@ -553,8 +552,8 @@
         8e9,
         [
             (0, VM((4, 256, 128), f32)),
-            (5, VM((512, 1536), bf16)),
-            (7, VM((3072, 128), bf16)),
+            (5, VM((512, 768), bf16)),
+            (7, VM((1536, 128), bf16)),
         ],
     )(sky, cols, t["w128"], t["tw_f"], t["r_y"], t["w_b"], t["tw_b"], t["r_b"])
     fold = exchange(fold, everywhere)

time: 152 us -> 146 us (0.961)
  starting transfers between devices: 20.8 us -> 26.8 us
  blocking collectives: 55.8 us -> 50.4 us
  Pallas kernels: 43.2 us -> 40.2 us
  waiting for transfers between devices: 33.5 us -> 30.8 us
    all_to_all x2, blocking collectives: 55.8 us -> 50.4 us  [exchange(): return lax.all_to_all(a, axis, split_axis=0, concat_axis=0, tiled=True)]
    ppermute x3, starting transfers between devices: 5.05 us -> 10.2 us  [per_device(): lax.ppermute(parts[k], 'base', [(i, (i + k) % n_base) for i in range(n_ba...]
    pallas_call x7, Pallas kernels: 43.2 us -> 40.2 us  [placed(): results = got(*arrays)]
    ppermute x3, waiting for transfers between devices: 7.34 us -> 5.36 us  [per_device(): lax.ppermute(parts[k], 'base', [(i, (i + k) % n_base) for i in range(n_ba...]
where the time goes in v4:
time: 146 us; the launch traced here: 149 us
  blocking collectives  50.4 us (35%)
  Pallas kernels  40.2 us (28%)
  waiting for transfers between devices  30.8 us (21%)
  starting transfers between devices  26.8 us (18%)
    all_to_all x2, blocking collectives, exchange(): return lax.all_to_all(a, axis, split_axis=0, concat_axis=0, tiled=True)  50.4 us
    pallas_call x7, Pallas kernels, placed(): results = got(*arrays)  40.2 us
    all_to_all x2, waiting for transfers between devices, exchange(): return lax.all_to_all(a, axis, split_axis=0, concat_axis=0, tiled=True)  25.4 us
    all_to_all x2, starting transfers between devices, exchange(): return lax.all_to_all(a, axis, split_axis=0, concat_axis=0, tiled=True)  16.6 us
    ppermute x3, starting transfers between devices, per_device(): lax.ppermute(parts[k], 'base', [(i, (i + k) % n_base) for i in range(n_ba...  10.2 us
    ppermute x3, waiting for transfers between devices, per_device(): lax.ppermute(parts[k], 'base', [(i, (i + k) % n_base) for i in range(n_ba...  5.36 us
  transfers between devices with their start and end apart: 5, of which 3 were waited for; matrix products, arithmetic and copies ran while one was open for 0% of the time, Pallas kernels for 8%

profile of v4, /device:TPU:1, one launch (start us, length us, event | category | flops | bytes accessed | tf_op | source)
XLA Modules:
  0.0 148.7 jit_solution(17523160334352365834)
XLA Ops:
  0.0 5.1 %shard_map.172 = f32[128,25,1,128]{3,2,1,0:T(1,128)} custom-call(s32[128]{0:T(128)} %bitcast.4, s32[128]{0:T(128)} %refs_1_.3, f32[128,2,128]{2,1,0:T(2,128)} %refs_2_.4, f32[128,2,128]{2,1,0:T(2,128)} %refs_3_.4, f32[32,4096]{1,0:T(8,128)} %refs_4_.2, f32[32,4096]{1,0:T(8,128)} %refs_1_.4, f32[2,32,128]{2,1,0:T(8,128)} %constant.32.clone.refs_6_.refs_2_, ...), custom_call_target="tpu_custom_call" | custom-call | flops 2000000000 | bytes 3276800 | tf_op jit(solution)/shard_map/pallas_call | solution.py:208
  5.1 11.5 %all-to-all-start = ((f32[128,25,1,128]{3,2,1,0:T(1,128)}), f32[128,25,1,128]{3,2,1,0:T(1,128)S(1)}, u32[]{:S(2)}, u32[]{:S(2)}) async-start(f32[128,25,1,128]{3,2,1,0:T(1,128)} %shard_map.172), calls=%async_computation | async-start | bytes 3276800 | tf_op jit(solution)/shard_map/all_to_all | solution.py:481
  16.6 25.4 %all-to-all-done.refs_1_.refs_2_.refs_0_ = f32[128,25,1,128]{3,2,1,0:T(1,128)S(1)} async-done(((f32[128,25,1,128]{3,2,1,0:T(1,128)}), f32[128,25,1,128]{3,2,1,0:T(1,128)S(1)}, u32[]{:S(2)}, u32[]{:S(2)}) %all-to-all-start) | async-done | bytes 1638432 | tf_op jit(solution)/shard_map/all_to_all | solution.py:481
  42.0 0.3 fusion
  42.2 0.1 convert_element_type.6.refs_0_.refs_1_
  42.4 9.2 %shard_map.173 = f32[4,2,8,32,128]{4,3,2,1,0:T(8,128)} custom-call(s32[512]{0:T(512)S(1)} %convert_element_type.6.refs_0_.refs_1_, f32[128,25,1,128]{3,2,1,0:T(1,128)S(1)} %all-to-all-done.refs_1_.refs_2_.refs_0_), custom_call_target="tpu_custom_call" | custom-call | flops 20000000000 | bytes 2097152 | tf_op jit(solution)/shard_map/pallas_call | solution.py:208
  51.5 5.1 %all-to-all-start.1 = ((f32[4,2,8,32,128]{4,3,2,1,0:T(8,128)}), f32[4,2,8,32,128]{4,3,2,1,0:T(8,128)}, u32[]{:S(2)}, u32[]{:S(2)}) async-start(f32[4,2,8,32,128]{4,3,2,1,0:T(8,128)} %shard_map.173), calls=%async_computation.1 | async-start | bytes 2097152 | tf_op jit(solution)/shard_map/all_to_all | solution.py:481
  56.6 8.3 %shard_map.174 = (f32[2,8,32,128]{3,2,1,0:T(8,128)S(1)}, f32[2,8,32,128]{3,2,1,0:T(8,128)S(1)}, f32[2,8,32,128]{3,2,1,0:T(8,128)S(1)}, f32[2,8,32,128]{3,2,1,0:T(8,128)S(1)}) custom-call(s32[1]{0:T(128)} %bitcast.refs_0_, s32[512]{0:T(512)S(1)} %convert_element_type.6.refs_0_.refs_1_, f32[128,25,1,128]{3,2,1,0:T(1,128)S(1)} %all-to-all-done.refs_1_.refs_2_.refs_0_), custom_call_target="tpu_custom_call" | custom-call | flops 20000000000 | bytes 2097152 | tf_op jit(solution)/shard_map/pallas_call | solution.py:208
  64.9 7.8 %collective-permute-start = (f32[2,8,32,128]{3,2,1,0:T(8,128)S(1)}, f32[2,8,32,128]{3,2,1,0:T(8,128)S(1)}, u32[]{:S(2)}, u32[]{:S(2)}) collective-permute-start(f32[2,8,32,128]{3,2,1,0:T(8,128)S(1)} %get-tuple-element.28), channel_id=1, source_target_pairs={{0,32},{32,64},{64,96},{96,0},{1,33},{33,65},{65,97},{97,1},{2,34}... | collective-permute-start | bytes 786440 | tf_op jit(solution)/shard_map/ppermute | solution.py:521
  72.7 2.5 %collective-permute-start.2 = (f32[2,8,32,128]{3,2,1,0:T(8,128)S(1)}, f32[2,8,32,128]{3,2,1,0:T(8,128)S(1)}, u32[]{:S(2)}, u32[]{:S(2)}) collective-permute-start(f32[2,8,32,128]{3,2,1,0:T(8,128)S(1)} %get-tuple-element.30), channel_id=1, source_target_pairs={{0,96},{32,0},{64,32},{96,64},{1,97},{33,1},{65,33},{97,65},{2,98}... | collective-permute-start | bytes 786440 | tf_op jit(solution)/shard_map/ppermute | solution.py:521
  75.2 3.7 %shard_map.175.refs_0_ = f32[4,256,128]{2,1,0:T(8,128)} custom-call(f32[128,25,1,128]{3,2,1,0:T(1,128)S(1)} %all-to-all-done.refs_1_.refs_2_.refs_0_, bf16[256,768]{1,0:T(8,128)(2,1)} %constant.30.clone.refs_7_.refs_1_.refs_2_, f32[2,128,128]{2,1,0:T(8,128)} %constant.36.clone.refs_2_.refs_3_, bf16[768,128]{1,0:T(8,128)(2,1)} %constant.37.clone.refs_3_), custom_call_target="tpu_custom_call" | custom-call | flops 4000000000 | bytes 1048576 | tf_op jit(solution)/shard_map/pallas_call | solution.py:208
  78.8 5.1 %collective-permute-done.1.refs_4_ = f32[2,8,32,128]{3,2,1,0:T(8,128)S(1)} collective-permute-done((f32[2,8,32,128]{3,2,1,0:T(8,128)S(1)}, f32[2,8,32,128]{3,2,1,0:T(8,128)S(1)}, u32[]{:S(2)}, u32[]{:S(2)}) %collective-permute-start.1) | collective-permute-done | bytes 262176 | tf_op jit(solution)/shard_map/ppermute | solution.py:521
  83.9 0.3 collective-permute-done.2.refs_5_
  84.2 5.6 %shard_map.176 = f32[64,2,16,128]{3,2,1,0:T(8,128)S(1)} custom-call(s32[1]{0:T(128)} %bitcast.refs_0_, f32[4,2,8,32,128]{4,3,2,1,0:T(8,128)} %all-to-all-done.1.refs_1_, f32[2,8,32,128]{3,2,1,0:T(8,128)S(1)} %get-tuple-element.27.refs_2_, f32[2,8,32,128]{3,2,1,0:T(8,128)S(1)} %collective-permute-done.refs_3_, ...), custom_call_target="tpu_custom_call" | custom-call | flops 4000000000 | bytes 2097152 | tf_op jit(solution)/shard_map/pallas_call | solution.py:208
  89.8 0.0 copy-start.1
  89.8 0.0 copy-start.3
  89.8 0.0 copy-start.4
  89.8 0.0 copy-start.5
  89.8 31.7 %all_to_all.20.refs_1_ = f32[128,16,128]{2,1,0:T(8,128)S(1)} all-to-all(f32[128,16,128]{2,1,0:T(8,128)S(1)} %bitcast.3), channel_id=1, replica_groups=mesh['base'=4,'slab'=32] {'base','slab'}, dimensions={0} | all-to-all | bytes 2097152 | tf_op jit(solution)/shard_map/all_to_all | solution.py:481
  121.6 0.0 copy-start.2
  121.6 0.0 copy-start.6
  121.6 6.6 %shard_map.177 = f32[128,9,1,128]{3,2,1,0:T(1,128)S(1)} custom-call(f32[4,256,128]{2,1,0:T(8,128)} %shard_map.175.refs_0_, f32[128,16,128]{2,1,0:T(8,128)S(1)} %all_to_all.20.refs_1_, bf16[256,768]{1,0:T(8,128)(2,1)S(1)} %copy-done.1, f32[2,128,128]{2,1,0:T(8,128)S(1)} %copy-done.5, bf16[384,256]{1,0:T(8,128)(2,1)S(1)} %copy-done.4, ...), custom_call_target="tpu_custom_call" | custom-call | flops 8000000000 | bytes 1179648 | tf_op jit(solution)/shard_map/pallas_call | solution.py:208
  128.1 18.7 %all_to_all.21.refs_0_ = f32[128,9,1,128]{3,2,1,0:T(1,128)S(1)} all-to-all(f32[128,9,1,128]{3,2,1,0:T(1,128)S(1)} %shard_map.177), channel_id=1, replica_groups=mesh['base'=4,'slab'=32] {'base','slab'}, dimensions={0} | all-to-all | bytes 1179648 | tf_op jit(solution)/shard_map/all_to_all | solution.py:481
  146.8 1.8 %shard_map.178 = f32[32,4096]{1,0:T(8,128)} custom-call(f32[128,9,1,128]{3,2,1,0:T(1,128)S(1)} %all_to_all.21.refs_0_, f32[32,4096]{1,0:T(8,128)S(1)} %copy-done, f32[2,32,128]{2,1,0:T(8,128)S(1)} %copy-done.6, bf16[768,256]{1,0:T(8,128)(2,1)S(1)} %copy-done.2), custom_call_target="tpu_custom_call" | custom-call | flops 3000000000 | bytes 1048576 | tf_op jit(solution)/shard_map/pallas_call | solution.py:208
  (11 shorter events, 0.0 us)
Async XLA Ops:
  5.1 36.9 %all-to-all-start = ((f32[128,25,1,128]{3,2,1,0:T(1,128)}), f32[128,25,1,128]{3,2,1,0:T(1,128)S(1)}, u32[]{:S(2)}, u32[]{:S(2)}) async-start(f32[128,25,1,128]{3,2,1,0:T(1,128)} %shard_map.172), calls=%async_computation | async-start | bytes 3276800 | tf_op jit(solution)/shard_map/all_to_all | solution.py:481
  51.5 32.7 %all-to-all-start.1 = ((f32[4,2,8,32,128]{4,3,2,1,0:T(8,128)}), f32[4,2,8,32,128]{4,3,2,1,0:T(8,128)}, u32[]{:S(2)}, u32[]{:S(2)}) async-start(f32[4,2,8,32,128]{4,3,2,1,0:T(8,128)} %shard_map.173), calls=%async_computation.1 | async-start | bytes 2097152 | tf_op jit(solution)/shard_map/all_to_all | solution.py:481
  64.9 13.9 %collective-permute-start = (f32[2,8,32,128]{3,2,1,0:T(8,128)S(1)}, f32[2,8,32,128]{3,2,1,0:T(8,128)S(1)}, u32[]{:S(2)}, u32[]{:S(2)}) collective-permute-start(f32[2,8,32,128]{3,2,1,0:T(8,128)S(1)} %get-tuple-element.28), channel_id=1, source_target_pairs={{0,32},{32,64},{64,96},{96,0},{1,33},{33,65},{65,97},{97,1},{2,34}... | collective-permute-start | bytes 786440 | tf_op jit(solution)/shard_map/ppermute | solution.py:521
  72.7 11.2 %collective-permute-start.1 = (f32[2,8,32,128]{3,2,1,0:T(8,128)S(1)}, f32[2,8,32,128]{3,2,1,0:T(8,128)S(1)}, u32[]{:S(2)}, u32[]{:S(2)}) collective-permute-start(f32[2,8,32,128]{3,2,1,0:T(8,128)S(1)} %get-tuple-element.29), channel_id=1, source_target_pairs={{0,64},{32,96},{64,0},{96,32},{1,65},{33,97},{65,1},{97,33},{2,66}... | collective-permute-start | bytes 786440 | tf_op jit(solution)/shard_map/ppermute | solution.py:521
  72.7 11.5 %collective-permute-start.2 = (f32[2,8,32,128]{3,2,1,0:T(8,128)S(1)}, f32[2,8,32,128]{3,2,1,0:T(8,128)S(1)}, u32[]{:S(2)}, u32[]{:S(2)}) collective-permute-start(f32[2,8,32,128]{3,2,1,0:T(8,128)S(1)} %get-tuple-element.30), channel_id=1, source_target_pairs={{0,96},{32,0},{64,32},{96,64},{1,97},{33,1},{65,33},{97,65},{2,98}... | collective-permute-start | bytes 786440 | tf_op jit(solution)/shard_map/ppermute | solution.py:521
  89.8 31.7 %copy-start.1 = (bf16[256,768]{1,0:T(8,128)(2,1)S(1)}, bf16[256,768]{1,0:T(8,128)(2,1)}, u32[]{:S(2)}) copy-start(bf16[256,768]{1,0:T(8,128)(2,1)} %constant.30.clone.refs_7_.refs_1_.refs_2_) | copy-start | bytes 1179652
  89.8 31.7 %copy-start.3 = (f32[2,2,128,128]{3,2,1,0:T(8,128)S(1)}, f32[2,2,128,128]{3,2,1,0:T(8,128)}, u32[]{:S(2)}) copy-start(f32[2,2,128,128]{3,2,1,0:T(8,128)} %constant.40.clone.refs_6_) | copy-start | bytes 786436
  89.8 31.7 %copy-start.4 = (bf16[384,256]{1,0:T(8,128)(2,1)S(1)}, bf16[384,256]{1,0:T(8,128)(2,1)}, u32[]{:S(2)}) copy-start(bf16[384,256]{1,0:T(8,128)(2,1)} %constant.38.clone.refs_4_) | copy-start | bytes 589828
  89.8 31.7 %copy-start.5 = (f32[2,128,128]{2,1,0:T(8,128)S(1)}, f32[2,128,128]{2,1,0:T(8,128)}, u32[]{:S(2)}) copy-start(f32[2,128,128]{2,1,0:T(8,128)} %constant.36.clone.refs_2_.refs_3_) | copy-start | bytes 393220
  121.5 25.3 %copy-start = (f32[32,4096]{1,0:T(8,128)S(1)}, f32[32,4096]{1,0:T(8,128)}, u32[]{:S(2)}) copy-start(f32[32,4096]{1,0:T(8,128)} %refs_1_.4) | copy-start | bytes 1572868
  121.6 25.3 %copy-start.2 = (bf16[768,256]{1,0:T(8,128)(2,1)S(1)}, bf16[768,256]{1,0:T(8,128)(2,1)}, u32[]{:S(2)}) copy-start(bf16[768,256]{1,0:T(8,128)(2,1)} %constant.31.clone.refs_3_) | copy-start | bytes 1179652
  121.6 25.3 %copy-start.6 = (f32[2,32,128]{2,1,0:T(8,128)S(1)}, f32[2,32,128]{2,1,0:T(8,128)}, u32[]{:S(2)}) copy-start(f32[2,32,128]{2,1,0:T(8,128)} %constant.32.clone.refs_6_.refs_2_) | copy-start | bytes 98308

commit v5 on v4

--- a/solution.py
+++ b/solution.py
@@ -13,7 +13,8 @@
 G = 8192
 IMG = 4096
 TILE = 128
-GROUP = 12
+GROUP = 24
+REST = 8
 GRANT = 20 * 2**20
 
 NN = (((1,), (0,)), ((), ()))
@@ -215,7 +216,7 @@
 SM = pltpu.SMEM
 
 
-def first_kernel(owner, tile, residual, position, xi, amplitude, tw, w, out, count, mid):
+def first_kernel(owner, tile, residual, position, xi, amplitude, tw, w, out, count, mid, tags):
     n_base, n_slab = 4, 32
 
     def clear(i, _):
@@ -225,27 +226,32 @@
     lax.fori_loop(0, count.shape[0], clear, 0, unroll=8)
     owner, tile, residual, position = (a.ready() for a in (owner, tile, residual, position))
     lane = lax.broadcasted_iota(jnp.int32, (1, 128), 1)
+    tags[...] = jnp.zeros_like(tags)
 
     def step(i, _):
-        o, t = owner[i], tile[i]
-        row = (o & (n_slab - 1)) * 2 + (t >> 4)
-        group, col = o >> 5, t & 15
-        flip = (row >= n_slab).astype(jnp.int32)
-        row = jnp.where(flip == 1, 2 * n_slab - 1 - row, row)
-        group = jnp.where(flip == 1, n_base - 1 - group, group)
-        col = jnp.where(flip == 1, 15 - col, col)
-        k = count[o]
-        count[o] = k + 1
-        slot = flip * 2 + (k & 1)
-        to = group * n_slab + row
-        for part in range(2):
-            out[to, slot * 4 + part] = residual[i, part : part + 1, :]
-            out[to, slot * 4 + 2 + part] = position[i, part : part + 1, :]
-        out[to, 24] = jnp.where(lane == 64 + slot, (col + 1).astype(f32), out[to, 24])
+        placed = []
+        for u in range(8):
+            at = i * 8 + u
+            o, t = owner[at], tile[at]
+            row = (o & (n_slab - 1)) * 2 + (t >> 4)
+            group, col = o >> 5, t & 15
+            flip = (row >= n_slab).astype(jnp.int32)
+            row = jnp.where(flip == 1, 2 * n_slab - 1 - row, row)
+            group = jnp.where(flip == 1, n_base - 1 - group, group)
+            col = jnp.where(flip == 1, 15 - col, col)
+            k = count[o]
+            count[o] = k + 1
+            placed.append((at, group * n_slab + row, flip * 2 + (k & 1), (col + 1).astype(f32)))
+        parts = [(residual[at], position[at]) for at, _, _, _ in placed]
+        for (at, to, slot, tag), (value, place) in zip(placed, parts):
+            for part in range(2):
+                out[to, slot * 4 + part] = value[part : part + 1]
+                out[to, slot * 4 + 2 + part] = place[part : part + 1]
+            tags[to] = jnp.where(lane == 64 + slot, tag, tags[to])
         return 0
 
-    row_transform(*(a.ready() for a in (xi, amplitude, tw, w)), out, mid)
-    lax.fori_loop(0, owner.shape[0], step, 0, unroll=4)
+    lax.fori_loop(0, owner.shape[0] // 8, step, 0)
+    row_transform(*(a.ready() for a in (xi, amplitude, tw, w)), out, mid, tags)
 
 
 def taps(d):
@@ -277,32 +283,40 @@
         return n + ((tag > 0) & (tag <= wide)).astype(jnp.int32)
 
     n = lax.fori_loop(0, slots, scan, jnp.int32(0), unroll=8)
-    for extra in range(GROUP):
+    for extra in range(REST):
         order[n + extra] = order[jnp.maximum(n - 1, 0)]
 
     def down(row):
         return jnp.transpose(jnp.broadcast_to(row, (TILE, TILE)))
 
-    def group(g, _):
-        for u in range(GROUP):
-            at = g * GROUP + u
-            s = order[at]
-            used = (at < n).astype(f32)
-            src, slot = s >> 2, s & 3
-            flip = slot >> 1
-            t = jnp.clip(tags[s] - first - 1, 0, wide - 1)
-            value_re = data[src, slot * 4] * used
-            value_im = data[src, slot * 4 + 1] * (used * (1.0 - 2.0 * flip.astype(f32)))
-            rows = taps(cells[flip] - data[src, slot * 4 + 2] * 0.25)
-            cols = taps(cells[2 + flip] - down(data[src, slot * 4 + 3] * 0.25))
-            weighted = jnp.concatenate([cols * down(value_re), cols * down(value_im)], axis=1)
-            sub = mm(spread(rows, LEFT[6], 1), spread(weighted, RIGHT[6], 0))
-            for q in range(4):
-                for ri in range(2):
-                    total[(q - me) & 3, ri, t] += sub[32 * q : 32 * q + 32, 128 * ri : 128 * ri + 128]
-        return 0
-
-    lax.fori_loop(0, (n + GROUP - 1) // GROUP, group, 0)
+    def add(at):
+        s = order[at]
+        used = (at < n).astype(f32)
+        src, slot = s >> 2, s & 3
+        flip = slot >> 1
+        t = jnp.clip(tags[s] - first - 1, 0, wide - 1)
+        value_re = data[src, slot * 4] * used
+        value_im = data[src, slot * 4 + 1] * (used * (1.0 - 2.0 * flip.astype(f32)))
+        rows = taps(cells[flip] - data[src, slot * 4 + 2] * 0.25)
+        cols = taps(cells[2 + flip] - down(data[src, slot * 4 + 3] * 0.25))
+        weighted = jnp.concatenate([cols * down(value_re), cols * down(value_im)], axis=1)
+        sub = mm(spread(rows, LEFT[6], 1), spread(weighted, RIGHT[6], 0))
+        for q in range(4):
+            for ri in range(2):
+                total[(q - me) & 3, ri, t] += sub[32 * q : 32 * q + 32, 128 * ri : 128 * ri + 128]
+
+    def turn(start, count):
+        def body(g, _):
+            for u in range(count):
+                add(start + g * count + u)
+            return 0
+
+        return body
+
+    whole = n // GROUP
+    lax.fori_loop(0, whole, turn(0, GROUP), 0)
+    begun = whole * GROUP
+    lax.fori_loop(0, (n - begun + REST - 1) // REST, turn(begun, REST), 0)
 
 
 def cols_kernel(*refs):
@@ -340,7 +354,7 @@
                 out[:, chunk // 8, ri * 8 + chunk % 8, :] = res[64 * ri : 64 * ri + 64, 128 * k : 128 * k + 128]
 
 
-def row_transform(xi, amplitude, tw, w, out, mid):
+def row_transform(xi, amplitude, tw, w, out, mid, tags):
     def rows(i, _):
         at = pl.ds(pl.multiple_of(i * 8, 8), 8)
         first = [
@@ -365,7 +379,7 @@
                 out[:, 16 + ri * 4 + 2 * pair + k, 0, :] = res[128 * ri : 128 * ri + 128, 128 * k : 128 * k + 128]
     part = spread(mid[16:20].reshape(128, 256), RIGHT[3], 1)
     res = mm(w[...], part, NT)
-    out[:, 24, 0, :] = beside(res[0:128], res[128:256])
+    out[:, 24, 0, :] = beside(res[0:128], res[128:256]) + tags[:, 0, :]
 
 
 def low_lanes():
@@ -487,7 +501,7 @@
         first_kernel,
         (devices, 25, 1, 128),
         [SM, SM] + [VM] * 6,
-        [SM((devices,), jnp.int32), VM((20, 32, 256), f32)],
+        [SM((devices,), jnp.int32), VM((20, 32, 256), f32), VM((devices, 1, 128), f32)],
         2e9,
         [
             (0, SM((blocks,), jnp.int32)),
@@ -502,7 +516,7 @@
     )(owner[:, 0], tile_local, residual, position, xi, amplitude, t["tw_row"], t["w128"])
     data = exchange(packed, everywhere)
     tags = data[:, 24, 0, 64:68].reshape(4 * devices).astype(jnp.int32)
-    spare = [VM((4, TILE, TILE), f32), SM((4 * devices + GROUP,), jnp.int32)]
+    spare = [VM((4, TILE, TILE), f32), SM((4 * devices + REST,), jnp.int32)]
     shape = (2, 8, 32, 128)
     whole = call(
         functools.partial(grid_whole_kernel, 0), (n_base, *shape), [SM, VM], spare, 2e10

time: 146 us -> 146 us (level); the launches traced: 149 us -> 145 us
  starting transfers between devices: 26.8 us -> 21.2 us
  waiting for transfers between devices: 30.8 us -> 35.3 us
    ppermute x3, starting transfers between devices: 10.2 us -> 5.47 us  [per_device(): lax.ppermute(parts[k], 'base', [(i, (i + k) % n_base) for i in range(n_ba...]
    ppermute x3, waiting for transfers between devices: 5.36 us -> 9.87 us  [per_device(): lax.ppermute(parts[k], 'base', [(i, (i + k) % n_base) for i in range(n_ba...]
  transfers between devices with their start and end apart: 5 -> 5, of which waited for: 3 -> 3; matrix products, arithmetic and copies ran while one was open for 0% -> 0% of each run, Pallas kernels for 8% -> 7%
where the time goes in v5:
time: 146 us; the launch traced here: 145 us
  blocking collectives  49.5 us (34%)
  Pallas kernels  38.8 us (27%)
  waiting for transfers between devices  35.3 us (24%)
  starting transfers between devices  21.2 us (15%)
    all_to_all x2, blocking collectives, exchange(): return lax.all_to_all(a, axis, split_axis=0, concat_axis=0, tiled=True)  49.5 us
    pallas_call x7, Pallas kernels, placed(): results = got(*arrays)  38.8 us
    all_to_all x2, waiting for transfers between devices, exchange(): return lax.all_to_all(a, axis, split_axis=0, concat_axis=0, tiled=True)  25.4 us
    all_to_all x2, starting transfers between devices, exchange(): return lax.all_to_all(a, axis, split_axis=0, concat_axis=0, tiled=True)  15.7 us
    ppermute x3, waiting for transfers between devices, per_device(): lax.ppermute(parts[k], 'base', [(i, (i + k) % n_base) for i in range(n_ba...  9.87 us
    ppermute x3, starting transfers between devices, per_device(): lax.ppermute(parts[k], 'base', [(i, (i + k) % n_base) for i in range(n_ba...  5.47 us
  transfers between devices with their start and end apart: 5, of which 3 were waited for; matrix products, arithmetic and copies ran while one was open for 0% of the time, Pallas kernels for 7%

profile of v5, /device:TPU:1, one launch (start us, length us, event | category | flops | bytes accessed | tf_op | source)
XLA Modules:
  0.0 145.3 jit_solution(11371904055403436015)
XLA Ops:
  0.0 4.7 %shard_map.172 = f32[128,25,1,128]{3,2,1,0:T(1,128)} custom-call(s32[128]{0:T(128)} %bitcast.4, s32[128]{0:T(128)} %refs_1_.3, f32[128,2,128]{2,1,0:T(2,128)} %refs_2_.4, f32[128,2,128]{2,1,0:T(2,128)} %refs_3_.4, f32[32,4096]{1,0:T(8,128)} %refs_4_.2, f32[32,4096]{1,0:T(8,128)} %refs_1_.4, f32[2,32,128]{2,1,0:T(8,128)} %constant.32.clone.refs_6_.refs_2_, ...), custom_call_target="tpu_custom_call" | custom-call | flops 2000000000 | bytes 3276800 | tf_op jit(solution)/shard_map/pallas_call | solution.py:209
  4.7 11.5 %all-to-all-start = ((f32[128,25,1,128]{3,2,1,0:T(1,128)}), f32[128,25,1,128]{3,2,1,0:T(1,128)S(1)}, u32[]{:S(2)}, u32[]{:S(2)}) async-start(f32[128,25,1,128]{3,2,1,0:T(1,128)} %shard_map.172), calls=%async_computation | async-start | bytes 3276800 | tf_op jit(solution)/shard_map/all_to_all | solution.py:495
  16.2 25.4 %all-to-all-done.refs_1_.refs_2_.refs_0_ = f32[128,25,1,128]{3,2,1,0:T(1,128)S(1)} async-done(((f32[128,25,1,128]{3,2,1,0:T(1,128)}), f32[128,25,1,128]{3,2,1,0:T(1,128)S(1)}, u32[]{:S(2)}, u32[]{:S(2)}) %all-to-all-start) | async-done | bytes 1638432 | tf_op jit(solution)/shard_map/all_to_all | solution.py:495
  41.6 0.3 fusion
  41.9 0.1 convert_element_type.6.refs_0_.refs_1_
  42.0 9.3 %shard_map.173 = f32[4,2,8,32,128]{4,3,2,1,0:T(8,128)} custom-call(s32[512]{0:T(512)S(1)} %convert_element_type.6.refs_0_.refs_1_, f32[128,25,1,128]{3,2,1,0:T(1,128)S(1)} %all-to-all-done.refs_1_.refs_2_.refs_0_), custom_call_target="tpu_custom_call" | custom-call | flops 20000000000 | bytes 2097152 | tf_op jit(solution)/shard_map/pallas_call | solution.py:209
  51.3 4.2 %all-to-all-start.1 = ((f32[4,2,8,32,128]{4,3,2,1,0:T(8,128)}), f32[4,2,8,32,128]{4,3,2,1,0:T(8,128)}, u32[]{:S(2)}, u32[]{:S(2)}) async-start(f32[4,2,8,32,128]{4,3,2,1,0:T(8,128)} %shard_map.173), calls=%async_computation.1 | async-start | bytes 2097152 | tf_op jit(solution)/shard_map/all_to_all | solution.py:495
  55.5 7.1 %shard_map.174 = (f32[2,8,32,128]{3,2,1,0:T(8,128)S(1)}, f32[2,8,32,128]{3,2,1,0:T(8,128)S(1)}, f32[2,8,32,128]{3,2,1,0:T(8,128)S(1)}, f32[2,8,32,128]{3,2,1,0:T(8,128)S(1)}) custom-call(s32[1]{0:T(128)} %bitcast.refs_0_, s32[512]{0:T(512)S(1)} %convert_element_type.6.refs_0_.refs_1_, f32[128,25,1,128]{3,2,1,0:T(1,128)S(1)} %all-to-all-done.refs_1_.refs_2_.refs_0_), custom_call_target="tpu_custom_call" | custom-call | flops 20000000000 | bytes 2097152 | tf_op jit(solution)/shard_map/pallas_call | solution.py:209
  62.7 2.7 %collective-permute-start = (f32[2,8,32,128]{3,2,1,0:T(8,128)S(1)}, f32[2,8,32,128]{3,2,1,0:T(8,128)S(1)}, u32[]{:S(2)}, u32[]{:S(2)}) collective-permute-start(f32[2,8,32,128]{3,2,1,0:T(8,128)S(1)} %get-tuple-element.28), channel_id=1, source_target_pairs={{0,32},{32,64},{64,96},{96,0},{1,33},{33,65},{65,97},{97,1},{2,34}... | collective-permute-start | bytes 786440 | tf_op jit(solution)/shard_map/ppermute | solution.py:535
  65.4 1.1 collective-permute-start.1
  66.5 1.6 %collective-permute-start.2 = (f32[2,8,32,128]{3,2,1,0:T(8,128)S(1)}, f32[2,8,32,128]{3,2,1,0:T(8,128)S(1)}, u32[]{:S(2)}, u32[]{:S(2)}) collective-permute-start(f32[2,8,32,128]{3,2,1,0:T(8,128)S(1)} %get-tuple-element.30), channel_id=1, source_target_pairs={{0,96},{32,0},{64,32},{96,64},{1,97},{33,1},{65,33},{97,65},{2,98}... | collective-permute-start | bytes 786440 | tf_op jit(solution)/shard_map/ppermute | solution.py:535
  68.1 3.7 %shard_map.175.refs_0_ = f32[4,256,128]{2,1,0:T(8,128)} custom-call(f32[128,25,1,128]{3,2,1,0:T(1,128)S(1)} %all-to-all-done.refs_1_.refs_2_.refs_0_, bf16[256,768]{1,0:T(8,128)(2,1)} %constant.30.clone.refs_7_.refs_1_.refs_2_, f32[2,128,128]{2,1,0:T(8,128)} %constant.36.clone.refs_2_.refs_3_, bf16[768,128]{1,0:T(8,128)(2,1)} %constant.37.clone.refs_3_), custom_call_target="tpu_custom_call" | custom-call | flops 4000000000 | bytes 1048576 | tf_op jit(solution)/shard_map/pallas_call | solution.py:209
  71.8 5.4 %collective-permute-done.refs_3_ = f32[2,8,32,128]{3,2,1,0:T(8,128)S(1)} collective-permute-done((f32[2,8,32,128]{3,2,1,0:T(8,128)S(1)}, f32[2,8,32,128]{3,2,1,0:T(8,128)S(1)}, u32[]{:S(2)}, u32[]{:S(2)}) %collective-permute-start) | collective-permute-done | bytes 262176 | tf_op jit(solution)/shard_map/ppermute | solution.py:535
  77.2 4.4 %collective-permute-done.1.refs_4_ = f32[2,8,32,128]{3,2,1,0:T(8,128)S(1)} collective-permute-done((f32[2,8,32,128]{3,2,1,0:T(8,128)S(1)}, f32[2,8,32,128]{3,2,1,0:T(8,128)S(1)}, u32[]{:S(2)}, u32[]{:S(2)}) %collective-permute-start.1) | collective-permute-done | bytes 262176 | tf_op jit(solution)/shard_map/ppermute | solution.py:535
  81.7 5.6 %shard_map.176 = f32[64,2,16,128]{3,2,1,0:T(8,128)S(1)} custom-call(s32[1]{0:T(128)} %bitcast.refs_0_, f32[4,2,8,32,128]{4,3,2,1,0:T(8,128)} %all-to-all-done.1.refs_1_, f32[2,8,32,128]{3,2,1,0:T(8,128)S(1)} %get-tuple-element.27.refs_2_, f32[2,8,32,128]{3,2,1,0:T(8,128)S(1)} %collective-permute-done.refs_3_, ...), custom_call_target="tpu_custom_call" | custom-call | flops 4000000000 | bytes 2097152 | tf_op jit(solution)/shard_map/pallas_call | solution.py:209
  87.3 0.0 copy-start.1
  87.3 0.0 copy-start.3
  87.3 0.0 copy-start.4
  87.3 0.0 copy-start.5
  87.3 30.8 %all_to_all.20.refs_1_ = f32[128,16,128]{2,1,0:T(8,128)S(1)} all-to-all(f32[128,16,128]{2,1,0:T(8,128)S(1)} %bitcast.3), channel_id=1, replica_groups=mesh['base'=4,'slab'=32] {'base','slab'}, dimensions={0} | all-to-all | bytes 2097152 | tf_op jit(solution)/shard_map/all_to_all | solution.py:495
  118.2 0.0 copy-start.2
  118.2 6.6 %shard_map.177 = f32[128,9,1,128]{3,2,1,0:T(1,128)S(1)} custom-call(f32[4,256,128]{2,1,0:T(8,128)} %shard_map.175.refs_0_, f32[128,16,128]{2,1,0:T(8,128)S(1)} %all_to_all.20.refs_1_, bf16[256,768]{1,0:T(8,128)(2,1)S(1)} %copy-done.1, f32[2,128,128]{2,1,0:T(8,128)S(1)} %copy-done.5, bf16[384,256]{1,0:T(8,128)(2,1)S(1)} %copy-done.4, ...), custom_call_target="tpu_custom_call" | custom-call | flops 8000000000 | bytes 1179648 | tf_op jit(solution)/shard_map/pallas_call | solution.py:209
  124.8 18.7 %all_to_all.21.refs_0_ = f32[128,9,1,128]{3,2,1,0:T(1,128)S(1)} all-to-all(f32[128,9,1,128]{3,2,1,0:T(1,128)S(1)} %shard_map.177), channel_id=1, replica_groups=mesh['base'=4,'slab'=32] {'base','slab'}, dimensions={0} | all-to-all | bytes 1179648 | tf_op jit(solution)/shard_map/all_to_all | solution.py:495
  143.4 1.8 %shard_map.178 = f32[32,4096]{1,0:T(8,128)} custom-call(f32[128,9,1,128]{3,2,1,0:T(1,128)S(1)} %all_to_all.21.refs_0_, f32[32,4096]{1,0:T(8,128)S(1)} %copy-done, f32[2,32,128]{2,1,0:T(8,128)S(1)} %copy-done.6, bf16[768,256]{1,0:T(8,128)(2,1)S(1)} %copy-done.2), custom_call_target="tpu_custom_call" | custom-call | flops 3000000000 | bytes 1048576 | tf_op jit(solution)/shard_map/pallas_call | solution.py:209
  (11 shorter events, 0.0 us)
Async XLA Ops:
  4.7 36.9 %all-to-all-start = ((f32[128,25,1,128]{3,2,1,0:T(1,128)}), f32[128,25,1,128]{3,2,1,0:T(1,128)S(1)}, u32[]{:S(2)}, u32[]{:S(2)}) async-start(f32[128,25,1,128]{3,2,1,0:T(1,128)} %shard_map.172), calls=%async_computation | async-start | bytes 3276800 | tf_op jit(solution)/shard_map/all_to_all | solution.py:495
  51.3 30.4 %all-to-all-start.1 = ((f32[4,2,8,32,128]{4,3,2,1,0:T(8,128)}), f32[4,2,8,32,128]{4,3,2,1,0:T(8,128)}, u32[]{:S(2)}, u32[]{:S(2)}) async-start(f32[4,2,8,32,128]{4,3,2,1,0:T(8,128)} %shard_map.173), calls=%async_computation.1 | async-start | bytes 2097152 | tf_op jit(solution)/shard_map/all_to_all | solution.py:495
  62.7 14.6 %collective-permute-start = (f32[2,8,32,128]{3,2,1,0:T(8,128)S(1)}, f32[2,8,32,128]{3,2,1,0:T(8,128)S(1)}, u32[]{:S(2)}, u32[]{:S(2)}) collective-permute-start(f32[2,8,32,128]{3,2,1,0:T(8,128)S(1)} %get-tuple-element.28), channel_id=1, source_target_pairs={{0,32},{32,64},{64,96},{96,0},{1,33},{33,65},{65,97},{97,1},{2,34}... | collective-permute-start | bytes 786440 | tf_op jit(solution)/shard_map/ppermute | solution.py:535
  65.4 16.3 %collective-permute-start.1 = (f32[2,8,32,128]{3,2,1,0:T(8,128)S(1)}, f32[2,8,32,128]{3,2,1,0:T(8,128)S(1)}, u32[]{:S(2)}, u32[]{:S(2)}) collective-permute-start(f32[2,8,32,128]{3,2,1,0:T(8,128)S(1)} %get-tuple-element.29), channel_id=1, source_target_pairs={{0,64},{32,96},{64,0},{96,32},{1,65},{33,97},{65,1},{97,33},{2,66}... | collective-permute-start | bytes 786440 | tf_op jit(solution)/shard_map/ppermute | solution.py:535
  66.5 15.1 %collective-permute-start.2 = (f32[2,8,32,128]{3,2,1,0:T(8,128)S(1)}, f32[2,8,32,128]{3,2,1,0:T(8,128)S(1)}, u32[]{:S(2)}, u32[]{:S(2)}) collective-permute-start(f32[2,8,32,128]{3,2,1,0:T(8,128)S(1)} %get-tuple-element.30), channel_id=1, source_target_pairs={{0,96},{32,0},{64,32},{96,64},{1,97},{33,1},{65,33},{97,65},{2,98}... | collective-permute-start | bytes 786440 | tf_op jit(solution)/shard_map/ppermute | solution.py:535
  87.3 30.9 %copy-start.1 = (bf16[256,768]{1,0:T(8,128)(2,1)S(1)}, bf16[256,768]{1,0:T(8,128)(2,1)}, u32[]{:S(2)}) copy-start(bf16[256,768]{1,0:T(8,128)(2,1)} %constant.30.clone.refs_7_.refs_1_.refs_2_) | copy-start | bytes 1179652
  87.3 30.8 %copy-start.3 = (f32[2,2,128,128]{3,2,1,0:T(8,128)S(1)}, f32[2,2,128,128]{3,2,1,0:T(8,128)}, u32[]{:S(2)}) copy-start(f32[2,2,128,128]{3,2,1,0:T(8,128)} %constant.40.clone.refs_6_) | copy-start | bytes 786436
  87.3 30.8 %copy-start.4 = (bf16[384,256]{1,0:T(8,128)(2,1)S(1)}, bf16[384,256]{1,0:T(8,128)(2,1)}, u32[]{:S(2)}) copy-start(bf16[384,256]{1,0:T(8,128)(2,1)} %constant.38.clone.refs_4_) | copy-start | bytes 589828
  87.3 30.8 %copy-start.5 = (f32[2,128,128]{2,1,0:T(8,128)S(1)}, f32[2,128,128]{2,1,0:T(8,128)}, u32[]{:S(2)}) copy-start(f32[2,128,128]{2,1,0:T(8,128)} %constant.36.clone.refs_2_.refs_3_) | copy-start | bytes 393220
  118.1 25.3 %copy-start = (f32[32,4096]{1,0:T(8,128)S(1)}, f32[32,4096]{1,0:T(8,128)}, u32[]{:S(2)}) copy-start(f32[32,4096]{1,0:T(8,128)} %refs_1_.4) | copy-start | bytes 1572868
  118.2 25.3 %copy-start.2 = (bf16[768,256]{1,0:T(8,128)(2,1)S(1)}, bf16[768,256]{1,0:T(8,128)(2,1)}, u32[]{:S(2)}) copy-start(bf16[768,256]{1,0:T(8,128)(2,1)} %constant.31.clone.refs_3_) | copy-start | bytes 1179652
  118.2 25.3 %copy-start.6 = (f32[2,32,128]{2,1,0:T(8,128)S(1)}, f32[2,32,128]{2,1,0:T(8,128)}, u32[]{:S(2)}) copy-start(f32[2,32,128]{2,1,0:T(8,128)} %constant.32.clone.refs_6_.refs_2_) | copy-start | bytes 98308

commit v6 on v5

--- a/solution.py
+++ b/solution.py
@@ -241,7 +241,8 @@
             col = jnp.where(flip == 1, 15 - col, col)
             k = count[o]
             count[o] = k + 1
-            placed.append((at, group * n_slab + row, flip * 2 + (k & 1), (col + 1).astype(f32)))
+            to = group * n_slab + (row & ~1) + flip
+            placed.append((at, to, k & 1, ((row & 1) * 16 + col + 1).astype(f32)))
         parts = [(residual[at], position[at]) for at, _, _, _ in placed]
         for (at, to, slot, tag), (value, place) in zip(placed, parts):
             for part in range(2):
@@ -259,30 +260,35 @@
     return x * x * x
 
 
-def grid_whole_kernel(first, tags, data, total, cells, order):
-    grid_into(first, 0, tags, data, total, cells, order)
-
-
-def grid_parts_kernel(first, me, tags, data, out0, out1, out2, out3, cells, order, total):
-    grid_into(first, me[0], tags, data, total, cells, order)
+def grid_whole_kernel(first, me, own, others, data, mate, total, cells, order):
+    grid_into(first, 0, me[1], own, others, data, mate, total, cells, order)
+
+
+def grid_parts_kernel(first, me, own, others, data, mate, out0, out1, out2, out3, cells, order, total):
+    grid_into(first, me[0], me[1], own, others, data, mate, total, cells, order)
     for k, out in enumerate((out0, out1, out2, out3)):
         out[...] = total[k]
 
 
-def grid_into(first, me, tags, data, total, cells, order):
-    slots, wide = tags.shape[0], total.shape[2]
+def grid_into(first, me, core, own, others, data, mate, total, cells, order):
+    first = first + 16 * core
+    slots, wide = own.shape[0], total.shape[2]
     for axis in range(2):
         at = lax.broadcasted_iota(jnp.int32, (TILE, TILE), axis).astype(f32)
         cells[2 * axis] = at * 0.25
         cells[2 * axis + 1] = (float(TILE) - at) * 0.25
     total[...] = jnp.zeros_like(total)
 
-    def scan(s, n):
-        order[n] = s
-        tag = tags[s] - first
-        return n + ((tag > 0) & (tag <= wide)).astype(jnp.int32)
-
-    n = lax.fori_loop(0, slots, scan, jnp.int32(0), unroll=8)
+    def scan(tags, begin):
+        def step(s, n):
+            order[n] = begin + s
+            tag = tags[s] - first
+            return n + ((tag > 0) & (tag <= wide)).astype(jnp.int32)
+
+        return step
+
+    n = lax.fori_loop(0, slots, scan(own, 0), jnp.int32(0), unroll=8)
+    n = lax.fori_loop(0, slots, scan(others, slots), n, unroll=8)
     for extra in range(REST):
         order[n + extra] = order[jnp.maximum(n - 1, 0)]
 
@@ -292,13 +298,18 @@
     def add(at):
         s = order[at]
         used = (at < n).astype(f32)
-        src, slot = s >> 2, s & 3
-        flip = slot >> 1
-        t = jnp.clip(tags[s] - first - 1, 0, wide - 1)
-        value_re = data[src, slot * 4] * used
-        value_im = data[src, slot * 4 + 1] * (used * (1.0 - 2.0 * flip.astype(f32)))
-        rows = taps(cells[flip] - data[src, slot * 4 + 2] * 0.25)
-        cols = taps(cells[2 + flip] - down(data[src, slot * 4 + 3] * 0.25))
+        far = (s >= slots).astype(jnp.int32)
+        s = s - far * slots
+        src, slot = s >> 1, s & 1
+        flip = (core + far) & 1
+        t = jnp.clip(jnp.where(far == 1, others[s], own[s]) - first - 1, 0, wide - 1)
+        value_re, value_im, row, col = (
+            jnp.where(far == 1, mate[src, slot * 4 + i], data[src, slot * 4 + i]) for i in range(4)
+        )
+        value_re = value_re * used
+        value_im = value_im * (used * (1.0 - 2.0 * flip.astype(f32)))
+        rows = taps(cells[flip] - row * 0.25)
+        cols = taps(cells[2 + flip] - down(col * 0.25))
         weighted = jnp.concatenate([cols * down(value_re), cols * down(value_im)], axis=1)
         sub = mm(spread(rows, LEFT[6], 1), spread(weighted, RIGHT[6], 0))
         for q in range(4):
@@ -320,7 +331,7 @@
 
 
 def cols_kernel(*refs):
-    me, whole, parts, (tw, w, w_back, out, mid) = refs[0], refs[1].ready(), refs[2:6], refs[6:]
+    me, whole, parts, (tw, w, w_back, out, mid) = refs[0], refs[1], refs[2:6], refs[6:]
     tw = tw.ready()
 
     def tile(b, ri, at):
@@ -376,10 +387,10 @@
         res = mm(w[...], part, NT)
         for k in range(2):
             for ri in range(2):
-                out[:, 16 + ri * 4 + 2 * pair + k, 0, :] = res[128 * ri : 128 * ri + 128, 128 * k : 128 * k + 128]
+                out[:, 8 + ri * 4 + 2 * pair + k, 0, :] = res[128 * ri : 128 * ri + 128, 128 * k : 128 * k + 128]
     part = spread(mid[16:20].reshape(128, 256), RIGHT[3], 1)
     res = mm(w[...], part, NT)
-    out[:, 24, 0, :] = beside(res[0:128], res[128:256]) + tags[:, 0, :]
+    out[:, 16, 0, :] = beside(res[0:128], res[128:256]) + tags[:, 0, :]
 
 
 def low_lanes():
@@ -395,11 +406,11 @@
     chunk = []
     for k in range(2):
         j = 2 * pair + k
-        re, im = field[:, 16 + j % 4, 0, :], field[:, 20 + j % 4, 0, :]
+        re, im = field[:, 8 + j % 4, 0, :], field[:, 12 + j % 4, 0, :]
         if j >= 4:
             im = -im
         if j == 4:
-            own = field[:, 24, 0, :]
+            own = field[:, 16, 0, :]
             re, im = jnp.where(low_lanes(), own, re), jnp.where(low_lanes(), pltpu.roll(own, 96, 1), im)
         chunk.append((re, im))
     return jnp.concatenate(
@@ -496,10 +507,10 @@
 
     rows, width = xi.shape
     blocks = residual.shape[0]
-    me = lax.axis_index("base").astype(jnp.int32).reshape(1)
+    me = jnp.stack([lax.axis_index("base"), lax.axis_index("slab") & 1]).astype(jnp.int32)
     packed = call(
         first_kernel,
-        (devices, 25, 1, 128),
+        (devices, 17, 1, 128),
         [SM, SM] + [VM] * 6,
         [SM((devices,), jnp.int32), VM((20, 32, 256), f32), VM((devices, 1, 128), f32)],
         2e9,
@@ -515,21 +526,22 @@
         ],
     )(owner[:, 0], tile_local, residual, position, xi, amplitude, t["tw_row"], t["w128"])
     data = exchange(packed, everywhere)
-    tags = data[:, 24, 0, 64:68].reshape(4 * devices).astype(jnp.int32)
+    mate = lax.ppermute(data, "slab", [(i, i ^ 1) for i in range(n_slab)])
+    tags = tuple(a[:, 16, 0, 64:66].reshape(2 * devices).astype(jnp.int32) for a in (data, mate))
     spare = [VM((4, TILE, TILE), f32), SM((4 * devices + REST,), jnp.int32)]
     shape = (2, 8, 32, 128)
     whole = call(
-        functools.partial(grid_whole_kernel, 0), (n_base, *shape), [SM, VM], spare, 2e10
-    )(tags, data)
+        functools.partial(grid_whole_kernel, 0), (n_base, *shape), [SM, SM, SM, VM, VM], spare, 2e10
+    )(me, *tags, data, mate)
     whole, tags = lax.optimization_barrier((whole, tags))
     whole = exchange(whole, "base")
     parts = call(
         functools.partial(grid_parts_kernel, 8),
         [shape] * n_base,
-        [SM, SM, VM],
+        [SM, SM, SM, VM, VM],
         [*spare, VM((n_base, *shape), f32)],
         2e10,
-    )(me, tags, data)
+    )(me, *tags, data, mate)
     parts, field = lax.optimization_barrier((parts, data))
     parts = [parts[0]] + [
         lax.ppermute(parts[k], "base", [(i, (i + k) % n_base) for i in range(n_base)]) for k in range(1, n_base)
@@ -551,7 +563,6 @@
         [VM((64, 32, 256), f32)],
         4e9,
         [
-            (1, VM((n_base, *shape), f32)),
             (6, VM((n_base, 2, 64, 128), f32)),
             (7, VM((128, 1536), bf16)),
             (8, VM((128, 1536), bf16)),

time: 146 us -> 138 us (0.945)
  waiting for transfers between devices: 35.3 us -> 11.1 us
  blocking collectives: 49.5 us -> 72.9 us
  starting transfers between devices: 21.2 us -> 7.42 us
  Pallas kernels: 38.8 us -> 45.7 us
    all_to_all x2 -> x1, waiting for transfers between devices: 25.4 us -> 0.01 us  [exchange(): return lax.all_to_all(a, axis, split_axis=0, concat_axis=0, tiled=True)]
    all_to_all x2 -> x3, blocking collectives: 49.5 us -> 72.9 us  [exchange(): return lax.all_to_all(a, axis, split_axis=0, concat_axis=0, tiled=True)]
    all_to_all x2 -> x1, starting transfers between devices: 15.7 us -> 3.51 us  [exchange(): return lax.all_to_all(a, axis, split_axis=0, concat_axis=0, tiled=True)]
    pallas_call x7, Pallas kernels: 38.8 us -> 45.7 us  [placed(): results = got(*arrays)]
    ppermute x3, starting transfers between devices: 5.47 us -> 2.74 us  [per_device(): lax.ppermute(parts[k], 'base', [(i, (i + k) % n_base) for i in range(n_ba...]
    ppermute x0 -> x1, waiting for transfers between devices: none -> 1.9 us  [per_device(): mate = lax.ppermute(data, 'slab', [(i, i ^ 1) for i in range(n_slab)])]
  transfers between devices with their start and end apart: 5 -> 5, of which waited for: 3 -> 3; matrix products, arithmetic and copies ran while one was open for 0% -> 0% of each run, Pallas kernels for 7% -> 11%
where the time goes in v6:
time: 138 us
  blocking collectives  72.9 us (53%)
  Pallas kernels  45.7 us (33%)
  waiting for transfers between devices  11.1 us (8%)
  starting transfers between devices  7.42 us (5%)
    all_to_all x3, blocking collectives, exchange(): return lax.all_to_all(a, axis, split_axis=0, concat_axis=0, tiled=True)  72.9 us
    pallas_call x7, Pallas kernels, placed(): results = got(*arrays)  45.7 us
    ppermute x3, waiting for transfers between devices, per_device(): lax.ppermute(parts[k], 'base', [(i, (i + k) % n_base) for i in range(n_ba...  9.19 us
    all_to_all x1, starting transfers between devices, exchange(): return lax.all_to_all(a, axis, split_axis=0, concat_axis=0, tiled=True)  3.51 us
  transfers between devices with their start and end apart: 5, of which 3 were waited for; matrix products, arithmetic and copies ran while one was open for 0% of the time, Pallas kernels for 11%

profile of v6, /device:TPU:1, one launch (start us, length us, event | category | flops | bytes accessed | tf_op | source)
XLA Modules:
  0.0 138.1 jit_solution(12513516039797154683)
XLA Ops:
  0.0 3.7 %shard_map.172 = f32[128,17,1,128]{3,2,1,0:T(1,128)S(1)} custom-call(s32[128]{0:T(128)} %bitcast.5, s32[128]{0:T(128)} %refs_1_.3, f32[128,2,128]{2,1,0:T(2,128)} %refs_2_.4, f32[128,2,128]{2,1,0:T(2,128)} %refs_3_.4, f32[32,4096]{1,0:T(8,128)} %refs_4_.2, f32[32,4096]{1,0:T(8,128)} %refs_1_.4, f32[2,32,128]{2,1,0:T(8,128)} %constant.37.clone.refs_6_.refs_2_, ...), custom_call_target="tpu_custom_call" | custom-call | flops 2000000000 | bytes 2228224 | tf_op jit(solution)/shard_map/pallas_call | solution.py:209
  3.7 31.1 %all_to_all.20.refs_3_.refs_0_ = f32[128,17,1,128]{3,2,1,0:T(1,128)S(1)} all-to-all(f32[128,17,1,128]{3,2,1,0:T(1,128)S(1)} %shard_map.172), channel_id=1, replica_groups=mesh['base'=4,'slab'=32] {'base','slab'}, dimensions={0} | all-to-all | bytes 2228224 | tf_op jit(solution)/shard_map/all_to_all | solution.py:506
  34.8 1.2 collective-permute-start
  35.9 0.1 pad_add_fusion.refs_0_
  36.0 0.3 fusion.1
  36.3 0.1 convert_element_type.11.refs_1_
  36.4 1.9 %collective-permute-done.refs_4_ = f32[128,17,1,128]{3,2,1,0:T(1,128)S(1)} collective-permute-done((f32[128,17,1,128]{3,2,1,0:T(1,128)S(1)}, f32[128,17,1,128]{3,2,1,0:T(1,128)S(1)}, u32[]{:S(2)}, u32[]{:S(2)}) %collective-permute-start) | collective-permute-done | bytes 1114144 | tf_op jit(solution)/shard_map/ppermute | solution.py:529
  38.3 0.3 fusion
  38.6 0.1 convert_element_type.13.refs_2_
  38.7 12.5 %shard_map.173 = f32[4,2,8,32,128]{4,3,2,1,0:T(8,128)} custom-call(s32[2]{0:T(128)S(1)} %pad_add_fusion.refs_0_, s32[256]{0:T(256)S(1)} %convert_element_type.11.refs_1_, s32[256]{0:T(256)S(1)} %convert_element_type.13.refs_2_, f32[128,17,1,128]{3,2,1,0:T(1,128)S(1)} %all_to_all.20.refs_3_.refs_0_, f32[128,17,1,128]{3,2,1,0:T(1,128)S(1)} %collective-permute-done.refs_4_), custom_call_target="tpu_custom_call" | custom-call | flops 20000000000 | bytes 2097152 | tf_op jit(solution)/shard_map/pallas_call | solution.py:209
  51.2 3.5 %all-to-all-start.1 = ((f32[4,2,8,32,128]{4,3,2,1,0:T(8,128)}), f32[4,2,8,32,128]{4,3,2,1,0:T(8,128)S(1)}, u32[]{:S(2)}, u32[]{:S(2)}) async-start(f32[4,2,8,32,128]{4,3,2,1,0:T(8,128)} %shard_map.173), calls=%async_computation.1 | async-start | bytes 2097152 | tf_op jit(solution)/shard_map/all_to_all | solution.py:506
  54.8 11.6 %shard_map.174 = (f32[2,8,32,128]{3,2,1,0:T(8,128)S(1)}, f32[2,8,32,128]{3,2,1,0:T(8,128)S(1)}, f32[2,8,32,128]{3,2,1,0:T(8,128)S(1)}, f32[2,8,32,128]{3,2,1,0:T(8,128)S(1)}) custom-call(s32[2]{0:T(128)S(1)} %pad_add_fusion.refs_0_, s32[256]{0:T(256)S(1)} %convert_element_type.11.refs_1_, s32[256]{0:T(256)S(1)} %convert_element_type.13.refs_2_, ...), custom_call_target="tpu_custom_call" | custom-call | flops 20000000000 | bytes 2097152 | tf_op jit(solution)/shard_map/pallas_call | solution.py:209
  66.4 0.1 collective-permute-start.1
  66.5 0.8 collective-permute-start.2
  67.3 1.9 %collective-permute-start.3 = (f32[2,8,32,128]{3,2,1,0:T(8,128)S(1)}, f32[2,8,32,128]{3,2,1,0:T(8,128)S(1)}, u32[]{:S(2)}, u32[]{:S(2)}) collective-permute-start(f32[2,8,32,128]{3,2,1,0:T(8,128)S(1)} %get-tuple-element.32), channel_id=1, source_target_pairs={{0,96},{32,0},{64,32},{96,64},{1,97},{33,1},{65,33},{97,65},{2,98}... | collective-permute-start | bytes 786440 | tf_op jit(solution)/shard_map/ppermute | solution.py:547
  69.2 3.7 %shard_map.175.refs_0_ = f32[4,256,128]{2,1,0:T(8,128)} custom-call(f32[128,17,1,128]{3,2,1,0:T(1,128)S(1)} %all_to_all.20.refs_3_.refs_0_, bf16[256,768]{1,0:T(8,128)(2,1)} %constant.35.clone.refs_7_.refs_1_.refs_2_, f32[2,128,128]{2,1,0:T(8,128)} %constant.41.clone.refs_2_.refs_3_, bf16[768,128]{1,0:T(8,128)(2,1)} %constant.42.clone.refs_3_), custom_call_target="tpu_custom_call" | custom-call | flops 4000000000 | bytes 1048576 | tf_op jit(solution)/shard_map/pallas_call | solution.py:209
  72.8 9.1 %collective-permute-done.1.refs_3_ = f32[2,8,32,128]{3,2,1,0:T(8,128)S(1)} collective-permute-done((f32[2,8,32,128]{3,2,1,0:T(8,128)S(1)}, f32[2,8,32,128]{3,2,1,0:T(8,128)S(1)}, u32[]{:S(2)}, u32[]{:S(2)}) %collective-permute-start.1) | collective-permute-done | bytes 262176 | tf_op jit(solution)/shard_map/ppermute | solution.py:547
  82.0 0.1 collective-permute-done.3.refs_5_
  82.0 5.8 %shard_map.176 = f32[64,2,16,128]{3,2,1,0:T(8,128)S(1)} custom-call(s32[2]{0:T(128)S(1)} %pad_add_fusion.refs_0_, f32[4,2,8,32,128]{4,3,2,1,0:T(8,128)S(1)} %all-to-all-done.1.refs_1_, f32[2,8,32,128]{3,2,1,0:T(8,128)S(1)} %get-tuple-element.29.refs_2_, f32[2,8,32,128]{3,2,1,0:T(8,128)S(1)} %collective-permute-done.1.refs_3_, ...), custom_call_target="tpu_custom_call" | custom-call | flops 4000000000 | bytes 2097152 | tf_op jit(solution)/shard_map/pallas_call | solution.py:209
  87.8 0.0 copy-start.1
  87.9 23.1 %all_to_all.21.refs_1_ = f32[128,16,128]{2,1,0:T(8,128)S(1)} all-to-all(f32[128,16,128]{2,1,0:T(8,128)S(1)} %bitcast.4), channel_id=1, replica_groups=mesh['base'=4,'slab'=32] {'base','slab'}, dimensions={0} | all-to-all | bytes 2097152 | tf_op jit(solution)/shard_map/all_to_all | solution.py:506
  111.1 6.5 %shard_map.177 = f32[128,9,1,128]{3,2,1,0:T(1,128)S(1)} custom-call(f32[4,256,128]{2,1,0:T(8,128)} %shard_map.175.refs_0_, f32[128,16,128]{2,1,0:T(8,128)S(1)} %all_to_all.21.refs_1_, bf16[256,768]{1,0:T(8,128)(2,1)S(1)} %copy-done.1, f32[2,128,128]{2,1,0:T(8,128)S(1)} %copy-done.5, bf16[384,256]{1,0:T(8,128)(2,1)S(1)} %copy-done.4, ...), custom_call_target="tpu_custom_call" | custom-call | flops 8000000000 | bytes 1179648 | tf_op jit(solution)/shard_map/pallas_call | solution.py:209
  117.6 18.7 %all_to_all.22.refs_0_ = f32[128,9,1,128]{3,2,1,0:T(1,128)S(1)} all-to-all(f32[128,9,1,128]{3,2,1,0:T(1,128)S(1)} %shard_map.177), channel_id=1, replica_groups=mesh['base'=4,'slab'=32] {'base','slab'}, dimensions={0} | all-to-all | bytes 1179648 | tf_op jit(solution)/shard_map/all_to_all | solution.py:506
  136.3 1.8 %shard_map.178 = f32[32,4096]{1,0:T(8,128)} custom-call(f32[128,9,1,128]{3,2,1,0:T(1,128)S(1)} %all_to_all.22.refs_0_, f32[32,4096]{1,0:T(8,128)S(1)} %copy-done, f32[2,32,128]{2,1,0:T(8,128)S(1)} %copy-done.6, bf16[768,256]{1,0:T(8,128)(2,1)S(1)} %copy-done.2), custom_call_target="tpu_custom_call" | custom-call | flops 3000000000 | bytes 1048576 | tf_op jit(solution)/shard_map/pallas_call | solution.py:209
  (15 shorter events, 0.0 us)
Async XLA Ops:
  34.8 3.5 %collective-permute-start = (f32[128,17,1,128]{3,2,1,0:T(1,128)S(1)}, f32[128,17,1,128]{3,2,1,0:T(1,128)S(1)}, u32[]{:S(2)}, u32[]{:S(2)}) collective-permute-start(f32[128,17,1,128]{3,2,1,0:T(1,128)S(1)} %all_to_all.20.refs_3_.refs_0_), channel_id=1, source_target_pairs={{0,1},{1,0},{2,3},{3,2},{4,5},{5,4},{6,7},{7,6},{8,9},{9,8},{10,11... | collective-permute-start | bytes 3342344 | tf_op jit(solution)/shard_map/ppermute | solution.py:529
  51.2 30.8 %all-to-all-start.1 = ((f32[4,2,8,32,128]{4,3,2,1,0:T(8,128)}), f32[4,2,8,32,128]{4,3,2,1,0:T(8,128)S(1)}, u32[]{:S(2)}, u32[]{:S(2)}) async-start(f32[4,2,8,32,128]{4,3,2,1,0:T(8,128)} %shard_map.173), calls=%async_computation.1 | async-start | bytes 2097152 | tf_op jit(solution)/shard_map/all_to_all | solution.py:506
  66.4 15.6 %collective-permute-start.1 = (f32[2,8,32,128]{3,2,1,0:T(8,128)S(1)}, f32[2,8,32,128]{3,2,1,0:T(8,128)S(1)}, u32[]{:S(2)}, u32[]{:S(2)}) collective-permute-start(f32[2,8,32,128]{3,2,1,0:T(8,128)S(1)} %get-tuple-element.30), channel_id=1, source_target_pairs={{0,32},{32,64},{64,96},{96,0},{1,33},{33,65},{65,97},{97,1},{2,34}... | collective-permute-start | bytes 786440 | tf_op jit(solution)/shard_map/ppermute | solution.py:547
  66.5 15.5 %collective-permute-start.2 = (f32[2,8,32,128]{3,2,1,0:T(8,128)S(1)}, f32[2,8,32,128]{3,2,1,0:T(8,128)S(1)}, u32[]{:S(2)}, u32[]{:S(2)}) collective-permute-start(f32[2,8,32,128]{3,2,1,0:T(8,128)S(1)} %get-tuple-element.31), channel_id=1, source_target_pairs={{0,64},{32,96},{64,0},{96,32},{1,65},{33,97},{65,1},{97,33},{2,66}... | collective-permute-start | bytes 786440 | tf_op jit(solution)/shard_map/ppermute | solution.py:547
  67.3 14.7 %collective-permute-start.3 = (f32[2,8,32,128]{3,2,1,0:T(8,128)S(1)}, f32[2,8,32,128]{3,2,1,0:T(8,128)S(1)}, u32[]{:S(2)}, u32[]{:S(2)}) collective-permute-start(f32[2,8,32,128]{3,2,1,0:T(8,128)S(1)} %get-tuple-element.32), channel_id=1, source_target_pairs={{0,96},{32,0},{64,32},{96,64},{1,97},{33,1},{65,33},{97,65},{2,98}... | collective-permute-start | bytes 786440 | tf_op jit(solution)/shard_map/ppermute | solution.py:547
  87.8 23.2 %copy-start.1 = (bf16[256,768]{1,0:T(8,128)(2,1)S(1)}, bf16[256,768]{1,0:T(8,128)(2,1)}, u32[]{:S(2)}) copy-start(bf16[256,768]{1,0:T(8,128)(2,1)} %constant.35.clone.refs_7_.refs_1_.refs_2_) | copy-start | bytes 1179652
  87.9 23.2 %copy-start.3 = (f32[2,2,128,128]{3,2,1,0:T(8,128)S(1)}, f32[2,2,128,128]{3,2,1,0:T(8,128)}, u32[]{:S(2)}) copy-start(f32[2,2,128,128]{3,2,1,0:T(8,128)} %constant.45.clone.refs_6_) | copy-start | bytes 786436
  87.9 23.2 %copy-start.4 = (bf16[384,256]{1,0:T(8,128)(2,1)S(1)}, bf16[384,256]{1,0:T(8,128)(2,1)}, u32[]{:S(2)}) copy-start(bf16[384,256]{1,0:T(8,128)(2,1)} %constant.43.clone.refs_4_) | copy-start | bytes 589828
  87.9 23.2 %copy-start.5 = (f32[2,128,128]{2,1,0:T(8,128)S(1)}, f32[2,128,128]{2,1,0:T(8,128)}, u32[]{:S(2)}) copy-start(f32[2,128,128]{2,1,0:T(8,128)} %constant.41.clone.refs_2_.refs_3_) | copy-start | bytes 393220
  117.6 18.7 %copy-start = (f32[32,4096]{1,0:T(8,128)S(1)}, f32[32,4096]{1,0:T(8,128)}, u32[]{:S(2)}) copy-start(f32[32,4096]{1,0:T(8,128)} %refs_1_.4) | copy-start | bytes 1572868
  117.6 18.7 %copy-start.2 = (bf16[768,256]{1,0:T(8,128)(2,1)S(1)}, bf16[768,256]{1,0:T(8,128)(2,1)}, u32[]{:S(2)}) copy-start(bf16[768,256]{1,0:T(8,128)(2,1)} %constant.36.clone.refs_3_) | copy-start | bytes 1179652
  117.6 18.7 %copy-start.6 = (f32[2,32,128]{2,1,0:T(8,128)S(1)}, f32[2,32,128]{2,1,0:T(8,128)}, u32[]{:S(2)}) copy-start(f32[2,32,128]{2,1,0:T(8,128)} %constant.37.clone.refs_6_.refs_2_) | copy-start | bytes 98308

commit v7 on v6

--- a/solution.py
+++ b/solution.py
@@ -15,6 +15,7 @@
 TILE = 128
 GROUP = 24
 REST = 8
+CUT = 10
 GRANT = 20 * 2**20
 
 NN = (((1,), (0,)), ((), ()))
@@ -332,13 +333,14 @@
 
 def cols_kernel(*refs):
     me, whole, parts, (tw, w, w_back, out, mid) = refs[0], refs[1], refs[2:6], refs[6:]
+    parts = (parts[0].ready(), *parts[1:])
     tw = tw.ready()
 
     def tile(b, ri, at):
         group = b // 16
-        if b % 16 < 8:
-            return whole[(me[0] + group) & 3, ri, b % 8, at, :]
-        return parts[-group % 4][ri, b % 8, at, :]
+        if b % 16 < CUT:
+            return whole[(me[0] + group) & 3, ri, b % 16, at, :]
+        return parts[-group % 4][ri, b % 16 - CUT, at, :]
 
     def rows(i, _):
         at = pl.ds(pl.multiple_of(i * 8, 8), 8)
@@ -529,14 +531,14 @@
     mate = lax.ppermute(data, "slab", [(i, i ^ 1) for i in range(n_slab)])
     tags = tuple(a[:, 16, 0, 64:66].reshape(2 * devices).astype(jnp.int32) for a in (data, mate))
     spare = [VM((4, TILE, TILE), f32), SM((4 * devices + REST,), jnp.int32)]
-    shape = (2, 8, 32, 128)
     whole = call(
-        functools.partial(grid_whole_kernel, 0), (n_base, *shape), [SM, SM, SM, VM, VM], spare, 2e10
+        functools.partial(grid_whole_kernel, 0), (n_base, 2, CUT, 32, 128), [SM, SM, SM, VM, VM], spare, 2e10
     )(me, *tags, data, mate)
     whole, tags = lax.optimization_barrier((whole, tags))
     whole = exchange(whole, "base")
+    shape = (2, 16 - CUT, 32, 128)
     parts = call(
-        functools.partial(grid_parts_kernel, 8),
+        functools.partial(grid_parts_kernel, CUT),
         [shape] * n_base,
         [SM, SM, SM, VM, VM],
         [*spare, VM((n_base, *shape), f32)],
@@ -563,6 +565,7 @@
         [VM((64, 32, 256), f32)],
         4e9,
         [
+            (2, VM(shape, f32)),
             (6, VM((n_base, 2, 64, 128), f32)),
             (7, VM((128, 1536), bf16)),
             (8, VM((128, 1536), bf16)),

time: 138 us -> 140 us (1.014); the launches traced: 138 us -> 138 us
  starting transfers between devices: 7.42 us -> 12.8 us
  Pallas kernels: 45.7 us -> 40.7 us
  waiting for transfers between devices: 11.1 us -> 9.42 us
    pallas_call x7, Pallas kernels: 45.7 us -> 40.7 us  [placed(): results = got(*arrays)]
    ppermute x3, starting transfers between devices: 2.74 us -> 7.71 us  [per_device(): lax.ppermute(parts[k], 'base', [(i, (i + k) % n_base) for i in range(n_ba...]
    ppermute x3, waiting for transfers between devices: 9.19 us -> 7.52 us  [per_device(): lax.ppermute(parts[k], 'base', [(i, (i + k) % n_base) for i in range(n_ba...]
  transfers between devices with their start and end apart: 5 -> 5, of which waited for: 3 -> 3; matrix products, arithmetic and copies ran while one was open for 0% -> 0% of each run, Pallas kernels for 11% -> 7%
where the time goes in v7:
time: 140 us; the launch traced here: 138 us
  blocking collectives  73.9 us (53%)
  Pallas kernels  40.7 us (29%)
  starting transfers between devices  12.8 us (9%)
  waiting for transfers between devices  9.42 us (7%)
    all_to_all x3, blocking collectives, exchange(): return lax.all_to_all(a, axis, split_axis=0, concat_axis=0, tiled=True)  73.9 us
    pallas_call x7, Pallas kernels, placed(): results = got(*arrays)  40.7 us
    ppermute x3, starting transfers between devices, per_device(): lax.ppermute(parts[k], 'base', [(i, (i + k) % n_base) for i in range(n_ba...  7.71 us
    ppermute x3, waiting for transfers between devices, per_device(): lax.ppermute(parts[k], 'base', [(i, (i + k) % n_base) for i in range(n_ba...  7.52 us
    all_to_all x1, starting transfers between devices, exchange(): return lax.all_to_all(a, axis, split_axis=0, concat_axis=0, tiled=True)  3.97 us
  transfers between devices with their start and end apart: 5, of which 3 were waited for; matrix products, arithmetic and copies ran while one was open for 0% of the time, Pallas kernels for 7%

profile of v7, /device:TPU:1, one launch (start us, length us, event | category | flops | bytes accessed | tf_op | source)
XLA Modules:
  0.0 137.9 jit_solution(2385906724762812627)
XLA Ops:
  0.0 3.7 %shard_map.172 = f32[128,17,1,128]{3,2,1,0:T(1,128)S(1)} custom-call(s32[128]{0:T(128)} %bitcast.5, s32[128]{0:T(128)} %refs_1_.3, f32[128,2,128]{2,1,0:T(2,128)} %refs_2_.4, f32[128,2,128]{2,1,0:T(2,128)} %refs_3_.4, f32[32,4096]{1,0:T(8,128)} %refs_4_.2, f32[32,4096]{1,0:T(8,128)} %refs_1_.4, f32[2,32,128]{2,1,0:T(8,128)} %constant.37.clone.refs_6_.refs_2_, ...), custom_call_target="tpu_custom_call" | custom-call | flops 2000000000 | bytes 2228224 | tf_op jit(solution)/shard_map/pallas_call | solution.py:210
  3.7 31.1 %all_to_all.20.refs_3_.refs_0_ = f32[128,17,1,128]{3,2,1,0:T(1,128)S(1)} all-to-all(f32[128,17,1,128]{3,2,1,0:T(1,128)S(1)} %shard_map.172), channel_id=1, replica_groups=mesh['base'=4,'slab'=32] {'base','slab'}, dimensions={0} | all-to-all | bytes 2228224 | tf_op jit(solution)/shard_map/all_to_all | solution.py:508
  34.8 1.2 collective-permute-start
  35.9 0.1 pad_add_fusion.refs_0_
  36.0 0.3 fusion.1
  36.3 0.1 convert_element_type.11.refs_1_
  36.4 1.9 %collective-permute-done.refs_4_ = f32[128,17,1,128]{3,2,1,0:T(1,128)S(1)} collective-permute-done((f32[128,17,1,128]{3,2,1,0:T(1,128)S(1)}, f32[128,17,1,128]{3,2,1,0:T(1,128)S(1)}, u32[]{:S(2)}, u32[]{:S(2)}) %collective-permute-start) | collective-permute-done | bytes 1114144 | tf_op jit(solution)/shard_map/ppermute | solution.py:531
  38.3 0.3 fusion
  38.6 0.1 convert_element_type.13.refs_2_
  38.7 12.7 %shard_map.173 = f32[4,2,10,32,128]{4,3,2,1,0:T(8,128)} custom-call(s32[2]{0:T(128)S(1)} %pad_add_fusion.refs_0_, s32[256]{0:T(256)S(1)} %convert_element_type.11.refs_1_, s32[256]{0:T(256)S(1)} %convert_element_type.13.refs_2_, f32[128,17,1,128]{3,2,1,0:T(1,128)S(1)} %all_to_all.20.refs_3_.refs_0_, f32[128,17,1,128]{3,2,1,0:T(1,128)S(1)} %collective-permute-done.refs_4_), custom_call_target="tpu_custom_call" | custom-call | flops 20000000000 | bytes 2621440 | tf_op jit(solution)/shard_map/pallas_call | solution.py:210
  51.4 4.0 %all-to-all-start.1 = ((f32[4,2,10,32,128]{4,3,2,1,0:T(8,128)}), f32[4,2,10,32,128]{4,3,2,1,0:T(8,128)S(1)}, u32[]{:S(2)}, u32[]{:S(2)}) async-start(f32[4,2,10,32,128]{4,3,2,1,0:T(8,128)} %shard_map.173), calls=%async_computation.1 | async-start | bytes 2621440 | tf_op jit(solution)/shard_map/all_to_all | solution.py:508
  55.3 6.4 %shard_map.174 = (f32[2,6,32,128]{3,2,1,0:T(8,128)S(1)}, f32[2,6,32,128]{3,2,1,0:T(8,128)S(1)}, f32[2,6,32,128]{3,2,1,0:T(8,128)S(1)}, f32[2,6,32,128]{3,2,1,0:T(8,128)S(1)}) custom-call(s32[2]{0:T(128)S(1)} %pad_add_fusion.refs_0_, s32[256]{0:T(256)S(1)} %convert_element_type.11.refs_1_, s32[256]{0:T(256)S(1)} %convert_element_type.13.refs_2_, ...), custom_call_target="tpu_custom_call" | custom-call | flops 20000000000 | bytes 1572864 | tf_op jit(solution)/shard_map/pallas_call | solution.py:210
  61.8 5.1 %collective-permute-start.1 = (f32[2,6,32,128]{3,2,1,0:T(8,128)S(1)}, f32[2,6,32,128]{3,2,1,0:T(8,128)S(1)}, u32[]{:S(2)}, u32[]{:S(2)}) collective-permute-start(f32[2,6,32,128]{3,2,1,0:T(8,128)S(1)} %get-tuple-element.30), channel_id=1, source_target_pairs={{0,32},{32,64},{64,96},{96,0},{1,33},{33,65},{65,97},{97,1},{2,34}... | collective-permute-start | bytes 589832 | tf_op jit(solution)/shard_map/ppermute | solution.py:549
  66.9 0.6 collective-permute-start.2
  67.5 2.0 %collective-permute-start.3 = (f32[2,6,32,128]{3,2,1,0:T(8,128)S(1)}, f32[2,6,32,128]{3,2,1,0:T(8,128)S(1)}, u32[]{:S(2)}, u32[]{:S(2)}) collective-permute-start(f32[2,6,32,128]{3,2,1,0:T(8,128)S(1)} %get-tuple-element.32), channel_id=1, source_target_pairs={{0,96},{32,0},{64,32},{96,64},{1,97},{33,1},{65,33},{97,65},{2,98}... | collective-permute-start | bytes 589832 | tf_op jit(solution)/shard_map/ppermute | solution.py:549
  69.5 3.7 %shard_map.175.refs_0_ = f32[4,256,128]{2,1,0:T(8,128)} custom-call(f32[128,17,1,128]{3,2,1,0:T(1,128)S(1)} %all_to_all.20.refs_3_.refs_0_, bf16[256,768]{1,0:T(8,128)(2,1)} %constant.35.clone.refs_7_.refs_1_.refs_2_, f32[2,128,128]{2,1,0:T(8,128)} %constant.41.clone.refs_2_.refs_3_, bf16[768,128]{1,0:T(8,128)(2,1)} %constant.42.clone.refs_3_), custom_call_target="tpu_custom_call" | custom-call | flops 4000000000 | bytes 1048576 | tf_op jit(solution)/shard_map/pallas_call | solution.py:210
  73.1 3.9 %collective-permute-done.1.refs_3_ = f32[2,6,32,128]{3,2,1,0:T(8,128)S(1)} collective-permute-done((f32[2,6,32,128]{3,2,1,0:T(8,128)S(1)}, f32[2,6,32,128]{3,2,1,0:T(8,128)S(1)}, u32[]{:S(2)}, u32[]{:S(2)}) %collective-permute-start.1) | collective-permute-done | bytes 196640 | tf_op jit(solution)/shard_map/ppermute | solution.py:549
  77.1 3.6 %collective-permute-done.2.refs_4_ = f32[2,6,32,128]{3,2,1,0:T(8,128)S(1)} collective-permute-done((f32[2,6,32,128]{3,2,1,0:T(8,128)S(1)}, f32[2,6,32,128]{3,2,1,0:T(8,128)S(1)}, u32[]{:S(2)}, u32[]{:S(2)}) %collective-permute-start.2) | collective-permute-done | bytes 196640 | tf_op jit(solution)/shard_map/ppermute | solution.py:549
  80.7 5.9 %shard_map.176 = f32[64,2,16,128]{3,2,1,0:T(8,128)S(1)} custom-call(s32[2]{0:T(128)S(1)} %pad_add_fusion.refs_0_, f32[4,2,10,32,128]{4,3,2,1,0:T(8,128)S(1)} %all-to-all-done.1.refs_1_, f32[2,6,32,128]{3,2,1,0:T(8,128)} %copy-done.7, f32[2,6,32,128]{3,2,1,0:T(8,128)S(1)} %collective-permute-done.1.refs_3_, ...), custom_call_target="tpu_custom_call" | custom-call | flops 4000000000 | bytes 2097152 | tf_op jit(solution)/shard_map/pallas_call | solution.py:210
  86.6 0.0 copy-start.1
  86.7 24.1 %all_to_all.21.refs_1_ = f32[128,16,128]{2,1,0:T(8,128)S(1)} all-to-all(f32[128,16,128]{2,1,0:T(8,128)S(1)} %bitcast.4), channel_id=1, replica_groups=mesh['base'=4,'slab'=32] {'base','slab'}, dimensions={0} | all-to-all | bytes 2097152 | tf_op jit(solution)/shard_map/all_to_all | solution.py:508
  110.8 6.5 %shard_map.177 = f32[128,9,1,128]{3,2,1,0:T(1,128)S(1)} custom-call(f32[4,256,128]{2,1,0:T(8,128)} %shard_map.175.refs_0_, f32[128,16,128]{2,1,0:T(8,128)S(1)} %all_to_all.21.refs_1_, bf16[256,768]{1,0:T(8,128)(2,1)S(1)} %copy-done.1, f32[2,128,128]{2,1,0:T(8,128)S(1)} %copy-done.5, bf16[384,256]{1,0:T(8,128)(2,1)S(1)} %copy-done.4, ...), custom_call_target="tpu_custom_call" | custom-call | flops 8000000000 | bytes 1179648 | tf_op jit(solution)/shard_map/pallas_call | solution.py:210
  117.4 18.7 %all_to_all.22.refs_0_ = f32[128,9,1,128]{3,2,1,0:T(1,128)S(1)} all-to-all(f32[128,9,1,128]{3,2,1,0:T(1,128)S(1)} %shard_map.177), channel_id=1, replica_groups=mesh['base'=4,'slab'=32] {'base','slab'}, dimensions={0} | all-to-all | bytes 1179648 | tf_op jit(solution)/shard_map/all_to_all | solution.py:508
  136.1 1.9 %shard_map.178 = f32[32,4096]{1,0:T(8,128)} custom-call(f32[128,9,1,128]{3,2,1,0:T(1,128)S(1)} %all_to_all.22.refs_0_, f32[32,4096]{1,0:T(8,128)S(1)} %copy-done, f32[2,32,128]{2,1,0:T(8,128)S(1)} %copy-done.6, bf16[768,256]{1,0:T(8,128)(2,1)S(1)} %copy-done.2), custom_call_target="tpu_custom_call" | custom-call | flops 3000000000 | bytes 1048576 | tf_op jit(solution)/shard_map/pallas_call | solution.py:210
  (17 shorter events, 0.1 us)
Async XLA Ops:
  34.8 3.5 %collective-permute-start = (f32[128,17,1,128]{3,2,1,0:T(1,128)S(1)}, f32[128,17,1,128]{3,2,1,0:T(1,128)S(1)}, u32[]{:S(2)}, u32[]{:S(2)}) collective-permute-start(f32[128,17,1,128]{3,2,1,0:T(1,128)S(1)} %all_to_all.20.refs_3_.refs_0_), channel_id=1, source_target_pairs={{0,1},{1,0},{2,3},{3,2},{4,5},{5,4},{6,7},{7,6},{8,9},{9,8},{10,11... | collective-permute-start | bytes 3342344 | tf_op jit(solution)/shard_map/ppermute | solution.py:531
  51.4 29.3 %all-to-all-start.1 = ((f32[4,2,10,32,128]{4,3,2,1,0:T(8,128)}), f32[4,2,10,32,128]{4,3,2,1,0:T(8,128)S(1)}, u32[]{:S(2)}, u32[]{:S(2)}) async-start(f32[4,2,10,32,128]{4,3,2,1,0:T(8,128)} %shard_map.173), calls=%async_computation.1 | async-start | bytes 2621440 | tf_op jit(solution)/shard_map/all_to_all | solution.py:508
  61.8 11.4 %copy-start.7 = (f32[2,6,32,128]{3,2,1,0:T(8,128)}, f32[2,6,32,128]{3,2,1,0:T(8,128)S(1)}, u32[]{:S(2)}) copy-start(f32[2,6,32,128]{3,2,1,0:T(8,128)S(1)} %get-tuple-element.29.refs_2_) | copy-start | bytes 589828
  61.8 15.3 %collective-permute-start.1 = (f32[2,6,32,128]{3,2,1,0:T(8,128)S(1)}, f32[2,6,32,128]{3,2,1,0:T(8,128)S(1)}, u32[]{:S(2)}, u32[]{:S(2)}) collective-permute-start(f32[2,6,32,128]{3,2,1,0:T(8,128)S(1)} %get-tuple-element.30), channel_id=1, source_target_pairs={{0,32},{32,64},{64,96},{96,0},{1,33},{33,65},{65,97},{97,1},{2,34}... | collective-permute-start | bytes 589832 | tf_op jit(solution)/shard_map/ppermute | solution.py:549
  66.9 13.8 %collective-permute-start.2 = (f32[2,6,32,128]{3,2,1,0:T(8,128)S(1)}, f32[2,6,32,128]{3,2,1,0:T(8,128)S(1)}, u32[]{:S(2)}, u32[]{:S(2)}) collective-permute-start(f32[2,6,32,128]{3,2,1,0:T(8,128)S(1)} %get-tuple-element.31), channel_id=1, source_target_pairs={{0,64},{32,96},{64,0},{96,32},{1,65},{33,97},{65,1},{97,33},{2,66}... | collective-permute-start | bytes 589832 | tf_op jit(solution)/shard_map/ppermute | solution.py:549
  67.5 13.2 %collective-permute-start.3 = (f32[2,6,32,128]{3,2,1,0:T(8,128)S(1)}, f32[2,6,32,128]{3,2,1,0:T(8,128)S(1)}, u32[]{:S(2)}, u32[]{:S(2)}) collective-permute-start(f32[2,6,32,128]{3,2,1,0:T(8,128)S(1)} %get-tuple-element.32), channel_id=1, source_target_pairs={{0,96},{32,0},{64,32},{96,64},{1,97},{33,1},{65,33},{97,65},{2,98}... | collective-permute-start | bytes 589832 | tf_op jit(solution)/shard_map/ppermute | solution.py:549
  86.6 24.2 %copy-start.1 = (bf16[256,768]{1,0:T(8,128)(2,1)S(1)}, bf16[256,768]{1,0:T(8,128)(2,1)}, u32[]{:S(2)}) copy-start(bf16[256,768]{1,0:T(8,128)(2,1)} %constant.35.clone.refs_7_.refs_1_.refs_2_) | copy-start | bytes 1179652
  86.6 24.2 %copy-start.3 = (f32[2,2,128,128]{3,2,1,0:T(8,128)S(1)}, f32[2,2,128,128]{3,2,1,0:T(8,128)}, u32[]{:S(2)}) copy-start(f32[2,2,128,128]{3,2,1,0:T(8,128)} %constant.45.clone.refs_6_) | copy-start | bytes 786436
  86.6 24.2 %copy-start.4 = (bf16[384,256]{1,0:T(8,128)(2,1)S(1)}, bf16[384,256]{1,0:T(8,128)(2,1)}, u32[]{:S(2)}) copy-start(bf16[384,256]{1,0:T(8,128)(2,1)} %constant.43.clone.refs_4_) | copy-start | bytes 589828
  86.6 24.2 %copy-start.5 = (f32[2,128,128]{2,1,0:T(8,128)S(1)}, f32[2,128,128]{2,1,0:T(8,128)}, u32[]{:S(2)}) copy-start(f32[2,128,128]{2,1,0:T(8,128)} %constant.41.clone.refs_2_.refs_3_) | copy-start | bytes 393220
  117.3 18.7 %copy-start = (f32[32,4096]{1,0:T(8,128)S(1)}, f32[32,4096]{1,0:T(8,128)}, u32[]{:S(2)}) copy-start(f32[32,4096]{1,0:T(8,128)} %refs_1_.4) | copy-start | bytes 1572868
  117.3 18.7 %copy-start.2 = (bf16[768,256]{1,0:T(8,128)(2,1)S(1)}, bf16[768,256]{1,0:T(8,128)(2,1)}, u32[]{:S(2)}) copy-start(bf16[768,256]{1,0:T(8,128)(2,1)} %constant.36.clone.refs_3_) | copy-start | bytes 1179652
  117.3 18.7 %copy-start.6 = (f32[2,32,128]{2,1,0:T(8,128)S(1)}, f32[2,32,128]{2,1,0:T(8,128)}, u32[]{:S(2)}) copy-start(f32[2,32,128]{2,1,0:T(8,128)} %constant.37.clone.refs_6_.refs_2_) | copy-start | bytes 98308

commit v8 on v6

--- a/solution.py
+++ b/solution.py
@@ -242,13 +242,14 @@
             k = count[o]
             count[o] = k + 1
             to = group * n_slab + (row & ~1) + flip
-            placed.append((at, to, k & 1, ((row & 1) * 16 + col + 1).astype(f32)))
-        parts = [(residual[at], position[at]) for at, _, _, _ in placed]
-        for (at, to, slot, tag), (value, place) in zip(placed, parts):
+            k = k & 1
+            placed.append((at, to, k, (col + 1).astype(f32), 66 + 2 * (row & 1) + k, (1 + (col >> 3)).astype(f32)))
+        parts = [(residual[at], position[at]) for at, *_ in placed]
+        for (at, to, slot, tag, spot, phase), (value, place) in zip(placed, parts):
             for part in range(2):
                 out[to, slot * 4 + part] = value[part : part + 1]
                 out[to, slot * 4 + 2 + part] = place[part : part + 1]
-            tags[to] = jnp.where(lane == 64 + slot, tag, tags[to])
+            tags[to] = jnp.where(lane == 64 + slot, tag, jnp.where(lane == spot, phase, tags[to]))
         return 0
 
     lax.fori_loop(0, owner.shape[0] // 8, step, 0)
@@ -271,8 +272,8 @@
 
 
 def grid_into(first, me, core, own, others, data, mate, total, cells, order):
-    first = first + 16 * core
-    slots, wide = own.shape[0], total.shape[2]
+    sources, wide = own.shape[0] // 6, total.shape[2]
+    slots = 2 * sources
     for axis in range(2):
         at = lax.broadcasted_iota(jnp.int32, (TILE, TILE), axis).astype(f32)
         cells[2 * axis] = at * 0.25
@@ -280,15 +281,17 @@
     total[...] = jnp.zeros_like(total)
 
     def scan(tags, begin):
-        def step(s, n):
-            order[n] = begin + s
-            tag = tags[s] - first
-            return n + ((tag > 0) & (tag <= wide)).astype(jnp.int32)
+        def step(src, n):
+            for slot in range(2):
+                order[n] = begin + 2 * src + slot
+                phase = tags[6 * src + 2 + 2 * core + slot]
+                n = n + (phase & 1 if first == 0 else phase >> 1)
+            return n
 
         return step
 
-    n = lax.fori_loop(0, slots, scan(own, 0), jnp.int32(0), unroll=8)
-    n = lax.fori_loop(0, slots, scan(others, slots), n, unroll=8)
+    n = lax.fori_loop(0, sources, scan(own, 0), jnp.int32(0), unroll=8)
+    n = lax.fori_loop(0, sources, scan(others, slots), n, unroll=8)
     for extra in range(REST):
         order[n + extra] = order[jnp.maximum(n - 1, 0)]
 
@@ -302,7 +305,8 @@
         s = s - far * slots
         src, slot = s >> 1, s & 1
         flip = (core + far) & 1
-        t = jnp.clip(jnp.where(far == 1, others[s], own[s]) - first - 1, 0, wide - 1)
+        tag = 6 * src + slot
+        t = jnp.clip(jnp.where(far == 1, others[tag], own[tag]) - first - 1, 0, wide - 1)
         value_re, value_im, row, col = (
             jnp.where(far == 1, mate[src, slot * 4 + i], data[src, slot * 4 + i]) for i in range(4)
         )
@@ -332,7 +336,6 @@
 
 def cols_kernel(*refs):
     me, whole, parts, (tw, w, w_back, out, mid) = refs[0], refs[1], refs[2:6], refs[6:]
-    tw = tw.ready()
 
     def tile(b, ri, at):
         group = b // 16
@@ -344,16 +347,23 @@
         at = pl.ds(pl.multiple_of(i * 8, 8), 8)
         first = [(tile(b, 0, at), tile(b, 1, at)) for b in range(64)]
         for c, (re, im) in enumerate(fft_list(first)):
-            cos, sin = tw[me[0], 0, c : c + 1, :], tw[me[0], 1, c : c + 1, :]
             half, c = c // 32, c % 32
             to = 32 * half + c if c <= 16 else 32 * (1 - half) + 48 - c
-            mid[to, at, 0:128] = re * cos - im * sin
-            mid[to, at, 128:256] = re * sin + im * cos
+            mid[to, at, 0:128] = re
+            mid[to, at, 128:256] = im
         return 0
+
+    def turned_rows(to):
+        half, c = to // 32, to % 32
+        c = 32 * half + c if c <= 16 else 32 * (1 - half) + 48 - c
+        cos, sin = tw[me[0], 0, c : c + 1, :], tw[me[0], 1, c : c + 1, :]
+        re, im = mid[to, :, 0:128], mid[to, :, 128:256]
+        return jnp.concatenate([re * cos - im * sin, re * sin + im * cos], axis=1)
 
     lax.fori_loop(0, 4, rows, 0)
     for pair in range(8):
-        part = spread(mid[8 * pair : 8 * pair + 8].reshape(256, 256), RIGHT[6], 1)
+        part = jnp.concatenate([turned_rows(8 * pair + k) for k in range(8)], axis=0)
+        part = spread(part, RIGHT[6], 1)
         res = mm((w if pair % 4 < 2 else w_back)[...], part, NT)
         if pair % 4 == 2:
             own = mm(w[...], part[0:128], NT)
@@ -527,7 +537,7 @@
     )(owner[:, 0], tile_local, residual, position, xi, amplitude, t["tw_row"], t["w128"])
     data = exchange(packed, everywhere)
     mate = lax.ppermute(data, "slab", [(i, i ^ 1) for i in range(n_slab)])
-    tags = tuple(a[:, 16, 0, 64:66].reshape(2 * devices).astype(jnp.int32) for a in (data, mate))
+    tags = tuple(a[:, 16, 0, 64:70].reshape(6 * devices).astype(jnp.int32) for a in (data, mate))
     spare = [VM((4, TILE, TILE), f32), SM((4 * devices + REST,), jnp.int32)]
     shape = (2, 8, 32, 128)
     whole = call(

time: 138 us -> 140 us (1.014); the launches traced: 138 us -> 137 us
  Pallas kernels: 45.7 us -> 35.7 us
  blocking collectives: 72.9 us -> 77.4 us
  starting transfers between devices: 7.42 us -> 11.1 us
    pallas_call x7, Pallas kernels: 45.7 us -> 35.7 us  [placed(): results = got(*arrays)]
    all_to_all x3, blocking collectives: 72.9 us -> 77.4 us  [exchange(): return lax.all_to_all(a, axis, split_axis=0, concat_axis=0, tiled=True)]
    ppermute x3, starting transfers between devices: 2.74 us -> 6.09 us  [per_device(): lax.ppermute(parts[k], 'base', [(i, (i + k) % n_base) for i in range(n_ba...]
  transfers between devices with their start and end apart: 5 -> 5, of which waited for: 3 -> 3; matrix products, arithmetic and copies ran while one was open for 0% -> 0% of each run, Pallas kernels for 11% -> 8%
where the time goes in v8:
time: 140 us; the launch traced here: 137 us
  blocking collectives  77.4 us (55%)
  Pallas kernels  35.7 us (26%)
  waiting for transfers between devices  11.8 us (8%)
  starting transfers between devices  11.1 us (8%)
    all_to_all x3, blocking collectives, exchange(): return lax.all_to_all(a, axis, split_axis=0, concat_axis=0, tiled=True)  77.4 us
    pallas_call x7, Pallas kernels, placed(): results = got(*arrays)  35.7 us
    ppermute x3, waiting for transfers between devices, per_device(): lax.ppermute(parts[k], 'base', [(i, (i + k) % n_base) for i in range(n_ba...  9.91 us
    ppermute x3, starting transfers between devices, per_device(): lax.ppermute(parts[k], 'base', [(i, (i + k) % n_base) for i in range(n_ba...  6.09 us
    all_to_all x1, starting transfers between devices, exchange(): return lax.all_to_all(a, axis, split_axis=0, concat_axis=0, tiled=True)  3.87 us
  transfers between devices with their start and end apart: 5, of which 3 were waited for; matrix products, arithmetic and copies ran while one was open for 0% of the time, Pallas kernels for 8%

profile of v8, /device:TPU:1, one launch (start us, length us, event | category | flops | bytes accessed | tf_op | source)
XLA Modules:
  0.0 137.0 jit_solution(15467051949602270896)
XLA Ops:
  0.0 3.8 %shard_map.172 = f32[128,17,1,128]{3,2,1,0:T(1,128)S(1)} custom-call(s32[128]{0:T(128)} %bitcast.5, s32[128]{0:T(128)} %refs_1_.3, f32[128,2,128]{2,1,0:T(2,128)} %refs_2_.4, f32[128,2,128]{2,1,0:T(2,128)} %refs_3_.4, f32[32,4096]{1,0:T(8,128)} %refs_4_.2, f32[32,4096]{1,0:T(8,128)} %refs_1_.4, f32[2,32,128]{2,1,0:T(8,128)} %constant.37.clone.refs_6_.refs_2_, ...), custom_call_target="tpu_custom_call" | custom-call | flops 2000000000 | bytes 2228224 | tf_op jit(solution)/shard_map/pallas_call | solution.py:209
  3.8 31.1 %all_to_all.20.refs_3_.refs_0_ = f32[128,17,1,128]{3,2,1,0:T(1,128)S(1)} all-to-all(f32[128,17,1,128]{3,2,1,0:T(1,128)S(1)} %shard_map.172), channel_id=1, replica_groups=mesh['base'=4,'slab'=32] {'base','slab'}, dimensions={0} | all-to-all | bytes 2228224 | tf_op jit(solution)/shard_map/all_to_all | solution.py:516
  34.9 1.2 collective-permute-start
  36.1 0.1 pad_add_fusion.refs_0_
  36.2 0.3 fusion.1
  36.4 0.1 convert_element_type.11.refs_1_
  36.6 1.9 %collective-permute-done.refs_4_ = f32[128,17,1,128]{3,2,1,0:T(1,128)S(1)} collective-permute-done((f32[128,17,1,128]{3,2,1,0:T(1,128)S(1)}, f32[128,17,1,128]{3,2,1,0:T(1,128)S(1)}, u32[]{:S(2)}, u32[]{:S(2)}) %collective-permute-start) | collective-permute-done | bytes 1114144 | tf_op jit(solution)/shard_map/ppermute | solution.py:539
  38.5 0.3 fusion
  38.7 0.1 convert_element_type.13.refs_2_
  38.9 8.2 %shard_map.173 = f32[4,2,8,32,128]{4,3,2,1,0:T(8,128)} custom-call(s32[2]{0:T(128)S(1)} %pad_add_fusion.refs_0_, s32[768]{0:T(1024)S(1)} %convert_element_type.11.refs_1_, s32[768]{0:T(1024)S(1)} %convert_element_type.13.refs_2_, f32[128,17,1,128]{3,2,1,0:T(1,128)S(1)} %all_to_all.20.refs_3_.refs_0_, f32[128,17,1,128]{3,2,1,0:T(1,128)S(1)} %collective-permute-done.refs_4_), custom_call_target="tpu_custom_call" | custom-call | flops 20000000000 | bytes 2097152 | tf_op jit(solution)/shard_map/pallas_call | solution.py:209
  47.1 3.9 %all-to-all-start.1 = ((f32[4,2,8,32,128]{4,3,2,1,0:T(8,128)}), f32[4,2,8,32,128]{4,3,2,1,0:T(8,128)S(1)}, u32[]{:S(2)}, u32[]{:S(2)}) async-start(f32[4,2,8,32,128]{4,3,2,1,0:T(8,128)} %shard_map.173), calls=%async_computation.1 | async-start | bytes 2097152 | tf_op jit(solution)/shard_map/all_to_all | solution.py:516
  51.0 6.9 %shard_map.174 = (f32[2,8,32,128]{3,2,1,0:T(8,128)S(1)}, f32[2,8,32,128]{3,2,1,0:T(8,128)S(1)}, f32[2,8,32,128]{3,2,1,0:T(8,128)S(1)}, f32[2,8,32,128]{3,2,1,0:T(8,128)S(1)}) custom-call(s32[2]{0:T(128)S(1)} %pad_add_fusion.refs_0_, s32[768]{0:T(1024)S(1)} %convert_element_type.11.refs_1_, s32[768]{0:T(1024)S(1)} %convert_element_type.13.refs_2_, ...), custom_call_target="tpu_custom_call" | custom-call | flops 20000000000 | bytes 2097152 | tf_op jit(solution)/shard_map/pallas_call | solution.py:209
  57.9 2.8 %collective-permute-start.1 = (f32[2,8,32,128]{3,2,1,0:T(8,128)S(1)}, f32[2,8,32,128]{3,2,1,0:T(8,128)S(1)}, u32[]{:S(2)}, u32[]{:S(2)}) collective-permute-start(f32[2,8,32,128]{3,2,1,0:T(8,128)S(1)} %get-tuple-element.30), channel_id=1, source_target_pairs={{0,32},{32,64},{64,96},{96,0},{1,33},{33,65},{65,97},{97,1},{2,34}... | collective-permute-start | bytes 786440 | tf_op jit(solution)/shard_map/ppermute | solution.py:557
  60.7 3.3 %collective-permute-start.2 = (f32[2,8,32,128]{3,2,1,0:T(8,128)S(1)}, f32[2,8,32,128]{3,2,1,0:T(8,128)S(1)}, u32[]{:S(2)}, u32[]{:S(2)}) collective-permute-start(f32[2,8,32,128]{3,2,1,0:T(8,128)S(1)} %get-tuple-element.31), channel_id=1, source_target_pairs={{0,64},{32,96},{64,0},{96,32},{1,65},{33,97},{65,1},{97,33},{2,66}... | collective-permute-start | bytes 786440 | tf_op jit(solution)/shard_map/ppermute | solution.py:557
  64.0 3.7 %shard_map.175.refs_0_ = f32[4,256,128]{2,1,0:T(8,128)} custom-call(f32[128,17,1,128]{3,2,1,0:T(1,128)S(1)} %all_to_all.20.refs_3_.refs_0_, bf16[256,768]{1,0:T(8,128)(2,1)} %constant.35.clone.refs_7_.refs_1_.refs_2_, f32[2,128,128]{2,1,0:T(8,128)} %constant.41.clone.refs_2_.refs_3_, bf16[768,128]{1,0:T(8,128)(2,1)} %constant.42.clone.refs_3_), custom_call_target="tpu_custom_call" | custom-call | flops 4000000000 | bytes 1048576 | tf_op jit(solution)/shard_map/pallas_call | solution.py:209
  67.6 4.8 %collective-permute-done.1.refs_3_ = f32[2,8,32,128]{3,2,1,0:T(8,128)S(1)} collective-permute-done((f32[2,8,32,128]{3,2,1,0:T(8,128)S(1)}, f32[2,8,32,128]{3,2,1,0:T(8,128)S(1)}, u32[]{:S(2)}, u32[]{:S(2)}) %collective-permute-start.1) | collective-permute-done | bytes 262176 | tf_op jit(solution)/shard_map/ppermute | solution.py:557
  72.5 5.1 %collective-permute-done.2.refs_4_ = f32[2,8,32,128]{3,2,1,0:T(8,128)S(1)} collective-permute-done((f32[2,8,32,128]{3,2,1,0:T(8,128)S(1)}, f32[2,8,32,128]{3,2,1,0:T(8,128)S(1)}, u32[]{:S(2)}, u32[]{:S(2)}) %collective-permute-start.2) | collective-permute-done | bytes 262176 | tf_op jit(solution)/shard_map/ppermute | solution.py:557
  77.6 4.7 %shard_map.176 = f32[64,2,16,128]{3,2,1,0:T(8,128)S(1)} custom-call(s32[2]{0:T(128)S(1)} %pad_add_fusion.refs_0_, f32[4,2,8,32,128]{4,3,2,1,0:T(8,128)S(1)} %all-to-all-done.1.refs_1_, f32[2,8,32,128]{3,2,1,0:T(8,128)S(1)} %get-tuple-element.29.refs_2_, f32[2,8,32,128]{3,2,1,0:T(8,128)S(1)} %collective-permute-done.1.refs_3_, ...), custom_call_target="tpu_custom_call" | custom-call | flops 4000000000 | bytes 2097152 | tf_op jit(solution)/shard_map/pallas_call | solution.py:209
  82.3 0.0 copy-start.1
  82.3 0.0 copy-start.3
  82.3 27.6 %all_to_all.21.refs_1_ = f32[128,16,128]{2,1,0:T(8,128)S(1)} all-to-all(f32[128,16,128]{2,1,0:T(8,128)S(1)} %bitcast.4), channel_id=1, replica_groups=mesh['base'=4,'slab'=32] {'base','slab'}, dimensions={0} | all-to-all | bytes 2097152 | tf_op jit(solution)/shard_map/all_to_all | solution.py:516
  109.9 6.5 %shard_map.177 = f32[128,9,1,128]{3,2,1,0:T(1,128)S(1)} custom-call(f32[4,256,128]{2,1,0:T(8,128)} %shard_map.175.refs_0_, f32[128,16,128]{2,1,0:T(8,128)S(1)} %all_to_all.21.refs_1_, bf16[256,768]{1,0:T(8,128)(2,1)S(1)} %copy-done.1, f32[2,128,128]{2,1,0:T(8,128)S(1)} %copy-done.5, bf16[384,256]{1,0:T(8,128)(2,1)S(1)} %copy-done.4, ...), custom_call_target="tpu_custom_call" | custom-call | flops 8000000000 | bytes 1179648 | tf_op jit(solution)/shard_map/pallas_call | solution.py:209
  116.5 18.7 %all_to_all.22.refs_0_ = f32[128,9,1,128]{3,2,1,0:T(1,128)S(1)} all-to-all(f32[128,9,1,128]{3,2,1,0:T(1,128)S(1)} %shard_map.177), channel_id=1, replica_groups=mesh['base'=4,'slab'=32] {'base','slab'}, dimensions={0} | all-to-all | bytes 1179648 | tf_op jit(solution)/shard_map/all_to_all | solution.py:516
  135.2 1.8 %shard_map.178 = f32[32,4096]{1,0:T(8,128)} custom-call(f32[128,9,1,128]{3,2,1,0:T(1,128)S(1)} %all_to_all.22.refs_0_, f32[32,4096]{1,0:T(8,128)S(1)} %copy-done, f32[2,32,128]{2,1,0:T(8,128)S(1)} %copy-done.6, bf16[768,256]{1,0:T(8,128)(2,1)S(1)} %copy-done.2), custom_call_target="tpu_custom_call" | custom-call | flops 3000000000 | bytes 1048576 | tf_op jit(solution)/shard_map/pallas_call | solution.py:209
  (15 shorter events, 0.0 us)
Async XLA Ops:
  34.9 3.5 %collective-permute-start = (f32[128,17,1,128]{3,2,1,0:T(1,128)S(1)}, f32[128,17,1,128]{3,2,1,0:T(1,128)S(1)}, u32[]{:S(2)}, u32[]{:S(2)}) collective-permute-start(f32[128,17,1,128]{3,2,1,0:T(1,128)S(1)} %all_to_all.20.refs_3_.refs_0_), channel_id=1, source_target_pairs={{0,1},{1,0},{2,3},{3,2},{4,5},{5,4},{6,7},{7,6},{8,9},{9,8},{10,11... | collective-permute-start | bytes 3342344 | tf_op jit(solution)/shard_map/ppermute | solution.py:539
  47.1 30.4 %all-to-all-start.1 = ((f32[4,2,8,32,128]{4,3,2,1,0:T(8,128)}), f32[4,2,8,32,128]{4,3,2,1,0:T(8,128)S(1)}, u32[]{:S(2)}, u32[]{:S(2)}) async-start(f32[4,2,8,32,128]{4,3,2,1,0:T(8,128)} %shard_map.173), calls=%async_computation.1 | async-start | bytes 2097152 | tf_op jit(solution)/shard_map/all_to_all | solution.py:516
  57.9 14.6 %collective-permute-start.1 = (f32[2,8,32,128]{3,2,1,0:T(8,128)S(1)}, f32[2,8,32,128]{3,2,1,0:T(8,128)S(1)}, u32[]{:S(2)}, u32[]{:S(2)}) collective-permute-start(f32[2,8,32,128]{3,2,1,0:T(8,128)S(1)} %get-tuple-element.30), channel_id=1, source_target_pairs={{0,32},{32,64},{64,96},{96,0},{1,33},{33,65},{65,97},{97,1},{2,34}... | collective-permute-start | bytes 786440 | tf_op jit(solution)/shard_map/ppermute | solution.py:557
  60.7 16.8 %collective-permute-start.2 = (f32[2,8,32,128]{3,2,1,0:T(8,128)S(1)}, f32[2,8,32,128]{3,2,1,0:T(8,128)S(1)}, u32[]{:S(2)}, u32[]{:S(2)}) collective-permute-start(f32[2,8,32,128]{3,2,1,0:T(8,128)S(1)} %get-tuple-element.31), channel_id=1, source_target_pairs={{0,64},{32,96},{64,0},{96,32},{1,65},{33,97},{65,1},{97,33},{2,66}... | collective-permute-start | bytes 786440 | tf_op jit(solution)/shard_map/ppermute | solution.py:557
  64.0 13.6 %collective-permute-start.3 = (f32[2,8,32,128]{3,2,1,0:T(8,128)S(1)}, f32[2,8,32,128]{3,2,1,0:T(8,128)S(1)}, u32[]{:S(2)}, u32[]{:S(2)}) collective-permute-start(f32[2,8,32,128]{3,2,1,0:T(8,128)S(1)} %get-tuple-element.32), channel_id=1, source_target_pairs={{0,96},{32,0},{64,32},{96,64},{1,97},{33,1},{65,33},{97,65},{2,98}... | collective-permute-start | bytes 786440 | tf_op jit(solution)/shard_map/ppermute | solution.py:557
  82.3 27.6 %copy-start.1 = (bf16[256,768]{1,0:T(8,128)(2,1)S(1)}, bf16[256,768]{1,0:T(8,128)(2,1)}, u32[]{:S(2)}) copy-start(bf16[256,768]{1,0:T(8,128)(2,1)} %constant.35.clone.refs_7_.refs_1_.refs_2_) | copy-start | bytes 1179652
  82.3 27.6 %copy-start.3 = (f32[2,2,128,128]{3,2,1,0:T(8,128)S(1)}, f32[2,2,128,128]{3,2,1,0:T(8,128)}, u32[]{:S(2)}) copy-start(f32[2,2,128,128]{3,2,1,0:T(8,128)} %constant.45.clone.refs_6_) | copy-start | bytes 786436
  82.3 27.6 %copy-start.4 = (bf16[384,256]{1,0:T(8,128)(2,1)S(1)}, bf16[384,256]{1,0:T(8,128)(2,1)}, u32[]{:S(2)}) copy-start(bf16[384,256]{1,0:T(8,128)(2,1)} %constant.43.clone.refs_4_) | copy-start | bytes 589828
  82.3 27.6 %copy-start.5 = (f32[2,128,128]{2,1,0:T(8,128)S(1)}, f32[2,128,128]{2,1,0:T(8,128)}, u32[]{:S(2)}) copy-start(f32[2,128,128]{2,1,0:T(8,128)} %constant.41.clone.refs_2_.refs_3_) | copy-start | bytes 393220
  116.4 18.7 %copy-start = (f32[32,4096]{1,0:T(8,128)S(1)}, f32[32,4096]{1,0:T(8,128)}, u32[]{:S(2)}) copy-start(f32[32,4096]{1,0:T(8,128)} %refs_1_.4) | copy-start | bytes 1572868
  116.5 18.7 %copy-start.2 = (bf16[768,256]{1,0:T(8,128)(2,1)S(1)}, bf16[768,256]{1,0:T(8,128)(2,1)}, u32[]{:S(2)}) copy-start(bf16[768,256]{1,0:T(8,128)(2,1)} %constant.36.clone.refs_3_) | copy-start | bytes 1179652
  116.5 18.7 %copy-start.6 = (f32[2,32,128]{2,1,0:T(8,128)S(1)}, f32[2,32,128]{2,1,0:T(8,128)}, u32[]{:S(2)}) copy-start(f32[2,32,128]{2,1,0:T(8,128)} %constant.37.clone.refs_6_.refs_2_) | copy-start | bytes 98308

commit v9 on v8

--- a/solution.py
+++ b/solution.py
@@ -261,10 +261,6 @@
     return x * x * x
 
 
-def grid_whole_kernel(first, me, own, others, data, mate, total, cells, order):
-    grid_into(first, 0, me[1], own, others, data, mate, total, cells, order)
-
-
 def grid_parts_kernel(first, me, own, others, data, mate, out0, out1, out2, out3, cells, order, total):
     grid_into(first, me[0], me[1], own, others, data, mate, total, cells, order)
     for k, out in enumerate((out0, out1, out2, out3)):
@@ -335,13 +331,10 @@
 
 
 def cols_kernel(*refs):
-    me, whole, parts, (tw, w, w_back, out, mid) = refs[0], refs[1], refs[2:6], refs[6:]
+    me, parts, (tw, w, w_back, out, mid) = refs[0], refs[1:9], refs[9:]
 
     def tile(b, ri, at):
-        group = b // 16
-        if b % 16 < 8:
-            return whole[(me[0] + group) & 3, ri, b % 8, at, :]
-        return parts[-group % 4][ri, b % 8, at, :]
+        return parts[b % 16 // 8 * 4 + -(b // 16) % 4][ri, b % 8, at, :]
 
     def rows(i, _):
         at = pl.ds(pl.multiple_of(i * 8, 8), 8)
@@ -540,22 +533,22 @@
     tags = tuple(a[:, 16, 0, 64:70].reshape(6 * devices).astype(jnp.int32) for a in (data, mate))
     spare = [VM((4, TILE, TILE), f32), SM((4 * devices + REST,), jnp.int32)]
     shape = (2, 8, 32, 128)
-    whole = call(
-        functools.partial(grid_whole_kernel, 0), (n_base, *shape), [SM, SM, SM, VM, VM], spare, 2e10
-    )(me, *tags, data, mate)
-    whole, tags = lax.optimization_barrier((whole, tags))
-    whole = exchange(whole, "base")
-    parts = call(
-        functools.partial(grid_parts_kernel, 8),
-        [shape] * n_base,
-        [SM, SM, SM, VM, VM],
-        [*spare, VM((n_base, *shape), f32)],
-        2e10,
-    )(me, *tags, data, mate)
-    parts, field = lax.optimization_barrier((parts, data))
-    parts = [parts[0]] + [
-        lax.ppermute(parts[k], "base", [(i, (i + k) % n_base) for i in range(n_base)]) for k in range(1, n_base)
-    ]
+    grids = []
+    for phase in range(2):
+        parts = call(
+            functools.partial(grid_parts_kernel, 8 * phase),
+            [shape] * n_base,
+            [SM, SM, SM, VM, VM],
+            [*spare, VM((n_base, *shape), f32)],
+            2e10,
+        )(me, *tags, data, mate)
+        if phase == 0:
+            parts, tags = lax.optimization_barrier((parts, tags))
+        else:
+            parts, grids, field = lax.optimization_barrier((parts, grids, data))
+        grids = [*grids, parts[0]] + [
+            lax.ppermute(parts[k], "base", [(i, (i + k) % n_base) for i in range(n_base)]) for k in range(1, n_base)
+        ]
     sky = call(
         sky_kernel,
         (4, 256, 128),
@@ -565,19 +558,19 @@
         [(1, VM((256, 768), bf16)), (2, VM((2, 128, 128), f32)), (3, VM((768, 128), bf16))],
         True,
     )(field, t["w128"], t["tw_f"], t["r_f"])
-    parts[0], sky = lax.optimization_barrier((parts[0], sky))
+    grids[0], sky = lax.optimization_barrier((grids[0], sky))
     cols = call(
         cols_kernel,
         (devices // 2, 2, 16, 128),
-        [SM] + [VM] * 8,
+        [SM] + [VM] * 11,
         [VM((64, 32, 256), f32)],
         4e9,
         [
-            (6, VM((n_base, 2, 64, 128), f32)),
-            (7, VM((128, 1536), bf16)),
-            (8, VM((128, 1536), bf16)),
+            (9, VM((n_base, 2, 64, 128), f32)),
+            (10, VM((128, 1536), bf16)),
+            (11, VM((128, 1536), bf16)),
         ],
-    )(me, whole, *parts, t["tw_cols"], t["w_cols"], t["w_back"])
+    )(me, *grids, t["tw_cols"], t["w_cols"], t["w_back"])
     cols = exchange(cols.reshape(devices, 16, 128), everywhere)
     fold = call(
         image_kernel,

time: 140 us -> 138 us (0.986); the launches traced: 137 us -> 137 us
  waiting for transfers between devices: 11.8 us -> 13.7 us
  starting transfers between devices: 11.1 us -> 9.3 us
    all_to_all x1 -> x0, starting transfers between devices: 3.87 us -> none  [exchange(): return lax.all_to_all(a, axis, split_axis=0, concat_axis=0, tiled=True)]
    ppermute x3 -> x6, starting transfers between devices: 6.09 us -> 8.13 us  [per_device(): lax.ppermute(parts[k], 'base', [(i, (i + k) % n_base) for i in range(n_ba...]
    ppermute x3 -> x6, waiting for transfers between devices: 9.91 us -> 11.8 us  [per_device(): lax.ppermute(parts[k], 'base', [(i, (i + k) % n_base) for i in range(n_ba...]
  transfers between devices with their start and end apart: 5 -> 7, of which waited for: 3 -> 5; matrix products, arithmetic and copies ran while one was open for 0% -> 0% of each run, Pallas kernels for 8% -> 8%
where the time goes in v9:
time: 138 us; the launch traced here: 137 us
  blocking collectives  76.9 us (56%)
  Pallas kernels  36 us (26%)
  waiting for transfers between devices  13.7 us (10%)
  starting transfers between devices  9.3 us (7%)
    all_to_all x3, blocking collectives, exchange(): return lax.all_to_all(a, axis, split_axis=0, concat_axis=0, tiled=True)  76.9 us
    pallas_call x7, Pallas kernels, placed(): results = got(*arrays)  36 us
    ppermute x6, waiting for transfers between devices, per_device(): lax.ppermute(parts[k], 'base', [(i, (i + k) % n_base) for i in range(n_ba...  11.8 us
    ppermute x6, starting transfers between devices, per_device(): lax.ppermute(parts[k], 'base', [(i, (i + k) % n_base) for i in range(n_ba...  8.13 us
  transfers between devices with their start and end apart: 7, of which 5 were waited for; matrix products, arithmetic and copies ran while one was open for 0% of the time, Pallas kernels for 8%

profile of v9, /device:TPU:1, one launch (start us, length us, event | category | flops | bytes accessed | tf_op | source)
XLA Modules:
  0.0 137.0 jit_solution(8182094086619785962)
XLA Ops:
  0.0 3.8 %shard_map.172 = f32[128,17,1,128]{3,2,1,0:T(1,128)S(1)} custom-call(s32[128]{0:T(128)} %bitcast.5, s32[128]{0:T(128)} %refs_1_.3, f32[128,2,128]{2,1,0:T(2,128)} %refs_2_.4, f32[128,2,128]{2,1,0:T(2,128)} %refs_3_.4, f32[32,4096]{1,0:T(8,128)} %refs_4_.2, f32[32,4096]{1,0:T(8,128)} %refs_1_.4, f32[2,32,128]{2,1,0:T(8,128)} %constant.37.clone.refs_6_.refs_2_, ...), custom_call_target="tpu_custom_call" | custom-call | flops 2000000000 | bytes 2228224 | tf_op jit(solution)/shard_map/pallas_call | solution.py:209
  3.8 31.1 %all_to_all.15.refs_3_.refs_0_ = f32[128,17,1,128]{3,2,1,0:T(1,128)S(1)} all-to-all(f32[128,17,1,128]{3,2,1,0:T(1,128)S(1)} %shard_map.172), channel_id=1, replica_groups=mesh['base'=4,'slab'=32] {'base','slab'}, dimensions={0} | all-to-all | bytes 2228224 | tf_op jit(solution)/shard_map/all_to_all | solution.py:509
  34.9 1.2 collective-permute-start
  36.2 0.3 fusion.1
  36.4 0.1 convert_element_type.11.refs_1_
  36.6 1.9 %collective-permute-done.refs_4_ = f32[128,17,1,128]{3,2,1,0:T(1,128)S(1)} collective-permute-done((f32[128,17,1,128]{3,2,1,0:T(1,128)S(1)}, f32[128,17,1,128]{3,2,1,0:T(1,128)S(1)}, u32[]{:S(2)}, u32[]{:S(2)}) %collective-permute-start) | collective-permute-done | bytes 1114144 | tf_op jit(solution)/shard_map/ppermute | solution.py:532
  38.5 0.3 fusion
  38.7 0.1 convert_element_type.13.refs_2_
  38.9 8.2 %shard_map.173 = (f32[2,8,32,128]{3,2,1,0:T(8,128)S(1)}, f32[2,8,32,128]{3,2,1,0:T(8,128)S(1)}, f32[2,8,32,128]{3,2,1,0:T(8,128)S(1)}, f32[2,8,32,128]{3,2,1,0:T(8,128)S(1)}) custom-call(s32[2]{0:T(128)S(1)} %pad_add_fusion.refs_0_, s32[768]{0:T(1024)S(1)} %convert_element_type.11.refs_1_, s32[768]{0:T(1024)S(1)} %convert_element_type.13.refs_2_, ...), custom_call_target="tpu_custom_call" | custom-call | flops 20000000000 | bytes 2097152 | tf_op jit(solution)/shard_map/pallas_call | solution.py:209
  47.2 1.5 %collective-permute-start.2 = (f32[2,8,32,128]{3,2,1,0:T(8,128)S(1)}, f32[2,8,32,128]{3,2,1,0:T(8,128)S(1)}, u32[]{:S(2)}, u32[]{:S(2)}) collective-permute-start(f32[2,8,32,128]{3,2,1,0:T(8,128)S(1)} %get-tuple-element.42), channel_id=1, source_target_pairs={{0,64},{32,96},{64,0},{96,32},{1,65},{33,97},{65,1},{97,33},{2,66}... | collective-permute-start | bytes 786440 | tf_op jit(solution)/shard_map/ppermute | solution.py:550
  48.6 2.0 %collective-permute-start.3 = (f32[2,8,32,128]{3,2,1,0:T(8,128)S(1)}, f32[2,8,32,128]{3,2,1,0:T(8,128)S(1)}, u32[]{:S(2)}, u32[]{:S(2)}) collective-permute-start(f32[2,8,32,128]{3,2,1,0:T(8,128)S(1)} %get-tuple-element.43), channel_id=1, source_target_pairs={{0,96},{32,0},{64,32},{96,64},{1,97},{33,1},{65,33},{97,65},{2,98}... | collective-permute-start | bytes 786440 | tf_op jit(solution)/shard_map/ppermute | solution.py:550
  50.6 7.3 %shard_map.174 = (f32[2,8,32,128]{3,2,1,0:T(8,128)S(1)}, f32[2,8,32,128]{3,2,1,0:T(8,128)S(1)}, f32[2,8,32,128]{3,2,1,0:T(8,128)S(1)}, f32[2,8,32,128]{3,2,1,0:T(8,128)S(1)}) custom-call(s32[2]{0:T(128)S(1)} %pad_add_fusion.refs_0_, s32[768]{0:T(1024)S(1)} %convert_element_type.11.refs_1_, s32[768]{0:T(1024)S(1)} %convert_element_type.13.refs_2_, ...), custom_call_target="tpu_custom_call" | custom-call | flops 20000000000 | bytes 2097152 | tf_op jit(solution)/shard_map/pallas_call | solution.py:209
  57.9 3.6 %collective-permute-done.1.refs_2_ = f32[2,8,32,128]{3,2,1,0:T(8,128)S(1)} collective-permute-done((f32[2,8,32,128]{3,2,1,0:T(8,128)S(1)}, f32[2,8,32,128]{3,2,1,0:T(8,128)S(1)}, u32[]{:S(2)}, u32[]{:S(2)}) %collective-permute-start.1) | collective-permute-done | bytes 262176 | tf_op jit(solution)/shard_map/ppermute | solution.py:550
  61.5 0.3 collective-permute-done.3.refs_4_
  61.8 1.8 %collective-permute-start.4 = (f32[2,8,32,128]{3,2,1,0:T(8,128)S(1)}, f32[2,8,32,128]{3,2,1,0:T(8,128)S(1)}, u32[]{:S(2)}, u32[]{:S(2)}) collective-permute-start(f32[2,8,32,128]{3,2,1,0:T(8,128)S(1)} %get-tuple-element.52), channel_id=1, source_target_pairs={{0,32},{32,64},{64,96},{96,0},{1,33},{33,65},{65,97},{97,1},{2,34}... | collective-permute-start | bytes 786440 | tf_op jit(solution)/shard_map/ppermute | solution.py:550
  63.6 2.8 %collective-permute-start.5 = (f32[2,8,32,128]{3,2,1,0:T(8,128)S(1)}, f32[2,8,32,128]{3,2,1,0:T(8,128)S(1)}, u32[]{:S(2)}, u32[]{:S(2)}) collective-permute-start(f32[2,8,32,128]{3,2,1,0:T(8,128)S(1)} %get-tuple-element.53), channel_id=1, source_target_pairs={{0,64},{32,96},{64,0},{96,32},{1,65},{33,97},{65,1},{97,33},{2,66}... | collective-permute-start | bytes 786440 | tf_op jit(solution)/shard_map/ppermute | solution.py:550
  66.4 3.7 %shard_map.175.refs_0_ = f32[4,256,128]{2,1,0:T(8,128)} custom-call(f32[128,17,1,128]{3,2,1,0:T(1,128)S(1)} %all_to_all.15.refs_3_.refs_0_, bf16[256,768]{1,0:T(8,128)(2,1)} %constant.35.clone.refs_7_.refs_1_.refs_2_, f32[2,128,128]{2,1,0:T(8,128)} %constant.41.clone.refs_2_.refs_3_, bf16[768,128]{1,0:T(8,128)(2,1)} %constant.42.clone.refs_3_), custom_call_target="tpu_custom_call" | custom-call | flops 4000000000 | bytes 1048576 | tf_op jit(solution)/shard_map/pallas_call | solution.py:209
  70.1 0.7 collective-permute-done.4.refs_6_
  70.8 7.2 %collective-permute-done.5.refs_7_ = f32[2,8,32,128]{3,2,1,0:T(8,128)S(1)} collective-permute-done((f32[2,8,32,128]{3,2,1,0:T(8,128)S(1)}, f32[2,8,32,128]{3,2,1,0:T(8,128)S(1)}, u32[]{:S(2)}, u32[]{:S(2)}) %collective-permute-start.5) | collective-permute-done | bytes 262176 | tf_op jit(solution)/shard_map/ppermute | solution.py:550
  78.0 4.7 %shard_map.176 = f32[64,2,16,128]{3,2,1,0:T(8,128)S(1)} custom-call(s32[2]{0:T(128)S(1)} %pad_add_fusion.refs_0_, f32[2,8,32,128]{3,2,1,0:T(8,128)S(1)} %get-tuple-element.47.refs_1_, f32[2,8,32,128]{3,2,1,0:T(8,128)S(1)} %collective-permute-done.1.refs_2_, f32[2,8,32,128]{3,2,1,0:T(8,128)S(1)} %collective-permute-done.2.refs_3_, ...), custom_call_target="tpu_custom_call" | custom-call | flops 4000000000 | bytes 2097152 | tf_op jit(solution)/shard_map/pallas_call | solution.py:209
  82.8 27.1 %all_to_all.16.refs_1_ = f32[128,16,128]{2,1,0:T(8,128)S(1)} all-to-all(f32[128,16,128]{2,1,0:T(8,128)S(1)} %bitcast.4), channel_id=1, replica_groups=mesh['base'=4,'slab'=32] {'base','slab'}, dimensions={0} | all-to-all | bytes 2097152 | tf_op jit(solution)/shard_map/all_to_all | solution.py:509
  109.9 6.5 %shard_map.177 = f32[128,9,1,128]{3,2,1,0:T(1,128)S(1)} custom-call(f32[4,256,128]{2,1,0:T(8,128)} %shard_map.175.refs_0_, f32[128,16,128]{2,1,0:T(8,128)S(1)} %all_to_all.16.refs_1_, bf16[256,768]{1,0:T(8,128)(2,1)S(1)} %copy-done.1, f32[2,128,128]{2,1,0:T(8,128)S(1)} %copy-done.5, bf16[384,256]{1,0:T(8,128)(2,1)S(1)} %copy-done.4, ...), custom_call_target="tpu_custom_call" | custom-call | flops 8000000000 | bytes 1179648 | tf_op jit(solution)/shard_map/pallas_call | solution.py:209
  116.5 18.7 %all_to_all.17.refs_0_ = f32[128,9,1,128]{3,2,1,0:T(1,128)S(1)} all-to-all(f32[128,9,1,128]{3,2,1,0:T(1,128)S(1)} %shard_map.177), channel_id=1, replica_groups=mesh['base'=4,'slab'=32] {'base','slab'}, dimensions={0} | all-to-all | bytes 1179648 | tf_op jit(solution)/shard_map/all_to_all | solution.py:509
  135.2 1.8 %shard_map.178 = f32[32,4096]{1,0:T(8,128)} custom-call(f32[128,9,1,128]{3,2,1,0:T(1,128)S(1)} %all_to_all.17.refs_0_, f32[32,4096]{1,0:T(8,128)S(1)} %copy-done, f32[2,32,128]{2,1,0:T(8,128)S(1)} %copy-done.6, bf16[768,256]{1,0:T(8,128)(2,1)S(1)} %copy-done.2), custom_call_target="tpu_custom_call" | custom-call | flops 3000000000 | bytes 1048576 | tf_op jit(solution)/shard_map/pallas_call | solution.py:209
  (19 shorter events, 0.2 us)
Async XLA Ops:
  34.9 3.5 %collective-permute-start = (f32[128,17,1,128]{3,2,1,0:T(1,128)S(1)}, f32[128,17,1,128]{3,2,1,0:T(1,128)S(1)}, u32[]{:S(2)}, u32[]{:S(2)}) collective-permute-start(f32[128,17,1,128]{3,2,1,0:T(1,128)S(1)} %all_to_all.15.refs_3_.refs_0_), channel_id=1, source_target_pairs={{0,1},{1,0},{2,3},{3,2},{4,5},{5,4},{6,7},{7,6},{8,9},{9,8},{10,11... | collective-permute-start | bytes 3342344 | tf_op jit(solution)/shard_map/ppermute | solution.py:532
  47.1 14.4 %collective-permute-start.1 = (f32[2,8,32,128]{3,2,1,0:T(8,128)S(1)}, f32[2,8,32,128]{3,2,1,0:T(8,128)S(1)}, u32[]{:S(2)}, u32[]{:S(2)}) collective-permute-start(f32[2,8,32,128]{3,2,1,0:T(8,128)S(1)} %get-tuple-element.41), channel_id=1, source_target_pairs={{0,32},{32,64},{64,96},{96,0},{1,33},{33,65},{65,97},{97,1},{2,34}... | collective-permute-start | bytes 786440 | tf_op jit(solution)/shard_map/ppermute | solution.py:550
  47.2 14.3 %collective-permute-start.2 = (f32[2,8,32,128]{3,2,1,0:T(8,128)S(1)}, f32[2,8,32,128]{3,2,1,0:T(8,128)S(1)}, u32[]{:S(2)}, u32[]{:S(2)}) collective-permute-start(f32[2,8,32,128]{3,2,1,0:T(8,128)S(1)} %get-tuple-element.42), channel_id=1, source_target_pairs={{0,64},{32,96},{64,0},{96,32},{1,65},{33,97},{65,1},{97,33},{2,66}... | collective-permute-start | bytes 786440 | tf_op jit(solution)/shard_map/ppermute | solution.py:550
  48.6 13.2 %collective-permute-start.3 = (f32[2,8,32,128]{3,2,1,0:T(8,128)S(1)}, f32[2,8,32,128]{3,2,1,0:T(8,128)S(1)}, u32[]{:S(2)}, u32[]{:S(2)}) collective-permute-start(f32[2,8,32,128]{3,2,1,0:T(8,128)S(1)} %get-tuple-element.43), channel_id=1, source_target_pairs={{0,96},{32,0},{64,32},{96,64},{1,97},{33,1},{65,33},{97,65},{2,98}... | collective-permute-start | bytes 786440 | tf_op jit(solution)/shard_map/ppermute | solution.py:550
  61.8 9.0 %collective-permute-start.4 = (f32[2,8,32,128]{3,2,1,0:T(8,128)S(1)}, f32[2,8,32,128]{3,2,1,0:T(8,128)S(1)}, u32[]{:S(2)}, u32[]{:S(2)}) collective-permute-start(f32[2,8,32,128]{3,2,1,0:T(8,128)S(1)} %get-tuple-element.52), channel_id=1, source_target_pairs={{0,32},{32,64},{64,96},{96,0},{1,33},{33,65},{65,97},{97,1},{2,34}... | collective-permute-start | bytes 786440 | tf_op jit(solution)/shard_map/ppermute | solution.py:550
  63.6 14.4 %collective-permute-start.5 = (f32[2,8,32,128]{3,2,1,0:T(8,128)S(1)}, f32[2,8,32,128]{3,2,1,0:T(8,128)S(1)}, u32[]{:S(2)}, u32[]{:S(2)}) collective-permute-start(f32[2,8,32,128]{3,2,1,0:T(8,128)S(1)} %get-tuple-element.53), channel_id=1, source_target_pairs={{0,64},{32,96},{64,0},{96,32},{1,65},{33,97},{65,1},{97,33},{2,66}... | collective-permute-start | bytes 786440 | tf_op jit(solution)/shard_map/ppermute | solution.py:550
  66.4 11.6 %collective-permute-start.6 = (f32[2,8,32,128]{3,2,1,0:T(8,128)S(1)}, f32[2,8,32,128]{3,2,1,0:T(8,128)S(1)}, u32[]{:S(2)}, u32[]{:S(2)}) collective-permute-start(f32[2,8,32,128]{3,2,1,0:T(8,128)S(1)} %get-tuple-element.54), channel_id=1, source_target_pairs={{0,96},{32,0},{64,32},{96,64},{1,97},{33,1},{65,33},{97,65},{2,98}... | collective-permute-start | bytes 786440 | tf_op jit(solution)/shard_map/ppermute | solution.py:550
  82.7 27.2 %copy-start.1 = (bf16[256,768]{1,0:T(8,128)(2,1)S(1)}, bf16[256,768]{1,0:T(8,128)(2,1)}, u32[]{:S(2)}) copy-start(bf16[256,768]{1,0:T(8,128)(2,1)} %constant.35.clone.refs_7_.refs_1_.refs_2_) | copy-start | bytes 1179652
  82.7 27.2 %copy-start.3 = (f32[2,2,128,128]{3,2,1,0:T(8,128)S(1)}, f32[2,2,128,128]{3,2,1,0:T(8,128)}, u32[]{:S(2)}) copy-start(f32[2,2,128,128]{3,2,1,0:T(8,128)} %constant.45.clone.refs_6_) | copy-start | bytes 786436
  82.7 27.2 %copy-start.4 = (bf16[384,256]{1,0:T(8,128)(2,1)S(1)}, bf16[384,256]{1,0:T(8,128)(2,1)}, u32[]{:S(2)}) copy-start(bf16[384,256]{1,0:T(8,128)(2,1)} %constant.43.clone.refs_4_) | copy-start | bytes 589828
  82.7 27.2 %copy-start.5 = (f32[2,128,128]{2,1,0:T(8,128)S(1)}, f32[2,128,128]{2,1,0:T(8,128)}, u32[]{:S(2)}) copy-start(f32[2,128,128]{2,1,0:T(8,128)} %constant.41.clone.refs_2_.refs_3_) | copy-start | bytes 393220
  116.4 18.7 %copy-start = (f32[32,4096]{1,0:T(8,128)S(1)}, f32[32,4096]{1,0:T(8,128)}, u32[]{:S(2)}) copy-start(f32[32,4096]{1,0:T(8,128)} %refs_1_.4) | copy-start | bytes 1572868
  116.4 18.7 %copy-start.2 = (bf16[768,256]{1,0:T(8,128)(2,1)S(1)}, bf16[768,256]{1,0:T(8,128)(2,1)}, u32[]{:S(2)}) copy-start(bf16[768,256]{1,0:T(8,128)(2,1)} %constant.36.clone.refs_3_) | copy-start | bytes 1179652
  116.4 18.7 %copy-start.6 = (f32[2,32,128]{2,1,0:T(8,128)S(1)}, f32[2,32,128]{2,1,0:T(8,128)}, u32[]{:S(2)}) copy-start(f32[2,32,128]{2,1,0:T(8,128)} %constant.37.clone.refs_6_.refs_2_) | copy-start | bytes 98308

commit v10 on v9

--- a/solution.py
+++ b/solution.py
@@ -13,7 +13,7 @@
 G = 8192
 IMG = 4096
 TILE = 128
-GROUP = 24
+GROUP = 32
 REST = 8
 GRANT = 20 * 2**20
 
@@ -450,7 +450,8 @@
 def image_kernel(sky, uv, w, tw_f, r_y, w_b, tw_b, r_b, out):
     done = []
     for pair in range(4):
-        a = mm(w_b[...], spread(chunks(uv, pair), RIGHT[3], 0))
+        kept = spread(chunks(uv, pair), RIGHT[3], 0)
+        a = mm(w_b[...], kept)
         parts = [[], []]
         for h in range(2):
             for k, (re, im) in enumerate(zip(halves(a, 256 * h), halves(a, 256 * h + 128))):

time: 138 us -> 139 us (level); the launches traced: 137 us -> 141 us
  blocking collectives: 76.9 us -> 82.2 us
    all_to_all x3, blocking collectives: 76.9 us -> 82.2 us  [exchange(): return lax.all_to_all(a, axis, split_axis=0, concat_axis=0, tiled=True)]
where the time goes in v10:
time: 139 us; the launch traced here: 141 us
  blocking collectives  82.2 us (59%)
  Pallas kernels  35.5 us (26%)
  waiting for transfers between devices  13.9 us (10%)
  starting transfers between devices  8.18 us (6%)
    all_to_all x3, blocking collectives, exchange(): return lax.all_to_all(a, axis, split_axis=0, concat_axis=0, tiled=True)  82.2 us
    pallas_call x7, Pallas kernels, placed(): results = got(*arrays)  35.5 us
    ppermute x6, waiting for transfers between devices, per_device(): lax.ppermute(parts[k], 'base', [(i, (i + k) % n_base) for i in range(n_ba...  12 us
    ppermute x6, starting transfers between devices, per_device(): lax.ppermute(parts[k], 'base', [(i, (i + k) % n_base) for i in range(n_ba...  7.02 us
  transfers between devices with their start and end apart: 7, of which 5 were waited for; matrix products, arithmetic and copies ran while one was open for 0% of the time, Pallas kernels for 8%

profile of v10, /device:TPU:1, one launch (start us, length us, event | category | flops | bytes accessed | tf_op | source)
XLA Modules:
  0.0 140.8 jit_solution(3353044784119776271)
XLA Ops:
  0.0 3.8 %shard_map.172 = f32[128,17,1,128]{3,2,1,0:T(1,128)S(1)} custom-call(s32[128]{0:T(128)} %bitcast.5, s32[128]{0:T(128)} %refs_1_.3, f32[128,2,128]{2,1,0:T(2,128)} %refs_2_.4, f32[128,2,128]{2,1,0:T(2,128)} %refs_3_.4, f32[32,4096]{1,0:T(8,128)} %refs_4_.2, f32[32,4096]{1,0:T(8,128)} %refs_1_.4, f32[2,32,128]{2,1,0:T(8,128)} %constant.37.clone.refs_6_.refs_2_, ...), custom_call_target="tpu_custom_call" | custom-call | flops 2000000000 | bytes 2228224 | tf_op jit(solution)/shard_map/pallas_call | solution.py:209
  3.8 31.1 %all_to_all.15.refs_3_.refs_0_ = f32[128,17,1,128]{3,2,1,0:T(1,128)S(1)} all-to-all(f32[128,17,1,128]{3,2,1,0:T(1,128)S(1)} %shard_map.172), channel_id=1, replica_groups=mesh['base'=4,'slab'=32] {'base','slab'}, dimensions={0} | all-to-all | bytes 2228224 | tf_op jit(solution)/shard_map/all_to_all | solution.py:510
  34.9 1.2 collective-permute-start
  36.2 0.3 fusion.1
  36.4 0.1 convert_element_type.11.refs_1_
  36.6 1.9 %collective-permute-done.refs_4_ = f32[128,17,1,128]{3,2,1,0:T(1,128)S(1)} collective-permute-done((f32[128,17,1,128]{3,2,1,0:T(1,128)S(1)}, f32[128,17,1,128]{3,2,1,0:T(1,128)S(1)}, u32[]{:S(2)}, u32[]{:S(2)}) %collective-permute-start) | collective-permute-done | bytes 1114144 | tf_op jit(solution)/shard_map/ppermute | solution.py:533
  38.5 0.3 fusion
  38.9 7.5 %shard_map.173 = (f32[2,8,32,128]{3,2,1,0:T(8,128)S(1)}, f32[2,8,32,128]{3,2,1,0:T(8,128)S(1)}, f32[2,8,32,128]{3,2,1,0:T(8,128)S(1)}, f32[2,8,32,128]{3,2,1,0:T(8,128)S(1)}) custom-call(s32[2]{0:T(128)S(1)} %pad_add_fusion.refs_0_, s32[768]{0:T(1024)S(1)} %convert_element_type.11.refs_1_, s32[768]{0:T(1024)S(1)} %convert_element_type.13.refs_2_, ...), custom_call_target="tpu_custom_call" | custom-call | flops 20000000000 | bytes 2097152 | tf_op jit(solution)/shard_map/pallas_call | solution.py:209
  46.4 0.4 collective-permute-start.1
  46.8 1.7 %collective-permute-start.2 = (f32[2,8,32,128]{3,2,1,0:T(8,128)S(1)}, f32[2,8,32,128]{3,2,1,0:T(8,128)S(1)}, u32[]{:S(2)}, u32[]{:S(2)}) collective-permute-start(f32[2,8,32,128]{3,2,1,0:T(8,128)S(1)} %get-tuple-element.42), channel_id=1, source_target_pairs={{0,64},{32,96},{64,0},{96,32},{1,65},{33,97},{65,1},{97,33},{2,66}... | collective-permute-start | bytes 786440 | tf_op jit(solution)/shard_map/ppermute | solution.py:551
  48.5 0.7 collective-permute-start.3
  49.3 7.5 %shard_map.174 = (f32[2,8,32,128]{3,2,1,0:T(8,128)S(1)}, f32[2,8,32,128]{3,2,1,0:T(8,128)S(1)}, f32[2,8,32,128]{3,2,1,0:T(8,128)S(1)}, f32[2,8,32,128]{3,2,1,0:T(8,128)S(1)}) custom-call(s32[2]{0:T(128)S(1)} %pad_add_fusion.refs_0_, s32[768]{0:T(1024)S(1)} %convert_element_type.11.refs_1_, s32[768]{0:T(1024)S(1)} %convert_element_type.13.refs_2_, ...), custom_call_target="tpu_custom_call" | custom-call | flops 20000000000 | bytes 2097152 | tf_op jit(solution)/shard_map/pallas_call | solution.py:209
  56.8 2.5 %collective-permute-done.2.refs_3_ = f32[2,8,32,128]{3,2,1,0:T(8,128)S(1)} collective-permute-done((f32[2,8,32,128]{3,2,1,0:T(8,128)S(1)}, f32[2,8,32,128]{3,2,1,0:T(8,128)S(1)}, u32[]{:S(2)}, u32[]{:S(2)}) %collective-permute-start.2) | collective-permute-done | bytes 262176 | tf_op jit(solution)/shard_map/ppermute | solution.py:551
  59.3 1.9 %collective-permute-done.3.refs_4_ = f32[2,8,32,128]{3,2,1,0:T(8,128)S(1)} collective-permute-done((f32[2,8,32,128]{3,2,1,0:T(8,128)S(1)}, f32[2,8,32,128]{3,2,1,0:T(8,128)S(1)}, u32[]{:S(2)}, u32[]{:S(2)}) %collective-permute-start.3) | collective-permute-done | bytes 262176 | tf_op jit(solution)/shard_map/ppermute | solution.py:551
  61.2 1.1 collective-permute-start.4
  62.2 3.1 %collective-permute-start.5 = (f32[2,8,32,128]{3,2,1,0:T(8,128)S(1)}, f32[2,8,32,128]{3,2,1,0:T(8,128)S(1)}, u32[]{:S(2)}, u32[]{:S(2)}) collective-permute-start(f32[2,8,32,128]{3,2,1,0:T(8,128)S(1)} %get-tuple-element.53), channel_id=1, source_target_pairs={{0,64},{32,96},{64,0},{96,32},{1,65},{33,97},{65,1},{97,33},{2,66}... | collective-permute-start | bytes 786440 | tf_op jit(solution)/shard_map/ppermute | solution.py:551
  65.3 3.7 %shard_map.175.refs_0_ = f32[4,256,128]{2,1,0:T(8,128)} custom-call(f32[128,17,1,128]{3,2,1,0:T(1,128)S(1)} %all_to_all.15.refs_3_.refs_0_, bf16[256,768]{1,0:T(8,128)(2,1)} %constant.35.clone.refs_7_.refs_1_.refs_2_, f32[2,128,128]{2,1,0:T(8,128)} %constant.41.clone.refs_2_.refs_3_, bf16[768,128]{1,0:T(8,128)(2,1)} %constant.42.clone.refs_3_), custom_call_target="tpu_custom_call" | custom-call | flops 4000000000 | bytes 1048576 | tf_op jit(solution)/shard_map/pallas_call | solution.py:209
  69.0 0.3 collective-permute-done.4.refs_6_
  69.3 7.4 %collective-permute-done.5.refs_7_ = f32[2,8,32,128]{3,2,1,0:T(8,128)S(1)} collective-permute-done((f32[2,8,32,128]{3,2,1,0:T(8,128)S(1)}, f32[2,8,32,128]{3,2,1,0:T(8,128)S(1)}, u32[]{:S(2)}, u32[]{:S(2)}) %collective-permute-start.5) | collective-permute-done | bytes 262176 | tf_op jit(solution)/shard_map/ppermute | solution.py:551
  76.7 4.7 %shard_map.176 = f32[64,2,16,128]{3,2,1,0:T(8,128)S(1)} custom-call(s32[2]{0:T(128)S(1)} %pad_add_fusion.refs_0_, f32[2,8,32,128]{3,2,1,0:T(8,128)S(1)} %get-tuple-element.47.refs_1_, f32[2,8,32,128]{3,2,1,0:T(8,128)S(1)} %collective-permute-done.1.refs_2_, f32[2,8,32,128]{3,2,1,0:T(8,128)S(1)} %collective-permute-done.2.refs_3_, ...), custom_call_target="tpu_custom_call" | custom-call | flops 4000000000 | bytes 2097152 | tf_op jit(solution)/shard_map/pallas_call | solution.py:209
  81.4 32.4 %all_to_all.16.refs_1_ = f32[128,16,128]{2,1,0:T(8,128)S(1)} all-to-all(f32[128,16,128]{2,1,0:T(8,128)S(1)} %bitcast.4), channel_id=1, replica_groups=mesh['base'=4,'slab'=32] {'base','slab'}, dimensions={0} | all-to-all | bytes 2097152 | tf_op jit(solution)/shard_map/all_to_all | solution.py:510
  113.8 6.4 %shard_map.177 = f32[128,9,1,128]{3,2,1,0:T(1,128)S(1)} custom-call(f32[4,256,128]{2,1,0:T(8,128)} %shard_map.175.refs_0_, f32[128,16,128]{2,1,0:T(8,128)S(1)} %all_to_all.16.refs_1_, bf16[256,768]{1,0:T(8,128)(2,1)S(1)} %copy-done.1, f32[2,128,128]{2,1,0:T(8,128)S(1)} %copy-done.5, bf16[384,256]{1,0:T(8,128)(2,1)S(1)} %copy-done.4, ...), custom_call_target="tpu_custom_call" | custom-call | flops 8000000000 | bytes 1179648 | tf_op jit(solution)/shard_map/pallas_call | solution.py:209
  120.3 18.7 %all_to_all.17.refs_0_ = f32[128,9,1,128]{3,2,1,0:T(1,128)S(1)} all-to-all(f32[128,9,1,128]{3,2,1,0:T(1,128)S(1)} %shard_map.177), channel_id=1, replica_groups=mesh['base'=4,'slab'=32] {'base','slab'}, dimensions={0} | all-to-all | bytes 1179648 | tf_op jit(solution)/shard_map/all_to_all | solution.py:510
  139.0 1.8 %shard_map.178 = f32[32,4096]{1,0:T(8,128)} custom-call(f32[128,9,1,128]{3,2,1,0:T(1,128)S(1)} %all_to_all.17.refs_0_, f32[32,4096]{1,0:T(8,128)S(1)} %copy-done, f32[2,32,128]{2,1,0:T(8,128)S(1)} %copy-done.6, bf16[768,256]{1,0:T(8,128)(2,1)S(1)} %copy-done.2), custom_call_target="tpu_custom_call" | custom-call | flops 3000000000 | bytes 1048576 | tf_op jit(solution)/shard_map/pallas_call | solution.py:209
  (19 shorter events, 0.3 us)
Async XLA Ops:
  34.9 3.5 %collective-permute-start = (f32[128,17,1,128]{3,2,1,0:T(1,128)S(1)}, f32[128,17,1,128]{3,2,1,0:T(1,128)S(1)}, u32[]{:S(2)}, u32[]{:S(2)}) collective-permute-start(f32[128,17,1,128]{3,2,1,0:T(1,128)S(1)} %all_to_all.15.refs_3_.refs_0_), channel_id=1, source_target_pairs={{0,1},{1,0},{2,3},{3,2},{4,5},{5,4},{6,7},{7,6},{8,9},{9,8},{10,11... | collective-permute-start | bytes 3342344 | tf_op jit(solution)/shard_map/ppermute | solution.py:533
  46.4 10.4 %collective-permute-start.1 = (f32[2,8,32,128]{3,2,1,0:T(8,128)S(1)}, f32[2,8,32,128]{3,2,1,0:T(8,128)S(1)}, u32[]{:S(2)}, u32[]{:S(2)}) collective-permute-start(f32[2,8,32,128]{3,2,1,0:T(8,128)S(1)} %get-tuple-element.41), channel_id=1, source_target_pairs={{0,32},{32,64},{64,96},{96,0},{1,33},{33,65},{65,97},{97,1},{2,34}... | collective-permute-start | bytes 786440 | tf_op jit(solution)/shard_map/ppermute | solution.py:551
  46.8 12.5 %collective-permute-start.2 = (f32[2,8,32,128]{3,2,1,0:T(8,128)S(1)}, f32[2,8,32,128]{3,2,1,0:T(8,128)S(1)}, u32[]{:S(2)}, u32[]{:S(2)}) collective-permute-start(f32[2,8,32,128]{3,2,1,0:T(8,128)S(1)} %get-tuple-element.42), channel_id=1, source_target_pairs={{0,64},{32,96},{64,0},{96,32},{1,65},{33,97},{65,1},{97,33},{2,66}... | collective-permute-start | bytes 786440 | tf_op jit(solution)/shard_map/ppermute | solution.py:551
  48.5 12.6 %collective-permute-start.3 = (f32[2,8,32,128]{3,2,1,0:T(8,128)S(1)}, f32[2,8,32,128]{3,2,1,0:T(8,128)S(1)}, u32[]{:S(2)}, u32[]{:S(2)}) collective-permute-start(f32[2,8,32,128]{3,2,1,0:T(8,128)S(1)} %get-tuple-element.43), channel_id=1, source_target_pairs={{0,96},{32,0},{64,32},{96,64},{1,97},{33,1},{65,33},{97,65},{2,98}... | collective-permute-start | bytes 786440 | tf_op jit(solution)/shard_map/ppermute | solution.py:551
  61.2 8.1 %collective-permute-start.4 = (f32[2,8,32,128]{3,2,1,0:T(8,128)S(1)}, f32[2,8,32,128]{3,2,1,0:T(8,128)S(1)}, u32[]{:S(2)}, u32[]{:S(2)}) collective-permute-start(f32[2,8,32,128]{3,2,1,0:T(8,128)S(1)} %get-tuple-element.52), channel_id=1, source_target_pairs={{0,32},{32,64},{64,96},{96,0},{1,33},{33,65},{65,97},{97,1},{2,34}... | collective-permute-start | bytes 786440 | tf_op jit(solution)/shard_map/ppermute | solution.py:551
  62.2 14.4 %collective-permute-start.5 = (f32[2,8,32,128]{3,2,1,0:T(8,128)S(1)}, f32[2,8,32,128]{3,2,1,0:T(8,128)S(1)}, u32[]{:S(2)}, u32[]{:S(2)}) collective-permute-start(f32[2,8,32,128]{3,2,1,0:T(8,128)S(1)} %get-tuple-element.53), channel_id=1, source_target_pairs={{0,64},{32,96},{64,0},{96,32},{1,65},{33,97},{65,1},{97,33},{2,66}... | collective-permute-start | bytes 786440 | tf_op jit(solution)/shard_map/ppermute | solution.py:551
  65.3 11.3 %collective-permute-start.6 = (f32[2,8,32,128]{3,2,1,0:T(8,128)S(1)}, f32[2,8,32,128]{3,2,1,0:T(8,128)S(1)}, u32[]{:S(2)}, u32[]{:S(2)}) collective-permute-start(f32[2,8,32,128]{3,2,1,0:T(8,128)S(1)} %get-tuple-element.54), channel_id=1, source_target_pairs={{0,96},{32,0},{64,32},{96,64},{1,97},{33,1},{65,33},{97,65},{2,98}... | collective-permute-start | bytes 786440 | tf_op jit(solution)/shard_map/ppermute | solution.py:551
  81.4 32.4 %copy-start.1 = (bf16[256,768]{1,0:T(8,128)(2,1)S(1)}, bf16[256,768]{1,0:T(8,128)(2,1)}, u32[]{:S(2)}) copy-start(bf16[256,768]{1,0:T(8,128)(2,1)} %constant.35.clone.refs_7_.refs_1_.refs_2_) | copy-start | bytes 1179652
  81.4 32.4 %copy-start.3 = (f32[2,2,128,128]{3,2,1,0:T(8,128)S(1)}, f32[2,2,128,128]{3,2,1,0:T(8,128)}, u32[]{:S(2)}) copy-start(f32[2,2,128,128]{3,2,1,0:T(8,128)} %constant.45.clone.refs_6_) | copy-start | bytes 786436
  81.4 32.4 %copy-start.4 = (bf16[384,256]{1,0:T(8,128)(2,1)S(1)}, bf16[384,256]{1,0:T(8,128)(2,1)}, u32[]{:S(2)}) copy-start(bf16[384,256]{1,0:T(8,128)(2,1)} %constant.43.clone.refs_4_) | copy-start | bytes 589828
  81.4 32.4 %copy-start.5 = (f32[2,128,128]{2,1,0:T(8,128)S(1)}, f32[2,128,128]{2,1,0:T(8,128)}, u32[]{:S(2)}) copy-start(f32[2,128,128]{2,1,0:T(8,128)} %constant.41.clone.refs_2_.refs_3_) | copy-start | bytes 393220
  120.2 18.7 %copy-start = (f32[32,4096]{1,0:T(8,128)S(1)}, f32[32,4096]{1,0:T(8,128)}, u32[]{:S(2)}) copy-start(f32[32,4096]{1,0:T(8,128)} %refs_1_.4) | copy-start | bytes 1572868
  120.2 18.7 %copy-start.2 = (bf16[768,256]{1,0:T(8,128)(2,1)S(1)}, bf16[768,256]{1,0:T(8,128)(2,1)}, u32[]{:S(2)}) copy-start(bf16[768,256]{1,0:T(8,128)(2,1)} %constant.36.clone.refs_3_) | copy-start | bytes 1179652
  120.3 18.7 %copy-start.6 = (f32[2,32,128]{2,1,0:T(8,128)S(1)}, f32[2,32,128]{2,1,0:T(8,128)}, u32[]{:S(2)}) copy-start(f32[2,32,128]{2,1,0:T(8,128)} %constant.37.clone.refs_6_.refs_2_) | copy-start | bytes 98308

commit v11 on v10

--- a/solution.py
+++ b/solution.py
@@ -547,9 +547,10 @@
             parts, tags = lax.optimization_barrier((parts, tags))
         else:
             parts, grids, field = lax.optimization_barrier((parts, grids, data))
-        grids = [*grids, parts[0]] + [
-            lax.ppermute(parts[k], "base", [(i, (i + k) % n_base) for i in range(n_base)]) for k in range(1, n_base)
-        ]
+        moved = {
+            k: lax.ppermute(parts[k], "base", [(i, (i + k) % n_base) for i in range(n_base)]) for k in (2, 1, 3)
+        }
+        grids = [*grids, parts[0]] + [moved[k] for k in range(1, n_base)]
     sky = call(
         sky_kernel,
         (4, 256, 128),

time: 139 us -> 137 us (0.986); the launches traced: 141 us -> 137 us
  blocking collectives: 82.2 us -> 74.6 us
  Pallas kernels: 35.5 us -> 42.2 us
  waiting for transfers between devices: 13.9 us -> 10.6 us
    all_to_all x3, blocking collectives: 82.2 us -> 74.6 us  [exchange(): return lax.all_to_all(a, axis, split_axis=0, concat_axis=0, tiled=True)]
    pallas_call x7, Pallas kernels: 35.5 us -> 42.2 us  [placed(): results = got(*arrays)]
    ppermute x6, waiting for transfers between devices: 12 us -> 8.7 us  [per_device(): lax.ppermute(parts[k], 'base', [(i, (i + k) % n_base) for i in range(n_ba...]
  transfers between devices with their start and end apart: 7 -> 7, of which waited for: 5 -> 3; matrix products, arithmetic and copies ran while one was open for 0% -> 0% of each run, Pallas kernels for 8% -> 10%
where the time goes in v11:
time: 137 us
  blocking collectives  74.6 us (54%)
  Pallas kernels  42.2 us (31%)
  waiting for transfers between devices  10.6 us (8%)
  starting transfers between devices  8.03 us (6%)
    all_to_all x3, blocking collectives, exchange(): return lax.all_to_all(a, axis, split_axis=0, concat_axis=0, tiled=True)  74.6 us
    pallas_call x7, Pallas kernels, placed(): results = got(*arrays)  42.2 us
    ppermute x6, waiting for transfers between devices, per_device(): lax.ppermute(parts[k], 'base', [(i, (i + k) % n_base) for i in range(n_ba...  8.7 us
    ppermute x6, starting transfers between devices, per_device(): lax.ppermute(parts[k], 'base', [(i, (i + k) % n_base) for i in range(n_ba...  6.86 us
  transfers between devices with their start and end apart: 7, of which 3 were waited for; matrix products, arithmetic and copies ran while one was open for 0% of the time, Pallas kernels for 10%

profile of v11, /device:TPU:1, one launch (start us, length us, event | category | flops | bytes accessed | tf_op | source)
XLA Modules:
  0.0 136.5 jit_solution(3353044784119776271)
XLA Ops:
  0.0 3.8 %shard_map.172 = f32[128,17,1,128]{3,2,1,0:T(1,128)S(1)} custom-call(s32[128]{0:T(128)} %bitcast.5, s32[128]{0:T(128)} %refs_1_.3, f32[128,2,128]{2,1,0:T(2,128)} %refs_2_.4, f32[128,2,128]{2,1,0:T(2,128)} %refs_3_.4, f32[32,4096]{1,0:T(8,128)} %refs_4_.2, f32[32,4096]{1,0:T(8,128)} %refs_1_.4, f32[2,32,128]{2,1,0:T(8,128)} %constant.37.clone.refs_6_.refs_2_, ...), custom_call_target="tpu_custom_call" | custom-call | flops 2000000000 | bytes 2228224 | tf_op jit(solution)/shard_map/pallas_call | solution.py:209
  3.8 31.1 %all_to_all.15.refs_3_.refs_0_ = f32[128,17,1,128]{3,2,1,0:T(1,128)S(1)} all-to-all(f32[128,17,1,128]{3,2,1,0:T(1,128)S(1)} %shard_map.172), channel_id=1, replica_groups=mesh['base'=4,'slab'=32] {'base','slab'}, dimensions={0} | all-to-all | bytes 2228224 | tf_op jit(solution)/shard_map/all_to_all | solution.py:510
  34.9 1.2 collective-permute-start
  36.1 0.1 pad_add_fusion.refs_0_
  36.2 0.3 fusion.1
  36.4 0.1 convert_element_type.11.refs_1_
  36.6 1.9 %collective-permute-done.refs_4_ = f32[128,17,1,128]{3,2,1,0:T(1,128)S(1)} collective-permute-done((f32[128,17,1,128]{3,2,1,0:T(1,128)S(1)}, f32[128,17,1,128]{3,2,1,0:T(1,128)S(1)}, u32[]{:S(2)}, u32[]{:S(2)}) %collective-permute-start) | collective-permute-done | bytes 1114144 | tf_op jit(solution)/shard_map/ppermute | solution.py:533
  38.5 0.3 fusion
  38.7 0.1 convert_element_type.13.refs_2_
  38.9 11.2 %shard_map.173 = (f32[2,8,32,128]{3,2,1,0:T(8,128)S(1)}, f32[2,8,32,128]{3,2,1,0:T(8,128)S(1)}, f32[2,8,32,128]{3,2,1,0:T(8,128)S(1)}, f32[2,8,32,128]{3,2,1,0:T(8,128)S(1)}) custom-call(s32[2]{0:T(128)S(1)} %pad_add_fusion.refs_0_, s32[768]{0:T(1024)S(1)} %convert_element_type.11.refs_1_, s32[768]{0:T(1024)S(1)} %convert_element_type.13.refs_2_, ...), custom_call_target="tpu_custom_call" | custom-call | flops 20000000000 | bytes 2097152 | tf_op jit(solution)/shard_map/pallas_call | solution.py:209
  50.1 0.1 collective-permute-start.1
  50.2 0.1 collective-permute-start.2
  50.3 2.6 %collective-permute-start.3 = (f32[2,8,32,128]{3,2,1,0:T(8,128)S(1)}, f32[2,8,32,128]{3,2,1,0:T(8,128)S(1)}, u32[]{:S(2)}, u32[]{:S(2)}) collective-permute-start(f32[2,8,32,128]{3,2,1,0:T(8,128)S(1)} %get-tuple-element.43), channel_id=1, source_target_pairs={{0,96},{32,0},{64,32},{96,64},{1,97},{33,1},{65,33},{97,65},{2,98}... | collective-permute-start | bytes 786440 | tf_op jit(solution)/shard_map/ppermute | solution.py:551
  52.8 10.5 %shard_map.174 = (f32[2,8,32,128]{3,2,1,0:T(8,128)S(1)}, f32[2,8,32,128]{3,2,1,0:T(8,128)S(1)}, f32[2,8,32,128]{3,2,1,0:T(8,128)S(1)}, f32[2,8,32,128]{3,2,1,0:T(8,128)S(1)}) custom-call(s32[2]{0:T(128)S(1)} %pad_add_fusion.refs_0_, s32[768]{0:T(1024)S(1)} %convert_element_type.11.refs_1_, s32[768]{0:T(1024)S(1)} %convert_element_type.13.refs_2_, ...), custom_call_target="tpu_custom_call" | custom-call | flops 20000000000 | bytes 2097152 | tf_op jit(solution)/shard_map/pallas_call | solution.py:209
  63.4 1.2 collective-permute-done.1.refs_2_
  64.6 1.2 collective-permute-start.4
  65.8 2.9 %collective-permute-start.5 = (f32[2,8,32,128]{3,2,1,0:T(8,128)S(1)}, f32[2,8,32,128]{3,2,1,0:T(8,128)S(1)}, u32[]{:S(2)}, u32[]{:S(2)}) collective-permute-start(f32[2,8,32,128]{3,2,1,0:T(8,128)S(1)} %get-tuple-element.53), channel_id=1, source_target_pairs={{0,64},{32,96},{64,0},{96,32},{1,65},{33,97},{65,1},{97,33},{2,66}... | collective-permute-start | bytes 786440 | tf_op jit(solution)/shard_map/ppermute | solution.py:551
  68.7 3.7 %shard_map.175.refs_0_ = f32[4,256,128]{2,1,0:T(8,128)} custom-call(f32[128,17,1,128]{3,2,1,0:T(1,128)S(1)} %all_to_all.15.refs_3_.refs_0_, bf16[256,768]{1,0:T(8,128)(2,1)} %constant.35.clone.refs_7_.refs_1_.refs_2_, f32[2,128,128]{2,1,0:T(8,128)} %constant.41.clone.refs_2_.refs_3_, bf16[768,128]{1,0:T(8,128)(2,1)} %constant.42.clone.refs_3_), custom_call_target="tpu_custom_call" | custom-call | flops 4000000000 | bytes 1048576 | tf_op jit(solution)/shard_map/pallas_call | solution.py:209
  72.4 7.4 %collective-permute-done.5.refs_7_ = f32[2,8,32,128]{3,2,1,0:T(8,128)S(1)} collective-permute-done((f32[2,8,32,128]{3,2,1,0:T(8,128)S(1)}, f32[2,8,32,128]{3,2,1,0:T(8,128)S(1)}, u32[]{:S(2)}, u32[]{:S(2)}) %collective-permute-start.5) | collective-permute-done | bytes 262176 | tf_op jit(solution)/shard_map/ppermute | solution.py:551
  79.9 4.7 %shard_map.176 = f32[64,2,16,128]{3,2,1,0:T(8,128)S(1)} custom-call(s32[2]{0:T(128)S(1)} %pad_add_fusion.refs_0_, f32[2,8,32,128]{3,2,1,0:T(8,128)S(1)} %get-tuple-element.47.refs_1_, f32[2,8,32,128]{3,2,1,0:T(8,128)S(1)} %collective-permute-done.1.refs_2_, f32[2,8,32,128]{3,2,1,0:T(8,128)S(1)} %collective-permute-done.2.refs_3_, ...), custom_call_target="tpu_custom_call" | custom-call | flops 4000000000 | bytes 2097152 | tf_op jit(solution)/shard_map/pallas_call | solution.py:209
  84.7 24.9 %all_to_all.16.refs_1_ = f32[128,16,128]{2,1,0:T(8,128)S(1)} all-to-all(f32[128,16,128]{2,1,0:T(8,128)S(1)} %bitcast.4), channel_id=1, replica_groups=mesh['base'=4,'slab'=32] {'base','slab'}, dimensions={0} | all-to-all | bytes 2097152 | tf_op jit(solution)/shard_map/all_to_all | solution.py:510
  109.5 6.4 %shard_map.177 = f32[128,9,1,128]{3,2,1,0:T(1,128)S(1)} custom-call(f32[4,256,128]{2,1,0:T(8,128)} %shard_map.175.refs_0_, f32[128,16,128]{2,1,0:T(8,128)S(1)} %all_to_all.16.refs_1_, bf16[256,768]{1,0:T(8,128)(2,1)S(1)} %copy-done.1, f32[2,128,128]{2,1,0:T(8,128)S(1)} %copy-done.5, bf16[384,256]{1,0:T(8,128)(2,1)S(1)} %copy-done.4, ...), custom_call_target="tpu_custom_call" | custom-call | flops 8000000000 | bytes 1179648 | tf_op jit(solution)/shard_map/pallas_call | solution.py:209
  116.0 18.7 %all_to_all.17.refs_0_ = f32[128,9,1,128]{3,2,1,0:T(1,128)S(1)} all-to-all(f32[128,9,1,128]{3,2,1,0:T(1,128)S(1)} %shard_map.177), channel_id=1, replica_groups=mesh['base'=4,'slab'=32] {'base','slab'}, dimensions={0} | all-to-all | bytes 1179648 | tf_op jit(solution)/shard_map/all_to_all | solution.py:510
  134.7 1.8 %shard_map.178 = f32[32,4096]{1,0:T(8,128)} custom-call(f32[128,9,1,128]{3,2,1,0:T(1,128)S(1)} %all_to_all.17.refs_0_, f32[32,4096]{1,0:T(8,128)S(1)} %copy-done, f32[2,32,128]{2,1,0:T(8,128)S(1)} %copy-done.6, bf16[768,256]{1,0:T(8,128)(2,1)S(1)} %copy-done.2), custom_call_target="tpu_custom_call" | custom-call | flops 3000000000 | bytes 1048576 | tf_op jit(solution)/shard_map/pallas_call | solution.py:209
  (19 shorter events, 0.1 us)
Async XLA Ops:
  34.9 3.5 %collective-permute-start = (f32[128,17,1,128]{3,2,1,0:T(1,128)S(1)}, f32[128,17,1,128]{3,2,1,0:T(1,128)S(1)}, u32[]{:S(2)}, u32[]{:S(2)}) collective-permute-start(f32[128,17,1,128]{3,2,1,0:T(1,128)S(1)} %all_to_all.15.refs_3_.refs_0_), channel_id=1, source_target_pairs={{0,1},{1,0},{2,3},{3,2},{4,5},{5,4},{6,7},{7,6},{8,9},{9,8},{10,11... | collective-permute-start | bytes 3342344 | tf_op jit(solution)/shard_map/ppermute | solution.py:533
  50.1 14.5 %collective-permute-start.1 = (f32[2,8,32,128]{3,2,1,0:T(8,128)S(1)}, f32[2,8,32,128]{3,2,1,0:T(8,128)S(1)}, u32[]{:S(2)}, u32[]{:S(2)}) collective-permute-start(f32[2,8,32,128]{3,2,1,0:T(8,128)S(1)} %get-tuple-element.41), channel_id=1, source_target_pairs={{0,32},{32,64},{64,96},{96,0},{1,33},{33,65},{65,97},{97,1},{2,34}... | collective-permute-start | bytes 786440 | tf_op jit(solution)/shard_map/ppermute | solution.py:551
  50.2 14.4 %collective-permute-start.2 = (f32[2,8,32,128]{3,2,1,0:T(8,128)S(1)}, f32[2,8,32,128]{3,2,1,0:T(8,128)S(1)}, u32[]{:S(2)}, u32[]{:S(2)}) collective-permute-start(f32[2,8,32,128]{3,2,1,0:T(8,128)S(1)} %get-tuple-element.42), channel_id=1, source_target_pairs={{0,64},{32,96},{64,0},{96,32},{1,65},{33,97},{65,1},{97,33},{2,66}... | collective-permute-start | bytes 786440 | tf_op jit(solution)/shard_map/ppermute | solution.py:551
  50.3 14.4 %collective-permute-start.3 = (f32[2,8,32,128]{3,2,1,0:T(8,128)S(1)}, f32[2,8,32,128]{3,2,1,0:T(8,128)S(1)}, u32[]{:S(2)}, u32[]{:S(2)}) collective-permute-start(f32[2,8,32,128]{3,2,1,0:T(8,128)S(1)} %get-tuple-element.43), channel_id=1, source_target_pairs={{0,96},{32,0},{64,32},{96,64},{1,97},{33,1},{65,33},{97,65},{2,98}... | collective-permute-start | bytes 786440 | tf_op jit(solution)/shard_map/ppermute | solution.py:551
  64.6 7.8 %collective-permute-start.4 = (f32[2,8,32,128]{3,2,1,0:T(8,128)S(1)}, f32[2,8,32,128]{3,2,1,0:T(8,128)S(1)}, u32[]{:S(2)}, u32[]{:S(2)}) collective-permute-start(f32[2,8,32,128]{3,2,1,0:T(8,128)S(1)} %get-tuple-element.52), channel_id=1, source_target_pairs={{0,32},{32,64},{64,96},{96,0},{1,33},{33,65},{65,97},{97,1},{2,34}... | collective-permute-start | bytes 786440 | tf_op jit(solution)/shard_map/ppermute | solution.py:551
  65.8 14.1 %collective-permute-start.5 = (f32[2,8,32,128]{3,2,1,0:T(8,128)S(1)}, f32[2,8,32,128]{3,2,1,0:T(8,128)S(1)}, u32[]{:S(2)}, u32[]{:S(2)}) collective-permute-start(f32[2,8,32,128]{3,2,1,0:T(8,128)S(1)} %get-tuple-element.53), channel_id=1, source_target_pairs={{0,64},{32,96},{64,0},{96,32},{1,65},{33,97},{65,1},{97,33},{2,66}... | collective-permute-start | bytes 786440 | tf_op jit(solution)/shard_map/ppermute | solution.py:551
  68.7 11.2 %collective-permute-start.6 = (f32[2,8,32,128]{3,2,1,0:T(8,128)S(1)}, f32[2,8,32,128]{3,2,1,0:T(8,128)S(1)}, u32[]{:S(2)}, u32[]{:S(2)}) collective-permute-start(f32[2,8,32,128]{3,2,1,0:T(8,128)S(1)} %get-tuple-element.54), channel_id=1, source_target_pairs={{0,96},{32,0},{64,32},{96,64},{1,97},{33,1},{65,33},{97,65},{2,98}... | collective-permute-start | bytes 786440 | tf_op jit(solution)/shard_map/ppermute | solution.py:551
  84.6 24.9 %copy-start.1 = (bf16[256,768]{1,0:T(8,128)(2,1)S(1)}, bf16[256,768]{1,0:T(8,128)(2,1)}, u32[]{:S(2)}) copy-start(bf16[256,768]{1,0:T(8,128)(2,1)} %constant.35.clone.refs_7_.refs_1_.refs_2_) | copy-start | bytes 1179652
  84.6 24.9 %copy-start.3 = (f32[2,2,128,128]{3,2,1,0:T(8,128)S(1)}, f32[2,2,128,128]{3,2,1,0:T(8,128)}, u32[]{:S(2)}) copy-start(f32[2,2,128,128]{3,2,1,0:T(8,128)} %constant.45.clone.refs_6_) | copy-start | bytes 786436
  84.6 24.9 %copy-start.4 = (bf16[384,256]{1,0:T(8,128)(2,1)S(1)}, bf16[384,256]{1,0:T(8,128)(2,1)}, u32[]{:S(2)}) copy-start(bf16[384,256]{1,0:T(8,128)(2,1)} %constant.43.clone.refs_4_) | copy-start | bytes 589828
  84.7 24.9 %copy-start.5 = (f32[2,128,128]{2,1,0:T(8,128)S(1)}, f32[2,128,128]{2,1,0:T(8,128)}, u32[]{:S(2)}) copy-start(f32[2,128,128]{2,1,0:T(8,128)} %constant.41.clone.refs_2_.refs_3_) | copy-start | bytes 393220
  115.9 18.7 %copy-start = (f32[32,4096]{1,0:T(8,128)S(1)}, f32[32,4096]{1,0:T(8,128)}, u32[]{:S(2)}) copy-start(f32[32,4096]{1,0:T(8,128)} %refs_1_.4) | copy-start | bytes 1572868
  116.0 18.7 %copy-start.2 = (bf16[768,256]{1,0:T(8,128)(2,1)S(1)}, bf16[768,256]{1,0:T(8,128)(2,1)}, u32[]{:S(2)}) copy-start(bf16[768,256]{1,0:T(8,128)(2,1)} %constant.36.clone.refs_3_) | copy-start | bytes 1179652
  116.0 18.7 %copy-start.6 = (f32[2,32,128]{2,1,0:T(8,128)S(1)}, f32[2,32,128]{2,1,0:T(8,128)}, u32[]{:S(2)}) copy-start(f32[2,32,128]{2,1,0:T(8,128)} %constant.37.clone.refs_6_.refs_2_) | copy-start | bytes 98308
